TPU v7x, 32 devices: a whole 2x2x4 slice. The times are simulated.
32 devices in a mesh: dp: 2 (over y), context: 2 (over x), expert: 8 (over z, core).
Axes of the slice: x: 2, y: 2, z: 4, core: 2. Of those that a mesh axis runs over, the one named last changes fastest.
Arguments:
- tokens: bfloat16 [16, 256, 2048], P(('dp', 'expert'), 'context'), may hold values from -6 to 6
- cotangent: bfloat16 [16, 256, 2048], P(('dp', 'expert'), 'context'), may hold values from -6 to 6
- deal_order: int32 [16, 256], P(('dp', 'expert')), may hold values from 0 to 255, each once within a row
- seq_lengths: int32 [16, 2], P(('dp', 'expert')), may hold values from 1 to 192, 256 in all within a row
- expert_ids: int32 [16, 256, 4], P(('dp', 'expert'), 'context'), may hold values from 0 to 7, all different within a row
- w_query: bfloat16 [2048, 2048], P(('dp', 'context', 'expert')), may hold values from -0.125 to 0.125
- w_key: bfloat16 [2048, 2048], P(('dp', 'context', 'expert')), may hold values from -0.125 to 0.125
- w_value: bfloat16 [2048, 2048], P(('dp', 'context', 'expert')), may hold values from -0.125 to 0.125
- w_out: bfloat16 [2048, 2048], P(('dp', 'context', 'expert')), may hold values from -1 to 1
- bias_query: bfloat16 [2048], P(('dp', 'context', 'expert')), may hold values from -3 to 3
- bias_key: bfloat16 [2048], P(('dp', 'context', 'expert')), may hold values from -3 to 3
- bias_value: bfloat16 [2048], P(('dp', 'context', 'expert')), may hold values from -3 to 3
- norm_attn: bfloat16 [2048], P(('dp', 'context', 'expert')), may hold values from 0.099609375 to 1.8984375
- norm_ffn: bfloat16 [2048], P(('dp', 'context', 'expert')), may hold values from 0.099609375 to 1.8984375
- w_router: bfloat16 [2048, 8], P(('dp', 'context', 'expert')), may hold values from -0.06591797 to 0.06591797
- shared_gate: bfloat16 [2048, 5632], P(('dp', 'context'), 'expert'), may hold values from -0.125 to 0.125
- shared_up: bfloat16 [2048, 5632], P(('dp', 'context'), 'expert'), may hold values from -0.125 to 0.125
- shared_down: bfloat16 [5632, 2048], P('expert', ('dp', 'context')), may hold values from -0.21875 to 0.21875
- shared_switch: bfloat16 [2048], P(('dp', 'context', 'expert')), may hold values from -0.125 to 0.125
- expert_gate: bfloat16 [8, 2048, 1408], P('expert', ('dp', 'context')), may hold values from -0.125 to 0.125
- expert_up: bfloat16 [8, 2048, 1408], P('expert', ('dp', 'context')), may hold values from -0.125 to 0.125
- expert_down: bfloat16 [8, 1408, 2048], P('expert', None, ('dp', 'context')), may hold values from -1.25 to 1.25
Outputs:
- out_tokens: bfloat16 [16, 256, 2048], P(('dp', 'expert'), 'context')
- grad_tokens: bfloat16 [16, 256, 2048], P(('dp', 'expert'), 'context')
- grad_w_query: float32 [2048, 2048], P(('dp', 'context', 'expert'))
- grad_w_key: float32 [2048, 2048], P(('dp', 'context', 'expert'))
- grad_w_value: float32 [2048, 2048], P(('dp', 'context', 'expert'))
- grad_w_out: float32 [2048, 2048], P(('dp', 'context', 'expert'))
- grad_bias_query: float32 [2048], P(('dp', 'context', 'expert'))
- grad_bias_key: float32 [2048], P(('dp', 'context', 'expert'))
- grad_bias_value: float32 [2048], P(('dp', 'context', 'expert'))
- grad_norm_attn: float32 [2048], P(('dp', 'context', 'expert'))
- grad_norm_ffn: float32 [2048], P(('dp', 'context', 'expert'))
- grad_router: float32 [2048, 8], P(('dp', 'context', 'expert'))
- grad_shared_gate: float32 [2048, 5632], P(('dp', 'context'), 'expert')
- grad_shared_up: float32 [2048, 5632], P(('dp', 'context'), 'expert')
- grad_shared_down: float32 [5632, 2048], P('expert', ('dp', 'context'))
- grad_shared_switch: float32 [2048], P(('dp', 'context', 'expert'))
- grad_expert_gate: float32 [8, 2048, 1408], P('expert', ('dp', 'context'))
- grad_expert_up: float32 [8, 2048, 1408], P('expert', ('dp', 'context'))
- grad_expert_down: float32 [8, 1408, 2048], P('expert', None, ('dp', 'context'))
Inputs may be any that keep to these rules, and one draw needn't show every extreme that they name: `deal_order`: each row is a permutation of the 256 places of a group. `seq_lengths`: the 2 lengths of a group sum to 256; the longest is at most 192. `expert_ids`: the 4 experts of a token differ.
All inputs are finite; a program needn't handle non-finite values.
Results may differ from a plain program's by a relative error of at most 0.022.
Values may be sent and summed in bfloat16 or wider, within the bound.
No kernel may reach another device: no remote copies, remote signals or barrier semaphores. Data moves between devices by JAX's collectives and lax.ppermute only.
A program may use at most 448 MiB of HBM per device.

v0:
```python
import jax
import jax.numpy as jnp
from jax import lax
from jax.sharding import PartitionSpec as P

HD = 128

EPSILON = 1e-06
ROPE_BASE = 1000000.0
NEGATIVE = -1e30
F32 = jnp.float32
BF16 = jnp.bfloat16


def mat_dot(left_mat, right_mat):
    return jnp.dot(left_mat, right_mat, preferred_element_type=F32)


def left_dot(left_mat, right_mat):
    return lax.dot_general(
        left_mat, right_mat, (((0,), (0,)), ((), ())), preferred_element_type=F32
    )


def right_dot(left_mat, right_mat):
    return lax.dot_general(
        left_mat, right_mat, (((1,), (1,)), ((), ())), preferred_element_type=F32
    )


def shift(x, axis, step):
    n = lax.axis_size(axis)
    return lax.ppermute(x, axis, [(i, (i + step) % n) for i in range(n)])


def plane_blocks():
    return (
        lax.axis_size("dp"),
        lax.axis_size("context"),
        lax.axis_index("dp"),
        lax.axis_index("context"),
    )


def plane_gather(x, axis):
    ndp, nc, dp, ctx = plane_blocks()
    half = x.shape[0] // 2
    size = x.shape[axis]
    shape = list(x.shape)
    shape[axis] = size * ndp * nc
    full = jnp.zeros(shape, x.dtype)

    def place(full, piece, d, s, offset):
        block = lax.rem(dp - d + ndp, ndp) * nc + lax.rem(ctx - s + nc, nc)
        start = [0] * x.ndim
        start[0] = offset
        start[axis] = start[axis] + block * size
        return lax.dynamic_update_slice(full, piece, start)

    across = {s: shift(x, "context", s) for s in range(1, nc)}
    along = {d: shift(x, "dp", d) for d in range(1, ndp)}
    full = place(full, x, 0, 0, 0)
    for s in across:
        full = place(full, across[s], 0, s, 0)
    for d in along:
        full = place(full, along[d], d, 0, 0)
    for s in across:
        for d in along:
            full = place(full, shift(across[s][:half], "dp", d), d, s, 0)
            full = place(full, shift(along[d][half:], "context", s), d, s, half)
    return full


def plane_scatter(block_of, half):
    ndp, nc, dp, ctx = plane_blocks()

    def term(d, s):
        return block_of(lax.rem(dp + d, ndp) * nc + lax.rem(ctx + s, nc))

    first, second = {}, {}
    for d in range(1, ndp):
        for s in range(1, nc):
            far = term(d, s).astype(BF16)
            got = shift(far[:half], "context", s).astype(F32)
            first[d] = got if d not in first else first[d] + got
            got = shift(far[half:], "dp", d).astype(F32)
            second[s] = got if s not in second else second[s] + got
    upper, lower = [], []
    for d in range(1, ndp):
        near = term(d, 0)
        lower.append(shift(near[half:].astype(BF16), "dp", d))
        upper.append(shift((near[:half] + first[d]).astype(BF16), "dp", d))
    for s in range(1, nc):
        near = term(0, s)
        upper.append(shift(near[:half].astype(BF16), "context", s))
        lower.append(shift((near[half:] + second[s]).astype(BF16), "context", s))
    own = term(0, 0)
    top, bottom = own[:half], own[half:]
    for piece in upper:
        top = top + piece.astype(F32)
    for piece in lower:
        bottom = bottom + piece.astype(F32)
    return jnp.concatenate([top, bottom], 0)


def doubling_steps(axis):
    n = lax.axis_size(axis)
    step = 1
    while step < n:
        yield step, [(i, i ^ step) for i in range(n)]
        step *= 2


def small_gather(x):
    for axis in ("expert", "context", "dp"):
        place = lax.axis_index(axis)
        for step, pairs in doubling_steps(axis):
            other = lax.ppermute(x, axis, pairs)
            high = (place & step) != 0
            x = jnp.concatenate([jnp.where(high, other, x), jnp.where(high, x, other)], 0)
    return x


def small_scatter(x):
    for axis in ("dp", "context", "expert"):
        place = lax.axis_index(axis)
        for step, pairs in reversed(list(doubling_steps(axis))):
            half = x.shape[0] // 2
            high = (place & step) != 0
            low_part, high_part = x[:half], x[half:]
            other = lax.ppermute(jnp.where(high, low_part, high_part), axis, pairs)
            x = jnp.where(high, high_part, low_part) + other
    return x[0]


def core_exchange(x, group):
    count = lax.axis_size("expert")
    place = lax.rem(lax.axis_index("expert"), group)
    out = x
    for s in range(1, group):
        piece = lax.dynamic_slice_in_dim(x, lax.rem(place + s, group), 1)
        pairs = [(i, i // group * group + (i % group + s) % group) for i in range(count)]
        got = lax.ppermute(piece, "expert", pairs)
        out = lax.dynamic_update_slice_in_dim(out, got, lax.rem(place - s + group, group), 0)
    return out


def rotate(vals, cosine, sine_table):
    halfway = HD // 2
    turned = jnp.concatenate([-vals[..., halfway:], vals[..., :halfway]], -1)
    return vals * cosine[:, None, :] + turned * sine_table[:, None, :]


def rotate_back(grads, cosine, sine_table):
    halfway = HD // 2
    scaled = grads * sine_table[:, None, :]
    turned = jnp.concatenate([scaled[..., halfway:], -scaled[..., :halfway]], -1)
    return grads * cosine[:, None, :] + turned


def rms_unit(values):
    scaling = lax.rsqrt(jnp.mean(values * values, -1, keepdims=True) + EPSILON)
    return values * scaling, scaling


def body(
    tokens,
    cotangent,
    deal_order,
    seq_lengths,
    expert_ids,
    w_query,
    w_key,
    w_value,
    w_out,
    bias_query,
    bias_key,
    bias_value,
    norm_attn,
    norm_ffn,
    w_router,
    shared_gate,
    shared_up,
    shared_down,
    shared_switch,
    expert_gate,
    expert_up,
    expert_down,
):
    ndp, nc, dp, ctx = plane_blocks()
    planes = ndp * nc
    count = lax.axis_size("expert")
    here = lax.axis_index("expert")
    tok_count, width = tokens.shape[1], tokens.shape[2]
    group_tok = deal_order.shape[1]
    seqs = seq_lengths.shape[1]
    top = expert_ids.shape[2]
    rows_flat = w_query.shape[0]
    part = HD // rows_flat
    heads = planes // part
    runs = count // part
    run, member = here // part, lax.rem(here, part)
    fe_width = expert_gate.shape[2]
    fs_width = shared_gate.shape[1]
    hidden_width = fe_width + fs_width
    capacity = min(tok_count, 5 * tok_count * top // (4 * count))
    wide = heads * HD
    all_rows = count * tok_count

    token_rows = tokens[0]
    all_tokens = lax.all_gather(token_rows, "expert", axis=0, tiled=True)

    def by_head(w):
        w = w.reshape(rows_flat, part, heads, runs, HD).transpose(3, 1, 0, 2, 4)
        return w.reshape(count, rows_flat, wide)

    qkv_out = jnp.concatenate([by_head(w) for w in (w_query, w_key, w_value)], -1)
    qkv_rows = lax.all_to_all(qkv_out, "expert", split_axis=0, concat_axis=0, tiled=True)
    w_qkv = plane_gather(qkv_rows.reshape(count * rows_flat, 3 * wide), 0)
    wo_planes = plane_gather(w_out[None].reshape(rows_flat, width), 0)
    wo_mine = core_exchange(wo_planes.reshape(part, heads, rows_flat, width), part)
    w_o = wo_mine.transpose(1, 0, 2, 3).reshape(wide, width)

    small = jnp.concatenate(
        [
            v.astype(F32).reshape(-1)
            for v in (
                bias_query,
                bias_key,
                bias_value,
                norm_attn,
                norm_ffn,
                shared_switch,
                w_router,
                deal_order,
                seq_lengths,
                expert_ids,
            )
        ]
    )
    small_all = small_gather(small[None])
    columns = {}
    place = 0
    for name in ("bq", "bk", "bv", "na", "nf", "sw"):
        columns[name] = small_all[:, place : place + rows_flat].reshape(-1)
        place += rows_flat
    router = small_all[:, place : place + rows_flat * count].reshape(-1, count).astype(BF16)
    place += rows_flat * count
    plane_small = lax.dynamic_index_in_dim(
        small_all.reshape(ndp, nc, count, -1), dp, 0, keepdims=False
    )
    order = plane_small[0, :, place : place + group_tok].astype(jnp.int32)
    place += group_tok
    lengths = plane_small[0, :, place : place + seqs].astype(jnp.int32)
    place += seqs
    ids = plane_small[..., place:].reshape(nc, count, tok_count, top).astype(jnp.int32)
    gain_attn, gain_ffn = columns["na"], columns["nf"]
    router_switch = jnp.concatenate([router, columns["sw"].astype(BF16)[:, None]], 1)

    all_grads = lax.all_gather(cotangent[0], "expert", axis=0, tiled=True)

    gate_own = jnp.concatenate([expert_gate[0], shared_gate], 1)
    up_own = jnp.concatenate([expert_up[0], shared_up], 1)
    down_own = jnp.concatenate([expert_down[0], shared_down], 0)
    w_down = plane_gather(down_own, 1)
    w_gate = plane_gather(gate_own, 0)
    w_up = plane_gather(up_own, 0)

    hit = jnp.any(ids == here, -1)
    below = jnp.arange(tok_count)[:, None] < jnp.arange(tok_count)[None, :]
    slot = mat_dot(hit.reshape(nc * count, tok_count).astype(BF16), below.astype(BF16))
    kept = (hit & (slot.reshape(nc, count, tok_count) < capacity)).astype(F32)
    kept = kept.transpose(1, 0, 2).reshape(count, group_tok)
    local_index = ctx * tok_count + jnp.arange(tok_count, dtype=jnp.int32)
    kept_rows = jnp.sum(
        jnp.where(order[:, None, :] == local_index[None, :, None], kept[:, None, :], 0.0), -1
    ).reshape(all_rows)

    ends = jnp.cumsum(lengths, 1)
    starts = ends - lengths

    def segments(index):
        segment = jnp.sum((index[None, :, None] >= ends[:, None, :]).astype(jnp.int32), -1)
        hot = segment[..., None] == jnp.arange(seqs, dtype=jnp.int32)
        return segment, index[None, :] - jnp.sum(jnp.where(hot, starts[:, None, :], 0), -1)

    query_segment, position = segments(local_index)
    allowed = []
    for s in range(nc):
        key_index = local_index - s * tok_count
        key_segment, _ = segments(key_index)
        allowed.append(
            (query_segment[:, :, None] == key_segment[:, None, :])
            & (key_index[None, None, :] <= local_index[None, :, None])
            & (key_index >= 0)[None, None, :]
        )
    allowed = jnp.concatenate(allowed, -1)[:, None]
    frequency = ROPE_BASE ** (-2.0 * jnp.arange(HD // 2, dtype=F32) / HD)
    angles = position.reshape(-1).astype(F32)[:, None] * frequency[None, :]
    cosine = jnp.concatenate([jnp.cos(angles)] * 2, -1)
    sine_table = jnp.concatenate([jnp.sin(angles)] * 2, -1)

    unit_all, _ = rms_unit(all_tokens.astype(F32))
    normed = (unit_all * gain_attn).astype(BF16)

    def own_heads(row):
        row = row.reshape(part, heads, runs, HD)
        row = lax.dynamic_index_in_dim(row, member, 0, keepdims=False)
        return lax.dynamic_index_in_dim(row, run, 1, keepdims=False).reshape(-1)

    bias = jnp.concatenate([own_heads(columns[k]) for k in ("bq", "bk", "bv")])
    qkv = mat_dot(normed, w_qkv) + bias
    query_heads = rotate(qkv[:, :wide].reshape(all_rows, heads, HD), cosine, sine_table)
    key_heads = rotate(qkv[:, wide : 2 * wide].reshape(all_rows, heads, HD), cosine, sine_table)
    key_value = jnp.concatenate(
        [key_heads.reshape(all_rows, wide), qkv[:, 2 * wide :]], -1
    ).astype(BF16)
    earlier = [key_value] + [
        lax.ppermute(key_value, "context", [(i, i + s) for i in range(nc - s)])
        for s in range(1, nc)
    ]
    keyed = jnp.concatenate([kv.reshape(count, tok_count, 2 * wide) for kv in earlier], 1)
    keys = keyed[..., :wide].reshape(count, nc * tok_count, heads, HD)
    values = keyed[..., wide:].reshape(count, nc * tok_count, heads, HD)
    queries = query_heads.astype(BF16).reshape(count, tok_count, heads, HD)
    scores = jnp.einsum("gqhd,gkhd->ghqk", queries, keys, preferred_element_type=F32)
    scores = jnp.where(allowed, scores * HD ** (-0.5), NEGATIVE)
    expo = jnp.exp(scores - jnp.max(scores, -1, keepdims=True))
    prob = expo / jnp.sum(expo, -1, keepdims=True)
    prob_low = prob.astype(BF16)
    mixed = jnp.einsum("ghqk,gkhd->gqhd", prob_low, values, preferred_element_type=F32)
    mixed = mixed.astype(BF16).reshape(all_rows, wide)
    attn_out = lax.psum_scatter(
        mat_dot(mixed, w_o).astype(BF16), "expert", scatter_dimension=0, tiled=True
    )
    residual = token_rows.astype(F32) + attn_out.astype(F32)
    unit_two, scale_two = rms_unit(residual)
    rows = lax.all_gather(
        (unit_two * gain_ffn).astype(BF16), "expert", axis=0, tiled=True
    )

    grad_hidden = right_dot(all_grads, w_down)
    logits = mat_dot(rows, router_switch)
    prob_router = jax.nn.softmax(logits[:, :count], -1)
    switch = jax.nn.sigmoid(logits[:, count])
    own_hot = (jnp.arange(count) == here).astype(F32)[None, :]
    prob_own = jnp.sum(prob_router * own_hot, 1)
    share = prob_own * kept_rows
    is_expert = (jnp.arange(hidden_width) < fe_width)[None, :]
    scale = jnp.where(is_expert, share[:, None], switch[:, None])
    gate_x = mat_dot(rows, w_gate)
    up_x = mat_dot(rows, w_up)
    sig = jax.nn.sigmoid(gate_x)
    hidden = gate_x * sig * up_x
    product = grad_hidden * hidden
    grad_share = jnp.sum(product[:, :fe_width], 1)
    grad_switch = jnp.sum(product[:, fe_width:], 1)
    scaled = (scale * hidden).astype(BF16)
    grad_scaled = scale * grad_hidden
    grad_gate = (grad_scaled * up_x * sig * (1.0 + gate_x * (1.0 - sig))).astype(BF16)
    grad_up = (grad_scaled * gate_x * sig).astype(BF16)
    grad_small = jnp.concatenate(
        [
            (grad_share * share)[:, None] * (own_hot - prob_router),
            (grad_switch * switch * (1.0 - switch))[:, None],
        ],
        1,
    ).astype(BF16)
    grad_rows = (
        right_dot(grad_gate, w_gate) + right_dot(grad_up, w_up) + right_dot(grad_small, router_switch)
    )
    grad_normed_two = lax.psum_scatter(
        grad_rows.astype(BF16), "expert", scatter_dimension=0, tiled=True
    ).astype(F32)
    grad_router_switch = left_dot(rows, grad_small)

    block = width // planes

    def row_blocks(acts, grads):
        def block_of(r):
            return left_dot(lax.dynamic_slice_in_dim(acts, r * block, block, 1), grads)

        return block_of

    def down_blocks(r):
        return left_dot(scaled, lax.dynamic_slice_in_dim(all_grads, r * block, block, 1))

    grad_down_w = plane_scatter(down_blocks, hidden_width // 2)
    grad_gate_w = plane_scatter(row_blocks(rows, grad_gate), block // 2)
    grad_up_w = plane_scatter(row_blocks(rows, grad_up), block // 2)
    output = lax.psum_scatter(
        mat_dot(scaled, w_down).astype(BF16), "expert", scatter_dimension=0, tiled=True
    )
    out_tokens = (residual + output.astype(F32)).astype(BF16)

    grad_unit = grad_normed_two * gain_ffn
    grad_residual = cotangent[0].astype(F32) + scale_two * (
        grad_unit - unit_two * jnp.mean(grad_unit * unit_two, -1, keepdims=True)
    )
    grad_gain_ffn = jnp.sum(grad_normed_two * unit_two, 0)
    grad_attn = lax.all_gather(grad_residual.astype(BF16), "expert", axis=0, tiled=True)
    grad_mixed = (
        right_dot(grad_attn, w_o).astype(BF16).reshape(count, tok_count, heads, HD)
    )
    grad_value = jnp.einsum("ghqk,gqhd->gkhd", prob_low, grad_mixed, preferred_element_type=F32)
    grad_probs = jnp.einsum("gqhd,gkhd->ghqk", grad_mixed, values, preferred_element_type=F32)
    inner = jnp.sum(grad_probs * prob, -1, keepdims=True)
    grad_scores = (prob * (grad_probs - inner)).astype(BF16)
    grad_query = HD ** (-0.5) * jnp.einsum(
        "ghqk,gkhd->gqhd", grad_scores, keys, preferred_element_type=F32
    )
    grad_key = HD ** (-0.5) * jnp.einsum(
        "ghqk,gqhd->gkhd", grad_scores, queries, preferred_element_type=F32
    )
    grad_kv = jnp.concatenate([grad_key, grad_value], 2)
    kv_sum = grad_kv[:, :tok_count].reshape(all_rows, 2 * wide)
    for s in range(1, nc):
        piece = grad_kv[:, s * tok_count : (s + 1) * tok_count].reshape(all_rows, 2 * wide)
        kv_sum = kv_sum + lax.ppermute(
            piece.astype(BF16), "context", [(i + s, i) for i in range(nc - s)]
        ).astype(F32)
    grad_query = rotate_back(grad_query.reshape(all_rows, heads, HD), cosine, sine_table)
    grad_key = rotate_back(kv_sum[:, :wide].reshape(all_rows, heads, HD), cosine, sine_table)
    grad_qkv = jnp.concatenate(
        [grad_query.reshape(all_rows, wide), grad_key.reshape(all_rows, wide), kv_sum[:, wide:]],
        -1,
    ).astype(BF16)
    grad_normed = right_dot(grad_qkv, w_qkv)
    grad_normed_own = lax.psum_scatter(
        grad_normed.astype(BF16), "expert", scatter_dimension=0, tiled=True
    ).astype(F32)

    qkv_grad_rows = plane_scatter(row_blocks(normed, grad_qkv), block // 2)
    qkv_back = lax.all_to_all(
        qkv_grad_rows.astype(BF16).reshape(count, rows_flat, 3 * wide),
        "expert",
        split_axis=0,
        concat_axis=0,
        tiled=True,
    )

    def from_heads(i):
        w = qkv_back[..., i * wide : (i + 1) * wide].astype(F32)
        w = w.reshape(runs, part, rows_flat, heads, HD).transpose(2, 1, 3, 0, 4)
        return w.reshape(rows_flat, width)

    grad_wo = left_dot(mixed, grad_attn).astype(BF16).reshape(heads, part, rows_flat, width)
    wo_back = core_exchange(grad_wo.transpose(1, 0, 2, 3), part)
    wo_back = wo_back.reshape(planes, rows_flat, width)
    grad_w_out = plane_scatter(
        lambda r: lax.dynamic_index_in_dim(wo_back, r, 0, keepdims=False).astype(F32),
        rows_flat // 2,
    )

    def to_heads(row):
        full = jnp.zeros((part, heads, runs, HD), F32)
        full = lax.dynamic_update_slice(
            full, row.reshape(1, heads, 1, HD), (member, 0, run, 0)
        )
        return full.reshape(planes * count, rows_flat)

    bias_sums = jnp.sum(grad_qkv.astype(F32), 0)
    grad_gain_attn = jnp.sum(grad_normed * unit_all, 0)
    small_grads = jnp.concatenate(
        [to_heads(bias_sums[i * wide : (i + 1) * wide]) for i in range(3)]
        + [
            grad_gain_attn.reshape(-1, rows_flat),
            grad_gain_ffn.reshape(-1, rows_flat),
            grad_router_switch[:, count].reshape(-1, rows_flat),
            grad_router_switch[:, :count].reshape(planes * count, rows_flat * count),
        ],
        1,
    )
    small_sum = small_scatter(small_grads)
    pieces = [small_sum[i * rows_flat : (i + 1) * rows_flat] for i in range(6)]
    grad_router = small_sum[6 * rows_flat :].reshape(rows_flat, count)

    unit_one, scale_one = rms_unit(token_rows.astype(F32))
    grad_unit = grad_normed_own * gain_attn
    grad_tokens = grad_residual + scale_one * (
        grad_unit - unit_one * jnp.mean(grad_unit * unit_one, -1, keepdims=True)
    )
    return (
        out_tokens[None],
        grad_tokens.astype(BF16)[None],
        from_heads(0),
        from_heads(1),
        from_heads(2),
        grad_w_out,
        pieces[0],
        pieces[1],
        pieces[2],
        pieces[3],
        pieces[4],
        grad_router,
        grad_gate_w[:, fe_width:],
        grad_up_w[:, fe_width:],
        grad_down_w[fe_width:],
        pieces[5],
        grad_gate_w[None, :, :fe_width],
        grad_up_w[None, :, :fe_width],
        grad_down_w[None, :fe_width],
    )


def solution(mesh):
    every = ("dp", "context", "expert")
    plane = ("dp", "context")
    rows = P(("dp", "expert"), "context", None)
    groups = P(("dp", "expert"), None)
    return jax.shard_map(
        body,
        mesh=mesh,
        in_specs=(
            rows,
            rows,
            groups,
            groups,
            rows,
            *[P(every, None)] * 4,
            *[P(every)] * 5,
            P(every, None),
            P(plane, "expert"),
            P(plane, "expert"),
            P("expert", plane),
            P(every),
            P("expert", plane, None),
            P("expert", plane, None),
            P("expert", None, plane),
        ),
        out_specs=(
            rows,
            rows,
            *[P(every, None)] * 4,
            *[P(every)] * 5,
            P(every, None),
            P(plane, "expert"),
            P(plane, "expert"),
            P("expert", plane),
            P(every),
            P("expert", plane, None),
            P("expert", plane, None),
            P("expert", None, plane),
        ),
        check_vma=False,
    )
```

profile of v0, /device:TPU:0, one launch (start us, length us, event | category | flops | bytes accessed | tf_op | source)
XLA Modules:
  0.0 1092.5 jit_solution(3095176129138211232)
XLA Ops:
  31.2 24.6 %collective-permute-done.1 = f32[2,1666]{1,0:T(2,128)S(1)} collective-permute-done((f32[2,1666]{1,0:T(2,128)S(1)}, f32[2,1666]{1,0:T(2,128)S(1)}, u32[]{:S(2)}, u32[]{:S(2)}) %collective-permute-start.1) | collective-permute-done | bytes 13360 | tf_op jit(solution)/shard_map/ppermute | solution.py:118
  60.6 12.1 %collective-permute-done.2 = f32[4,1666]{1,0:T(4,128)S(1)} collective-permute-done((f32[4,1666]{1,0:T(4,128)S(1)}, f32[4,1666]{1,0:T(4,128)S(1)}, u32[]{:S(2)}, u32[]{:S(2)}) %collective-permute-start.2) | collective-permute-done | bytes 26688 | tf_op jit(solution)/shard_map/ppermute | solution.py:118
  101.7 11.8 %collective-permute-done.6 = bf16[512,768]{1,0:T(8,128)(2,1)} collective-permute-done((bf16[512,768]{1,0:T(8,128)(2,1)S(1)}, bf16[512,768]{1,0:T(8,128)(2,1)}, u32[]{:S(2)}, u32[]{:S(2)}) %collective-permute-start.6) | collective-permute-done | bytes 786464 | tf_op jit(solution)/shard_map/ppermute | solution.py:33
  133.6 7.0 convolution_add_fusion
  161.5 19.7 %collective-permute-done.9 = bf16[1024,512]{0,1:T(8,128)(2,1)S(1)} collective-permute-done((bf16[1024,512]{0,1:T(8,128)(2,1)S(1)}, bf16[1024,512]{0,1:T(8,128)(2,1)S(1)}, u32[]{:S(2)}, u32[]{:S(2)}) %collective-permute-start.9) | collective-permute-done | bytes 1048608 | tf_op jit(solution)/shard_map/ppermute | solution.py:319
  191.5 48.9 %reduce-scatter.5.cloned.1.call-done = bf16[128,2048]{1,0:T(8,128)(2,1)} async-done(((bf16[1024,2048]{1,0:T(8,128)(2,1)}), bf16[128,2048]{1,0:T(8,128)(2,1)}) %reduce-scatter.5.cloned.1.call-update) | async-done | bytes 524304 | tf_op jit(solution)/shard_map/reduce_scatter | solution.py:333
  275.7 27.1 %collective-permute-done.19 = bf16[512,2112]{0,1:T(8,128)(2,1)} collective-permute-done((bf16[512,2112]{0,1:T(8,128)(2,1)}, bf16[512,2112]{0,1:T(8,128)(2,1)}, u32[]{:S(2)}, u32[]{:S(2)}) %collective-permute-start.19) | collective-permute-done | bytes 2162720 | tf_op jit(solution)/shard_map/ppermute | solution.py:33
  314.3 34.8 %collective-permute-done.23 = bf16[2112,512]{1,0:T(8,128)(2,1)} collective-permute-done((bf16[2112,512]{1,0:T(8,128)(2,1)}, bf16[2112,512]{1,0:T(8,128)(2,1)}, u32[]{:S(2)}, u32[]{:S(2)}) %collective-permute-start.23) | collective-permute-done | bytes 2162720 | tf_op jit(solution)/shard_map/ppermute | solution.py:33
  361.1 34.3 %collective-permute-done.15 = bf16[512,2112]{0,1:T(8,128)(2,1)S(1)} collective-permute-done((bf16[512,2112]{0,1:T(8,128)(2,1)}, bf16[512,2112]{0,1:T(8,128)(2,1)S(1)}, u32[]{:S(2)}, u32[]{:S(2)}) %collective-permute-start.15) | collective-permute-done | bytes 2162720 | tf_op jit(solution)/shard_map/ppermute | solution.py:33
  401.6 41.5 %collective-permute-done.25 = bf16[1056,512]{1,0:T(8,128)(2,1)S(1)} collective-permute-done((bf16[1056,512]{1,0:T(8,128)(2,1)S(1)}, bf16[1056,512]{1,0:T(8,128)(2,1)S(1)}, u32[]{:S(2)}, u32[]{:S(2)}) %collective-permute-start.25) | collective-permute-done | bytes 1081376 | tf_op jit(solution)/shard_map/ppermute | solution.py:33
  448.4 14.3 %collective-permute-done.17 = bf16[256,2112]{0,1:T(8,128)(2,1)S(1)} collective-permute-done((bf16[256,2112]{0,1:T(8,128)(2,1)S(1)}, bf16[256,2112]{0,1:T(8,128)(2,1)S(1)}, u32[]{:S(2)}, u32[]{:S(2)}) %collective-permute-start.17) | collective-permute-done | bytes 1081376 | tf_op jit(solution)/shard_map/ppermute | solution.py:33
  464.9 16.3 %fusion.176 = f32[1024,2112]{0,1:T(8,128)} fusion(bf16[1024,2048]{1,0:T(8,128)(2,1)} %all-gather.7.cloned.1.call-done, bf16[2048,2112]{0,1:T(8,128)(2,1)} %constant_dynamic-update-slice_fusion.5), kind=kOutput, calls=%fused_computation.412 | convolution fusion | flops 8858370048 | bytes 21495808 | tf_op jit(solution)/shard_map/dot_general | solution.py:16
  481.2 13.7 %fusion.175 = f32[1024,2112]{0,1:T(8,128)} fusion(bf16[1024,2048]{1,0:T(8,128)(2,1)S(1)} %copy-done, bf16[2048,2112]{0,1:T(8,128)(2,1)} %constant_dynamic-update-slice_fusion.10), kind=kOutput, calls=%fused_computation.411 | convolution fusion | flops 8858370048 | bytes 21495808 | tf_op jit(solution)/shard_map/dot_general | solution.py:16
  494.9 22.2 %bitcast_multiply_fusion = (f32[1024,2112]{0,1:T(8,128)}, f32[2112,1024]{1,0:T(8,128)}) fusion(f32[1024,2112]{0,1:T(8,128)} %fusion.176, f32[1024,2112]{0,1:T(8,128)} %fusion.175, bf16[2112,2048]{1,0:T(8,128)(2,1)} %constant_dynamic-update-slice_fusion.26, bf16[1,1024,2048]{2,1,0:T(8,128)(2,1)} %all-gather.13.cloned.1.call-done), kind=kOutput, calls=%fused_computation.8 | convolution fusion | flops 8871346176 | bytes 47448064 | tf_op jit(solution)/shard_map/dot_general | solution.py:26
  524.4 15.2 %multiply_convert_fusion.1 = (bf16[1024,2112]{0,1:T(8,128)(2,1)}, bf16[1024,2112]{0,1:T(8,128)(2,1)}, bf16[1024,2112]{0,1:T(8,128)(2,1)S(1)}) fusion(f32[1024,2112]{0,1:T(8,128)} %fusion.175, f32[1024,2112]{0,1:T(8,128)} %fusion.176, f32[2112,1024]{1,0:T(8,128)} %get-tuple-element.234, f32[1024]{0:T(1024)S(1)} %bitcast.367, f32[1024]{0:T(1024)S(1)} %get-tuple-element.139, ...), kind=kLoop, calls=%fused_computation.10 | loop fusion | flops 41091072 | bytes 38938688 | tf_op jit(solution)/shard_map/convert_element_type | solution.py:360
  539.6 16.1 %fusion.177 = f32[1024,2048]{1,0:T(8,128)} fusion(bf16[1024,2112]{0,1:T(8,128)(2,1)S(1)} %get-tuple-element.144, bf16[2048,2112]{0,1:T(8,128)(2,1)} %constant_dynamic-update-slice_fusion.5), kind=kOutput, calls=%fused_computation.413 | convolution fusion | flops 8858370048 | bytes 21364736 | tf_op jit(solution)/shard_map/dot_general | solution.py:26
  557.0 17.4 %add_convert_fusion = bf16[1024,2048]{1,0:T(8,128)(2,1)} fusion(f32[1024,2048]{1,0:T(8,128)S(1)} %fusion.119, f32[1024,2048]{1,0:T(8,128)} %fusion.177, bf16[1024,2112]{0,1:T(8,128)(2,1)} %get-tuple-element.142, bf16[2048,2112]{0,1:T(8,128)(2,1)} %constant_dynamic-update-slice_fusion.10), kind=kOutput, calls=%fused_computation.16 | convolution fusion | flops 8864661504 | bytes 33947648 | tf_op jit(solution)/shard_map/dot_general | solution.py:26
  574.4 51.3 %reduce-scatter.9.cloned.1.call-done = bf16[128,2048]{1,0:T(8,128)(2,1)} async-done(((bf16[1024,2048]{1,0:T(8,128)(2,1)}), bf16[128,2048]{1,0:T(8,128)(2,1)}) %reduce-scatter.9.cloned.1.call-update) | async-done | bytes 524304 | tf_op jit(solution)/shard_map/reduce_scatter | solution.py:372
  630.3 45.4 %all-gather.9.cloned.1.call-done = bf16[1024,2048]{1,0:T(8,128)(2,1)} async-done(((bf16[128,2048]{1,0:T(8,128)(2,1)}), bf16[1024,2048]{1,0:T(8,128)(2,1)}) %all-gather.9.cloned.1.call-update) | async-done | bytes 4194320 | tf_op jit(solution)/shard_map/all_gather | solution.py:401
  697.6 17.1 %collective-permute-done.27 = bf16[1024,512]{0,1:T(8,128)(2,1)} collective-permute-done((bf16[1024,512]{0,1:T(8,128)(2,1)}, bf16[1024,512]{0,1:T(8,128)(2,1)}, u32[]{:S(2)}, u32[]{:S(2)}) %collective-permute-start.27) | collective-permute-done | bytes 1048608 | tf_op jit(solution)/shard_map/ppermute | solution.py:419
  732.4 8.0 fusion.5
  781.2 14.0 %convolution_convert_fusion.3 = bf16[1024,2048]{1,0:T(8,128)(2,1)} fusion(bf16[1024,2112]{0,1:T(8,128)(2,1)S(1)} %bitcast.320, bf16[2112,2048]{1,0:T(8,128)(2,1)} %constant_dynamic-update-slice_fusion.26), kind=kOutput, calls=%fused_computation.25 | convolution fusion | flops 8860467200 | bytes 17170432 | tf_op jit(solution)/shard_map/dot_general | solution.py:16
  826.5 17.2 %collective-permute-done.56 = bf16[256,2112]{0,1:T(8,128)(2,1)} collective-permute-done((bf16[256,2112]{0,1:T(8,128)(2,1)}, bf16[256,2112]{0,1:T(8,128)(2,1)}, u32[]{:S(2)}, u32[]{:S(2)}) %collective-permute-start.56) | collective-permute-done | bytes 1081376 | tf_op jit(solution)/shard_map/ppermute | solution.py:33
  852.3 14.5 %collective-permute-done.49 = bf16[256,2112]{0,1:T(8,128)(2,1)S(1)} collective-permute-done((bf16[256,2112]{0,1:T(8,128)(2,1)}, bf16[256,2112]{0,1:T(8,128)(2,1)S(1)}, u32[]{:S(2)}, u32[]{:S(2)}) %collective-permute-start.49) | collective-permute-done | bytes 1081376 | tf_op jit(solution)/shard_map/ppermute | solution.py:33
  869.6 20.5 %collective-permute-done.47 = bf16[256,2112]{0,1:T(8,128)(2,1)S(1)} collective-permute-done((bf16[256,2112]{0,1:T(8,128)(2,1)S(1)}, bf16[256,2112]{0,1:T(8,128)(2,1)S(1)}, u32[]{:S(2)}, u32[]{:S(2)}) %collective-permute-start.47) | collective-permute-done | bytes 1081376 | tf_op jit(solution)/shard_map/ppermute | solution.py:33
  895.2 18.0 %collective-permute-done.55 = bf16[256,2112]{0,1:T(8,128)(2,1)S(1)} collective-permute-done((bf16[256,2112]{0,1:T(8,128)(2,1)S(1)}, bf16[256,2112]{0,1:T(8,128)(2,1)S(1)}, u32[]{:S(2)}, u32[]{:S(2)}) %collective-permute-start.55) | collective-permute-done | bytes 1081376 | tf_op jit(solution)/shard_map/ppermute | solution.py:33
  915.9 20.5 %collective-permute-done.53 = bf16[256,2112]{0,1:T(8,128)(2,1)S(1)} collective-permute-done((bf16[256,2112]{0,1:T(8,128)(2,1)}, bf16[256,2112]{0,1:T(8,128)(2,1)S(1)}, u32[]{:S(2)}, u32[]{:S(2)}) %collective-permute-start.53) | collective-permute-done | bytes 1081376 | tf_op jit(solution)/shard_map/ppermute | solution.py:33
  944.2 15.3 %collective-permute-done.58 = bf16[1056,512]{1,0:T(8,128)(2,1)S(1)} collective-permute-done((bf16[1056,512]{1,0:T(8,128)(2,1)S(1)}, bf16[1056,512]{1,0:T(8,128)(2,1)S(1)}, u32[]{:S(2)}, u32[]{:S(2)}) %collective-permute-start.58) | collective-permute-done | bytes 1081376 | tf_op jit(solution)/shard_map/ppermute | solution.py:33
  963.4 17.5 %collective-permute-done.62 = bf16[1056,512]{1,0:T(8,128)(2,1)S(1)} collective-permute-done((bf16[1056,512]{1,0:T(8,128)(2,1)}, bf16[1056,512]{1,0:T(8,128)(2,1)S(1)}, u32[]{:S(2)}, u32[]{:S(2)}) %collective-permute-start.62) | collective-permute-done | bytes 1081376 | tf_op jit(solution)/shard_map/ppermute | solution.py:33
  1021.6 7.8 collective-permute-done.28
  1040.4 6.2 collective-permute-done.29
  1055.9 18.0 %all-to-all-done.1 = bf16[8,64,768]{2,1,0:T(8,128)(2,1)S(1)} async-done(((bf16[8,64,768]{2,1,0:T(8,128)(2,1)}), bf16[8,64,768]{2,1,0:T(8,128)(2,1)S(1)}, u32[]{:S(2)}, u32[]{:S(2)}) %all-to-all-start.1) | async-done | bytes 786464 | tf_op jit(solution)/shard_map/all_to_all | solution.py:434
  (615 shorter events, 408.0 us)
Async XLA Ops:
  7.2 121.9 %all-gather.11.cloned.1.call-start = ((), (), s32[]{:S(2)}) async-start(), calls=%async_computation.12 | async-start | bytes 4718592 | tf_op jit(solution)/shard_map/all_gather | solution.py:211
  7.2 78.6 %collective-permute-start.11 = (bf16[64,2048]{1,0:T(8,128)(2,1)}, bf16[64,2048]{1,0:T(8,128)(2,1)S(1)}, u32[]{:S(2)}, u32[]{:S(2)}) collective-permute-start(bf16[64,2048]{1,0:T(8,128)(2,1)} %param.30), channel_id=1, source_target_pairs={{0,16},{16,0},{1,17},{17,1},{2,18},{18,2},{3,19},{19,3},{4,20},{20... | collective-permute-start | bytes 786440 | tf_op jit(solution)/shard_map/ppermute | solution.py:33
  10.3 76.3 %collective-permute-start.10 = (bf16[64,2048]{1,0:T(8,128)(2,1)}, bf16[64,2048]{1,0:T(8,128)(2,1)}, u32[]{:S(2)}, u32[]{:S(2)}) collective-permute-start(bf16[64,2048]{1,0:T(8,128)(2,1)} %param.30), channel_id=1, source_target_pairs={{0,8},{8,0},{1,9},{9,1},{2,10},{10,2},{3,11},{11,3},{4,12},{12,4},... | collective-permute-start | bytes 786440 | tf_op jit(solution)/shard_map/ppermute | solution.py:33
  23.6 69.8 %all-to-all-start = ((bf16[8,64,768]{2,1,0:T(8,128)(2,1)}), bf16[8,64,768]{2,1,0:T(8,128)(2,1)S(1)}, u32[]{:S(2)}, u32[]{:S(2)}) async-start(bf16[8,64,768]{2,1,0:T(8,128)(2,1)} %pad_maximum_fusion.14), calls=%async_computation | async-start | bytes 1572864 | tf_op jit(solution)/shard_map/all_to_all | solution.py:218
  28.6 211.8 %reduce-scatter.5.cloned.1.call-start = ((), (), s32[]{:S(2)}) async-start(), calls=%async_computation.6 | async-start | bytes 4718592 | tf_op jit(solution)/shard_map/reduce_scatter | solution.py:333
  191.4 273.5 %all-gather.7.cloned.1.call-start = ((), (), s32[]{:S(2)}) async-start(), calls=%async_computation.7 | async-start | bytes 4718592 | tf_op jit(solution)/shard_map/all_gather | solution.py:338
  243.8 251.1 %all-gather.13.cloned.1.call-start = ((), (), s32[]{:S(2)}) async-start(), calls=%async_computation.13 | async-start | bytes 4718592 | tf_op jit(solution)/shard_map/all_gather | solution.py:260
  252.5 50.3 %collective-permute-start.19 = (bf16[512,2112]{0,1:T(8,128)(2,1)}, bf16[512,2112]{0,1:T(8,128)(2,1)}, u32[]{:S(2)}, u32[]{:S(2)}) collective-permute-start(bf16[512,2112]{0,1:T(8,128)(2,1)} %get-tuple-element.164), channel_id=1, source_target_pairs={{0,8},{8,0},{1,9},{9,1},{2,10},{10,2},{3,11},{11,3},{4,12},{12,4},... | collective-permute-start | bytes 6488072 | tf_op jit(solution)/shard_map/ppermute | solution.py:33
  254.0 51.9 %collective-permute-start.20 = (bf16[512,2112]{0,1:T(8,128)(2,1)}, bf16[512,2112]{0,1:T(8,128)(2,1)}, u32[]{:S(2)}, u32[]{:S(2)}) collective-permute-start(bf16[512,2112]{0,1:T(8,128)(2,1)} %get-tuple-element.164), channel_id=1, source_target_pairs={{0,16},{16,0},{1,17},{17,1},{2,18},{18,2},{3,19},{19,3},{4,20},{20... | collective-permute-start | bytes 6488072 | tf_op jit(solution)/shard_map/ppermute | solution.py:33
  262.4 86.8 %collective-permute-start.23 = (bf16[2112,512]{1,0:T(8,128)(2,1)}, bf16[2112,512]{1,0:T(8,128)(2,1)}, u32[]{:S(2)}, u32[]{:S(2)}) collective-permute-start(bf16[2112,512]{1,0:T(8,128)(2,1)} %get-tuple-element.166), channel_id=1, source_target_pairs={{0,8},{8,0},{1,9},{9,1},{2,10},{10,2},{3,11},{11,3},{4,12},{12,4},... | collective-permute-start | bytes 6488072 | tf_op jit(solution)/shard_map/ppermute | solution.py:33
  262.9 92.1 %collective-permute-start.24 = (bf16[2112,512]{1,0:T(8,128)(2,1)}, bf16[2112,512]{1,0:T(8,128)(2,1)}, u32[]{:S(2)}, u32[]{:S(2)}) collective-permute-start(bf16[2112,512]{1,0:T(8,128)(2,1)} %get-tuple-element.166), channel_id=1, source_target_pairs={{0,16},{16,0},{1,17},{17,1},{2,18},{18,2},{3,19},{19,3},{4,20},{20... | collective-permute-start | bytes 6488072 | tf_op jit(solution)/shard_map/ppermute | solution.py:33
  272.1 123.3 %collective-permute-start.15 = (bf16[512,2112]{0,1:T(8,128)(2,1)}, bf16[512,2112]{0,1:T(8,128)(2,1)S(1)}, u32[]{:S(2)}, u32[]{:S(2)}) collective-permute-start(bf16[512,2112]{0,1:T(8,128)(2,1)} %get-tuple-element.162), channel_id=1, source_target_pairs={{0,8},{8,0},{1,9},{9,1},{2,10},{10,2},{3,11},{11,3},{4,12},{12,4},... | collective-permute-start | bytes 6488072 | tf_op jit(solution)/shard_map/ppermute | solution.py:33
  273.6 352.2 %reduce-scatter.9.cloned.1.call-start = ((), (), s32[]{:S(2)}) async-start(), calls=%async_computation.9 | async-start | bytes 4718592 | tf_op jit(solution)/shard_map/reduce_scatter | solution.py:372
  302.8 95.7 %collective-permute-start.16 = (bf16[512,2112]{0,1:T(8,128)(2,1)}, bf16[512,2112]{0,1:T(8,128)(2,1)S(1)}, u32[]{:S(2)}, u32[]{:S(2)}) collective-permute-start(bf16[512,2112]{0,1:T(8,128)(2,1)} %get-tuple-element.162), channel_id=1, source_target_pairs={{0,16},{16,0},{1,17},{17,1},{2,18},{18,2},{3,19},{19,3},{4,20},{20... | collective-permute-start | bytes 6488072 | tf_op jit(solution)/shard_map/ppermute | solution.py:33
  305.9 140.2 %collective-permute-start.21 = (bf16[256,2112]{0,1:T(8,128)(2,1)S(1)}, bf16[256,2112]{0,1:T(8,128)(2,1)S(1)}, u32[]{:S(2)}, u32[]{:S(2)}) collective-permute-start(bf16[256,2112]{0,1:T(8,128)(2,1)S(1)} %slice.588), channel_id=1, source_target_pairs={{0,16},{16,0},{1,17},{17,1},{2,18},{18,2},{3,19},{19,3},{4,20},{20... | collective-permute-start | bytes 3244040 | tf_op jit(solution)/shard_map/ppermute | solution.py:33
  349.2 98.1 %collective-permute-start.22 = (bf16[256,2112]{0,1:T(8,128)(2,1)S(1)}, bf16[256,2112]{0,1:T(8,128)(2,1)S(1)}, u32[]{:S(2)}, u32[]{:S(2)}) collective-permute-start(bf16[256,2112]{0,1:T(8,128)(2,1)S(1)} %slice.589), channel_id=1, source_target_pairs={{0,8},{8,0},{1,9},{9,1},{2,10},{10,2},{3,11},{11,3},{4,12},{12,4},... | collective-permute-start | bytes 3244040 | tf_op jit(solution)/shard_map/ppermute | solution.py:33
  355.1 88.1 %collective-permute-start.25 = (bf16[1056,512]{1,0:T(8,128)(2,1)S(1)}, bf16[1056,512]{1,0:T(8,128)(2,1)S(1)}, u32[]{:S(2)}, u32[]{:S(2)}) collective-permute-start(bf16[1056,512]{1,0:T(8,128)(2,1)S(1)} %slice.590), channel_id=1, source_target_pairs={{0,16},{16,0},{1,17},{17,1},{2,18},{18,2},{3,19},{19,3},{4,20},{20... | collective-permute-start | bytes 3244040 | tf_op jit(solution)/shard_map/ppermute | solution.py:33
  395.4 49.5 %collective-permute-start.26 = (bf16[1056,512]{1,0:T(8,128)(2,1)S(1)}, bf16[1056,512]{1,0:T(8,128)(2,1)S(1)}, u32[]{:S(2)}, u32[]{:S(2)}) collective-permute-start(bf16[1056,512]{1,0:T(8,128)(2,1)S(1)} %slice.591), channel_id=1, source_target_pairs={{0,8},{8,0},{1,9},{9,1},{2,10},{10,2},{3,11},{11,3},{4,12},{12,4},... | collective-permute-start | bytes 3244040 | tf_op jit(solution)/shard_map/ppermute | solution.py:33
  398.5 64.2 %collective-permute-start.17 = (bf16[256,2112]{0,1:T(8,128)(2,1)S(1)}, bf16[256,2112]{0,1:T(8,128)(2,1)S(1)}, u32[]{:S(2)}, u32[]{:S(2)}) collective-permute-start(bf16[256,2112]{0,1:T(8,128)(2,1)S(1)} %slice.586), channel_id=1, source_target_pairs={{0,16},{16,0},{1,17},{17,1},{2,18},{18,2},{3,19},{19,3},{4,20},{20... | collective-permute-start | bytes 3244040 | tf_op jit(solution)/shard_map/ppermute | solution.py:33
  574.4 101.3 %all-gather.9.cloned.1.call-start = ((), (), s32[]{:S(2)}) async-start(), calls=%async_computation.10 | async-start | bytes 4718592 | tf_op jit(solution)/shard_map/all_gather | solution.py:401
  630.2 450.6 %reduce-scatter.11.cloned.1.call-start = ((), (), s32[]{:S(2)}) async-start(), calls=%async_computation.11 | async-start | bytes 4718592 | tf_op jit(solution)/shard_map/reduce_scatter | solution.py:429
  740.5 341.8 %reduce-scatter.7.cloned.1.call-start = ((), (), s32[]{:S(2)}) async-start(), calls=%async_computation.8 | async-start | bytes 4718592 | tf_op jit(solution)/shard_map/reduce_scatter | solution.py:391
  750.9 65.8 %collective-permute-start.46 = (bf16[256,2112]{0,1:T(8,128)(2,1)}, bf16[256,2112]{0,1:T(8,128)(2,1)}, u32[]{:S(2)}, u32[]{:S(2)}) collective-permute-start(bf16[256,2112]{0,1:T(8,128)(2,1)} %get-tuple-element.160), channel_id=1, source_target_pairs={{0,8},{8,0},{1,9},{9,1},{2,10},{10,2},{3,11},{11,3},{4,12},{12,4},... | collective-permute-start | bytes 3244040 | tf_op jit(solution)/shard_map/ppermute | solution.py:33
  750.9 68.3 %collective-permute-start.50 = (bf16[256,2112]{0,1:T(8,128)(2,1)S(1)}, bf16[256,2112]{0,1:T(8,128)(2,1)}, u32[]{:S(2)}, u32[]{:S(2)}) collective-permute-start(bf16[256,2112]{0,1:T(8,128)(2,1)S(1)} %get-tuple-element.161), channel_id=1, source_target_pairs={{0,16},{16,0},{1,17},{17,1},{2,18},{18,2},{3,19},{19,3},{4,20},{20... | collective-permute-start | bytes 3244040 | tf_op jit(solution)/shard_map/ppermute | solution.py:33
  756.4 95.3 %collective-permute-start.61 = (bf16[1056,512]{1,0:T(8,128)(2,1)}, bf16[1056,512]{1,0:T(8,128)(2,1)}, u32[]{:S(2)}, u32[]{:S(2)}) collective-permute-start(bf16[1056,512]{1,0:T(8,128)(2,1)} %get-tuple-element.156), channel_id=1, source_target_pairs={{0,8},{8,0},{1,9},{9,1},{2,10},{10,2},{3,11},{11,3},{4,12},{12,4},... | collective-permute-start | bytes 3244040 | tf_op jit(solution)/shard_map/ppermute | solution.py:33
  758.5 88.8 %collective-permute-start.59 = (bf16[1056,512]{1,0:T(8,128)(2,1)}, bf16[1056,512]{1,0:T(8,128)(2,1)}, u32[]{:S(2)}, u32[]{:S(2)}) collective-permute-start(bf16[1056,512]{1,0:T(8,128)(2,1)} %get-tuple-element.157), channel_id=1, source_target_pairs={{0,16},{16,0},{1,17},{17,1},{2,18},{18,2},{3,19},{19,3},{4,20},{20... | collective-permute-start | bytes 3244040 | tf_op jit(solution)/shard_map/ppermute | solution.py:33
  763.0 59.9 %collective-permute-start.52 = (bf16[256,2112]{0,1:T(8,128)(2,1)}, bf16[256,2112]{0,1:T(8,128)(2,1)}, u32[]{:S(2)}, u32[]{:S(2)}) collective-permute-start(bf16[256,2112]{0,1:T(8,128)(2,1)} %get-tuple-element.158), channel_id=1, source_target_pairs={{0,8},{8,0},{1,9},{9,1},{2,10},{10,2},{3,11},{11,3},{4,12},{12,4},... | collective-permute-start | bytes 3244040 | tf_op jit(solution)/shard_map/ppermute | solution.py:33
  851.8 61.4 %collective-permute-start.55 = (bf16[256,2112]{0,1:T(8,128)(2,1)S(1)}, bf16[256,2112]{0,1:T(8,128)(2,1)S(1)}, u32[]{:S(2)}, u32[]{:S(2)}) collective-permute-start(bf16[256,2112]{0,1:T(8,128)(2,1)S(1)} %copy-done.44), channel_id=1, source_target_pairs={{0,16},{16,0},{1,17},{17,1},{2,18},{18,2},{3,19},{19,3},{4,20},{20... | collective-permute-start | bytes 3244040 | tf_op jit(solution)/shard_map/ppermute | solution.py:33
  868.1 68.3 %collective-permute-start.53 = (bf16[256,2112]{0,1:T(8,128)(2,1)}, bf16[256,2112]{0,1:T(8,128)(2,1)S(1)}, u32[]{:S(2)}, u32[]{:S(2)}) collective-permute-start(bf16[256,2112]{0,1:T(8,128)(2,1)} %fusion.18), channel_id=1, source_target_pairs={{0,16},{16,0},{1,17},{17,1},{2,18},{18,2},{3,19},{19,3},{4,20},{20... | collective-permute-start | bytes 3244040 | tf_op jit(solution)/shard_map/ppermute | solution.py:33
  893.8 50.4 %collective-permute-start.63 = (bf16[1056,512]{1,0:T(8,128)(2,1)}, bf16[1056,512]{1,0:T(8,128)(2,1)S(1)}, u32[]{:S(2)}, u32[]{:S(2)}) collective-permute-start(bf16[1056,512]{1,0:T(8,128)(2,1)} %slice.830), channel_id=1, source_target_pairs={{0,8},{8,0},{1,9},{9,1},{2,10},{10,2},{3,11},{11,3},{4,12},{12,4},... | collective-permute-start | bytes 3244040 | tf_op jit(solution)/shard_map/ppermute | solution.py:33
  914.0 49.4 %collective-permute-start.60 = (bf16[1056,512]{1,0:T(8,128)(2,1)}, bf16[1056,512]{1,0:T(8,128)(2,1)S(1)}, u32[]{:S(2)}, u32[]{:S(2)}) collective-permute-start(bf16[1056,512]{1,0:T(8,128)(2,1)} %fusion.14), channel_id=1, source_target_pairs={{0,8},{8,0},{1,9},{9,1},{2,10},{10,2},{3,11},{11,3},{4,12},{12,4},... | collective-permute-start | bytes 3244040 | tf_op jit(solution)/shard_map/ppermute | solution.py:33
  1000.4 52.5 %collective-permute-start.37 = (bf16[32,2048]{1,0:T(8,128)(2,1)S(1)}, bf16[32,2048]{1,0:T(8,128)(2,1)S(1)}, u32[]{:S(2)}, u32[]{:S(2)}) collective-permute-start(bf16[32,2048]{1,0:T(8,128)(2,1)S(1)} %get-tuple-element.175), channel_id=1, source_target_pairs={{0,8},{8,0},{1,9},{9,1},{2,10},{10,2},{3,11},{11,3},{4,12},{12,4},... | collective-permute-start | bytes 393224 | tf_op jit(solution)/shard_map/ppermute | solution.py:33
  (130 other events, 2591.6 us)
Sparse Core Ops, SparseCore 0:
  11.9 65.4 all-gather.10
  191.5 48.8 reduce-scatter.4
  243.9 45.3 all-gather.6
  290.7 45.8 all-gather.12
  574.5 51.2 reduce-scatter.8
  630.3 45.2 all-gather.8
  740.6 47.7 reduce-scatter.10
  795.4 48.6 reduce-scatter.6
where the time goes:
time: 1100 us; the launch traced here: 1090 us
  waiting for transfers between devices  568 us (52%)
  matrix products  185 us (17%)
  local copies, waits for them, and re-layouts  137 us (12%)
  other arithmetic  105 us (10%)
  starting transfers between devices  80.8 us (7%)
  between operations  16.5 us (2%)
    ppermute x50, waiting for transfers between devices, shift(): return lax.ppermute(x, axis, [(i, (i + step) % n) for i in range(n)])  320 us
    dot_general x6, matrix products, right_dot(): lax.dot_general(left_mat, right_mat, (((1,), (1,)), ((), ())), preferred_...  68.5 us
    ppermute x50, starting transfers between devices, shift(): return lax.ppermute(x, axis, [(i, (i + step) % n) for i in range(n)])  55.9 us
    dot_general x7, matrix products, mat_dot(): return jnp.dot(left_mat, right_mat, preferred_element_type=F32)  55.6 us
    reduce_scatter x1, waiting for transfers between devices, body(): lax.psum_scatter(grad_rows.astype(BF16), 'expert', scatter_dimension=0, t...  51.3 us
    dot_general x18, matrix products, left_dot(): lax.dot_general(left_mat, right_mat, (((0,), (0,)), ((), ())), preferred_...  51.2 us
    reduce_scatter x1, waiting for transfers between devices, body(): lax.psum_scatter(mat_dot(mixed, w_o).astype(BF16), 'expert', scatter_dime...  48.9 us
    all_gather x1, waiting for transfers between devices, body(): lax.all_gather(grad_residual.astype(BF16), 'expert', axis=0, tiled=True)  45.4 us
  transfers between devices with their start and end apart: 74, of which 34 were waited for; matrix products, arithmetic and copies ran while one was open for 23% of the time, Pallas kernels for 0%

commit v1 on v0

v1 whole, which is shorter than its diff:
```python
import functools

import jax
import jax.numpy as jnp
from jax import lax
from jax.experimental import pallas as pl
from jax.experimental.pallas import tpu as pltpu
from jax.sharding import PartitionSpec as P

HD = 128

EPSILON = 1e-06
ROPE_BASE = 1000000.0
NEGATIVE = -1e30
F32 = jnp.float32
BF16 = jnp.bfloat16


def mat_dot(left_mat, right_mat):
    return jnp.dot(left_mat, right_mat, preferred_element_type=F32)


def left_dot(left_mat, right_mat):
    return lax.dot_general(
        left_mat, right_mat, (((0,), (0,)), ((), ())), preferred_element_type=F32
    )


def right_dot(left_mat, right_mat):
    return lax.dot_general(
        left_mat, right_mat, (((1,), (1,)), ((), ())), preferred_element_type=F32
    )


def shift(x, axis, step):
    n = lax.axis_size(axis)
    return lax.ppermute(x, axis, [(i, (i + step) % n) for i in range(n)])


def tie(value, others):
    return lax.optimization_barrier((value, others))


def plane_blocks():
    return (
        lax.axis_size("dp"),
        lax.axis_size("context"),
        lax.axis_index("dp"),
        lax.axis_index("context"),
    )


class Gather:
    def __init__(self, *own):
        self.own = list(own)
        self.half = own[0].shape[0] * len(own) // 2
        self.across, self.along = [{} for _ in own], [{} for _ in own]

    def send_across(self, h):
        nc = lax.axis_size("context")
        self.across[h] = {s: shift(self.own[h], "context", s) for s in range(1, nc)}

    def send_along(self, h):
        ndp = lax.axis_size("dp")
        self.along[h] = {d: shift(self.own[h], "dp", d) for d in range(1, ndp)}

    def send_far_along(self):
        ndp = lax.axis_size("dp")
        self.far_top = {
            (d, s): shift(x[: self.half], "dp", d)
            for s, x in self.across[0].items()
            for d in range(1, ndp)
        }

    def send_far_across(self):
        nc = lax.axis_size("context")
        self.far_bottom = {
            (d, s): shift(x[-self.half :], "context", s)
            for d, x in self.along[-1].items()
            for s in range(1, nc)
        }

    def direct(self):
        for h in range(len(self.own)):
            self.send_across(h)
            self.send_along(h)

    def far(self):
        self.send_far_along()
        self.send_far_across()


class Pieces:
    def __init__(self, gather):
        ndp, nc, dp, ctx = plane_blocks()
        found = []
        for h in range(len(gather.own)):
            found.append((0, 0, h, gather.own[h]))
            found += [(0, s, h, x) for s, x in gather.across[h].items()]
            found += [(d, 0, h, x) for d, x in gather.along[h].items()]
        found += [(*k, 0, x) for k, x in gather.far_top.items()]
        found += [(*k, 1, x) for k, x in gather.far_bottom.items()]
        self.half, self.columns = gather.half, gather.own[0].shape[1]
        self.arrays, self.counts, self.keys, self.found, places = [], [], [], {}, []
        for d, s, h, x in found:
            plane = lax.rem(dp - d + ndp, ndp) * nc + lax.rem(ctx - s + nc, nc)
            n = x.shape[0] // self.half
            self.arrays.append(x)
            self.counts.append(n)
            for i in range(n):
                self.keys.append((d, s, h + i))
                self.found[d, s, h + i] = (len(self.arrays) - 1, i * self.half)
                places.append(2 * plane + h + i)
        self.places = jnp.stack(places).astype(jnp.int32)


class Scatter:
    def __init__(self, halves_of):
        self.halves_of = halves_of

    def terms(self, keys, dtype):
        ndp, nc, dp, ctx = plane_blocks()
        numbers = [
            2 * (lax.rem(dp + d, ndp) * nc + lax.rem(ctx + s, nc)) + h for d, s, h in keys
        ]
        return dict(zip(keys, self.halves_of(numbers, dtype)))

    def far(self):
        ndp, nc, _, _ = plane_blocks()
        pairs = [(d, s) for d in range(1, ndp) for s in range(1, nc)]
        terms = self.terms([(*k, h) for k in pairs for h in range(2)], BF16)
        return (
            {k: shift(terms[*k, 0], "context", k[1]) for k in pairs},
            {k: shift(terms[*k, 1], "dp", k[0]) for k in pairs},
        )

    def free(self):
        ndp, nc, _, _ = plane_blocks()
        keys = [(0, s, 0) for s in range(1, nc)] + [(d, 0, 1) for d in range(1, ndp)]
        terms = self.terms(keys, BF16)
        return (
            [shift(terms[0, s, 0], "context", s) for s in range(1, nc)],
            [shift(terms[d, 0, 1], "dp", d) for d in range(1, ndp)],
        )

    def last(self, far):
        ndp, nc, _, _ = plane_blocks()
        keys = [(d, 0, 0) for d in range(1, ndp)] + [(0, s, 1) for s in range(1, nc)]
        terms = self.terms(keys + [(0, 0, 0), (0, 0, 1)], F32)
        self.own = [terms[0, 0, h] for h in range(2)]
        along, across = [], []
        for d in range(1, ndp):
            total = terms[d, 0, 0]
            for s in range(1, nc):
                total = total + far[0][d, s].astype(F32)
            along.append(shift(total.astype(BF16), "dp", d))
        for s in range(1, nc):
            total = terms[0, s, 1]
            for d in range(1, ndp):
                total = total + far[1][d, s].astype(F32)
            across.append(shift(total.astype(BF16), "context", s))
        return along, across

    def finish(self, free, last):
        out = []
        for h, pieces in enumerate((free[0] + last[0], free[1] + last[1])):
            total = self.own[h]
            for piece in pieces:
                total = total + piece.astype(F32)
            out.append(total)
        return jnp.concatenate(out, 0)


def doubling_steps(axis):
    n = lax.axis_size(axis)
    step = 1
    while step < n:
        yield step, [(i, i ^ step) for i in range(n)]
        step *= 2


def small_gather(x, axes):
    for axis in axes:
        place = lax.axis_index(axis)
        for step, pairs in doubling_steps(axis):
            other = lax.ppermute(x, axis, pairs)
            high = (place & step) != 0
            x = jnp.concatenate([jnp.where(high, other, x), jnp.where(high, x, other)], 0)
    return x


def small_scatter(x):
    for axis in ("dp", "context", "expert"):
        place = lax.axis_index(axis)
        for step, pairs in reversed(list(doubling_steps(axis))):
            half = x.shape[0] // 2
            high = (place & step) != 0
            low_part, high_part = x[:half], x[half:]
            other = lax.ppermute(jnp.where(high, low_part, high_part), axis, pairs)
            x = jnp.where(high, high_part, low_part) + other
    return x[0]


def core_exchange(x, group):
    count = lax.axis_size("expert")
    place = lax.rem(lax.axis_index("expert"), group)
    out = x
    for s in range(1, group):
        piece = lax.dynamic_slice_in_dim(x, lax.rem(place + s, group), 1)
        pairs = [(i, i // group * group + (i % group + s) % group) for i in range(count)]
        got = lax.ppermute(piece, "expert", pairs)
        out = lax.dynamic_update_slice_in_dim(out, got, lax.rem(place - s + group, group), 0)
    return out


LANES = 128
MIB = 1 << 20


def params(mib):
    return pltpu.CompilerParams(
        dimension_semantics=("arbitrary",), vmem_limit_bytes=mib * MIB
    )


def cost(flops, nbytes):
    return pl.CostEstimate(flops=flops, bytes_accessed=nbytes, transcendentals=0)


def assemble(places, full, refs, counts, half):
    i = 0
    for ref, n in zip(refs, counts):
        for k in range(n):
            start = pl.multiple_of(places[i] * half, half)
            full[pl.ds(start, half), :] = ref[k * half : (k + 1) * half, :]
            i += 1


def weight_grad_kernel(n, half, numbers, *refs):
    acts, grads, outs, turned = refs[:n], refs[n], refs[n + 1 : -1], refs[-1]

    @pl.when(pl.program_id(0) == 0)
    def _():
        for k in range(n):
            turned[k * half : (k + 1) * half, :] = acts[k][...].T

    total = mat_dot(turned[...], grads[...])
    for k in range(n):
        outs[k][...] = total[k * half : (k + 1) * half].astype(outs[k].dtype)


def weight_grad(acts, grads, numbers, half, dtype):
    m, columns = grads.shape
    n = len(numbers)
    tile = tile_of(m)

    def block(k):
        return pl.BlockSpec((m, half), lambda j, p: (0, p[k]))

    return pl.pallas_call(
        functools.partial(weight_grad_kernel, n, half),
        out_shape=[jax.ShapeDtypeStruct((half, columns), dtype)] * n,
        grid_spec=pltpu.PrefetchScalarGridSpec(
            num_scalar_prefetch=1,
            grid=(pl.cdiv(columns, tile),),
            in_specs=[block(k) for k in range(n)]
            + [pl.BlockSpec((m, tile), lambda j, p: (0, j))],
            out_specs=[pl.BlockSpec((half, tile), lambda j, p: (0, j))] * n,
            scratch_shapes=[pltpu.VMEM((n * half, m), BF16)],
        ),
        compiler_params=params(48),
        cost_estimate=cost(2 * m * n * half * columns, 12 * MIB),
        name="weight_grad",
    )(jnp.stack(numbers).astype(jnp.int32), *[acts] * n, grads)


def chunk(m):
    return min(m, 512)


def tile_of(m):
    return 768 if m <= 1024 else 256


def hidden_grad_kernel(counts, half, places, acts, *refs):
    out, full = refs[-2], refs[-1]
    assemble(places, full, refs[:-2], counts, half)
    step = chunk(acts.shape[0])

    @pl.loop(0, acts.shape[0] // step)
    def _(c):
        rows = pl.ds(pl.multiple_of(c * step, step), step)
        out[rows, :] = mat_dot(acts[rows, :], full[...])


def hidden_grad(acts, pieces):
    m, width = acts.shape
    tile_size = tile_of(m)
    tiles = pl.cdiv(pieces.columns, tile_size)
    return pl.pallas_call(
        functools.partial(hidden_grad_kernel, pieces.counts, pieces.half),
        out_shape=jax.ShapeDtypeStruct((m, pieces.columns), F32),
        grid_spec=pltpu.PrefetchScalarGridSpec(
            num_scalar_prefetch=1,
            grid=(tiles,),
            in_specs=[pl.BlockSpec((m, width), lambda j, p: (0, 0))]
            + [pl.BlockSpec((a.shape[0], tile_size), lambda j, p: (0, j)) for a in pieces.arrays],
            out_specs=pl.BlockSpec((m, tile_size), lambda j, p: (0, j)),
            scratch_shapes=[pltpu.VMEM((width, tile_size), BF16)],
        ),
        compiler_params=params(44),
        cost_estimate=cost(2 * m * width * pieces.columns, 20 * MIB),
        name="hidden_grad",
    )(pieces.places, acts, *pieces.arrays)


def fold(x):
    total = x[:, :LANES]
    for i in range(1, x.shape[1] // LANES):
        total = total + x[:, i * LANES : (i + 1) * LANES]
    return total


def ffn_kernel(g_counts, u_counts, half, tile, fe, count, columns, *refs):
    g_places, u_places, here, acts, router, kept, gh = refs[:7]
    refs, n = refs[7:], len(g_counts)
    gates, refs = refs[:n], refs[n:]
    ups, refs = refs[: len(u_counts)], refs[len(u_counts) :]
    scaled, gate_out, up_out, small = refs[:4]
    prob, share, switch, sum_e, sum_s, gate_full, up_full = refs[4:]
    step = chunk(acts.shape[0])
    j = pl.program_id(0)
    chunks = acts.shape[0] // step
    lane = lax.broadcasted_iota(jnp.int32, (1, LANES), 1)

    def rows_of(c):
        return pl.ds(pl.multiple_of(c * step, step), step)

    @pl.when(j == 0)
    def _():
        @pl.loop(0, chunks)
        def _(c):
            rows = rows_of(c)
            logits = mat_dot(acts[rows, :], router[...])
            sig = jax.nn.sigmoid(logits)
            masked = jnp.where(lane < count, logits, NEGATIVE)
            expo = jnp.exp(masked - jnp.max(masked, -1, keepdims=True))
            expo = jnp.where(lane < count, expo, 0.0)
            probs = expo / jnp.sum(expo, -1, keepdims=True)
            prob[rows, :] = probs
            own = jnp.sum(jnp.where(lane == here[0], probs, 0.0), -1, keepdims=True)
            share[rows, :] = own * kept[rows, :]
            switch[rows, :] = jnp.sum(jnp.where(lane == count, sig, 0.0), -1, keepdims=True)
            sum_e[rows, :] = jnp.zeros((step, LANES), F32)
            sum_s[rows, :] = jnp.zeros((step, LANES), F32)

    column = j * tile + lax.broadcasted_iota(jnp.int32, (1, tile), 1)
    routed = column < fe
    shared = (column >= fe) & (column < columns)
    assemble(g_places, gate_full, gates, g_counts, half)
    assemble(u_places, up_full, ups, u_counts, half)

    @pl.loop(0, chunks)
    def _(c):
        rows = rows_of(c)
        gate = mat_dot(acts[rows, :], gate_full[...])
        up = mat_dot(acts[rows, :], up_full[...])
        scale = jnp.where(routed, share[rows, :], switch[rows, :])
        sig = jax.nn.sigmoid(gate)
        silu = gate * sig
        hidden = silu * up
        grad = gh[rows, :]
        product = grad * hidden
        sum_e[rows, :] += fold(jnp.where(routed, product, 0.0))
        sum_s[rows, :] += fold(jnp.where(shared, product, 0.0))
        grad = grad * scale
        scaled[rows, :] = (scale * hidden).astype(BF16)
        gate_out[rows, :] = (grad * up * (sig + silu * (1.0 - sig))).astype(BF16)
        up_out[rows, :] = (grad * silu).astype(BF16)

    @pl.when(j == pl.num_programs(0) - 1)
    def _():
        @pl.loop(0, chunks)
        def _(c):
            rows = rows_of(c)
            grad_share = jnp.sum(sum_e[rows, :], -1, keepdims=True)
            grad_switch = jnp.sum(sum_s[rows, :], -1, keepdims=True)
            hot = (lane == here[0]).astype(F32)
            logit = grad_share * share[rows, :] * (hot - prob[rows, :])
            sw = switch[rows, :]
            pre = grad_switch * sw * (1.0 - sw)
            value = jnp.where(lane < count, logit, jnp.where(lane == count, pre, 0.0))
            small[rows, :] = value.astype(BF16)


def ffn(acts, router, kept, gh, here, gates, ups, fe, count):
    m, width = acts.shape
    columns = gates.columns
    tile_size = tile_of(m)
    tiles = pl.cdiv(columns, tile_size)
    whole = lambda j, g, u, h: (0, 0)
    tile = pl.BlockSpec((m, tile_size), lambda j, g, u, h: (0, j))
    weights = [
        pl.BlockSpec((a.shape[0], tile_size), lambda j, g, u, h: (0, j))
        for a in gates.arrays + ups.arrays
    ]
    hid = jax.ShapeDtypeStruct((m, columns), BF16)
    return pl.pallas_call(
        functools.partial(
            ffn_kernel, gates.counts, ups.counts, gates.half, tile_size, fe, count, columns
        ),
        out_shape=(hid, hid, hid, jax.ShapeDtypeStruct((m, LANES), BF16)),
        grid_spec=pltpu.PrefetchScalarGridSpec(
            num_scalar_prefetch=3,
            grid=(tiles,),
            in_specs=[
                pl.BlockSpec((m, width), whole),
                pl.BlockSpec((width, LANES), whole),
                pl.BlockSpec((m, 1), whole),
                tile,
            ]
            + weights,
            out_specs=[tile, tile, tile, pl.BlockSpec((m, LANES), whole)],
            scratch_shapes=[
                pltpu.VMEM((m, LANES), F32),
                pltpu.VMEM((m, 1), F32),
                pltpu.VMEM((m, 1), F32),
                pltpu.VMEM((m, LANES), F32),
                pltpu.VMEM((m, LANES), F32),
                pltpu.VMEM((width, tile_size), BF16),
                pltpu.VMEM((width, tile_size), BF16),
            ],
        ),
        compiler_params=params(52),
        cost_estimate=cost(4 * m * width * columns, 40 * MIB),
        name="ffn",
    )(gates.places, ups.places, here, acts, router, kept, gh, *gates.arrays, *ups.arrays)


def spread_kernel(arrays, half, extra, *refs):
    pairs = len(arrays)
    places, refs = refs[0], refs[1:]
    i = pl.program_id(0)
    acts, refs = refs[:pairs], refs[pairs:]
    weights = []
    for found in arrays:
        n = max(array for array, _ in found) + 1
        weights.append(refs[:n])
        refs = refs[n:]
    out, held = refs[-1 - pairs], refs[-pairs:]
    step = min(out.shape[0], 1024)
    for k in range(len(arrays[0])):

        @pl.when(i == k)
        def _(k=k):
            for pair in range(pairs):
                array, row = arrays[pair][k]
                held[pair][...] = weights[pair][array][row : row + half, :]

    @pl.loop(0, out.shape[0] // step)
    def _(c):
        rows = pl.ds(pl.multiple_of(c * step, step), step)
        total = right_dot(acts[0][rows, :], held[0][...])
        for pair in range(1, pairs):
            total += right_dot(acts[pair][rows, :], held[pair][...])
        if extra:
            total += right_dot(refs[0][rows, :], refs[1][...])
        out[rows, :] = total.astype(BF16)


def spread(pairs, extra=None):
    acts = [a for a, _ in pairs]
    first = pairs[0][1]
    half, steps = first.half, sum(first.counts)
    m = acts[0].shape[0]
    width = steps * half
    whole = lambda i, p: (0, 0)
    specs = [pl.BlockSpec(a.shape, whole) for a in acts]
    operands, arrays = list(acts), []
    for _, pieces in pairs:
        specs += [pl.BlockSpec(a.shape, whole) for a in pieces.arrays]
        operands += pieces.arrays
        arrays.append(tuple(pieces.found[k] for k in first.keys))
    if extra is not None:
        specs.append(pl.BlockSpec(extra[0].shape, whole))
        specs.append(pl.BlockSpec((half, LANES), lambda i, p: (p[i], 0)))
        operands += list(extra)
    return pl.pallas_call(
        functools.partial(spread_kernel, tuple(arrays), half, extra is not None),
        out_shape=jax.ShapeDtypeStruct((m, width), BF16),
        grid_spec=pltpu.PrefetchScalarGridSpec(
            num_scalar_prefetch=1,
            grid=(steps,),
            in_specs=specs,
            out_specs=pl.BlockSpec((m, half), lambda i, p: (0, p[i])),
            scratch_shapes=[pltpu.VMEM((half, first.columns), BF16)] * len(pairs),
        ),
        compiler_params=params(60),
        cost_estimate=cost(2 * m * width * first.columns * len(pairs), 20 * MIB),
        name="spread",
    )(first.places, *operands)


def turn(x):
    return pltpu.roll(x, HD // 2, 1)


def qkv_kernel(counts, half, wide, places, tok, gain, bias, cosine, sine, *refs):
    normed, query, key_value, inverse, full = refs[-5:]

    @pl.when(pl.program_id(0) == 0)
    def _():
        assemble(places, full, refs[:-5], counts, half)

    values = tok[...].astype(F32)
    inv = lax.rsqrt(jnp.mean(values * values, -1, keepdims=True) + EPSILON)
    inverse[...] = inv
    normed[...] = (values * inv * gain[...]).astype(BF16)
    out = mat_dot(normed[...], full[...]) + bias[...]
    for h in range(2 * wide // HD):
        head = out[:, h * HD : (h + 1) * HD]
        head = (head * cosine[...] + turn(head) * sine[...]).astype(BF16)
        if h < wide // HD:
            query[:, h * HD : (h + 1) * HD] = head
        else:
            key_value[:, h * HD - wide : (h + 1) * HD - wide] = head
    key_value[:, wide:] = out[:, 2 * wide :].astype(BF16)


def qkv_project(tok, gain, bias, cosine, sine, pieces, wide):
    m, width = tok.shape
    step = 256
    row = lambda i, p: (i, 0)
    whole = lambda i, p: (0, 0)
    return pl.pallas_call(
        functools.partial(qkv_kernel, pieces.counts, pieces.half, wide),
        out_shape=(
            jax.ShapeDtypeStruct((m, width), BF16),
            jax.ShapeDtypeStruct((m, wide), BF16),
            jax.ShapeDtypeStruct((m, 2 * wide), BF16),
            jax.ShapeDtypeStruct((m, 1), F32),
        ),
        grid_spec=pltpu.PrefetchScalarGridSpec(
            num_scalar_prefetch=1,
            grid=(m // step,),
            in_specs=[
                pl.BlockSpec((step, width), row),
                pl.BlockSpec((1, width), whole),
                pl.BlockSpec((1, 3 * wide), whole),
                pl.BlockSpec((step, HD), row),
                pl.BlockSpec((step, HD), row),
            ]
            + [pl.BlockSpec(a.shape, whole) for a in pieces.arrays],
            out_specs=[
                pl.BlockSpec((step, width), row),
                pl.BlockSpec((step, wide), row),
                pl.BlockSpec((step, 2 * wide), row),
                pl.BlockSpec((step, 1), row),
            ],
            scratch_shapes=[pltpu.VMEM((width, 3 * wide), BF16)],
        ),
        compiler_params=params(32),
        cost_estimate=cost(6 * m * width * wide, 12 * MIB),
        name="qkv_project",
    )(pieces.places, tok, gain, bias, cosine, sine, *pieces.arrays)


def head_probs(query, kvs, allowed, h):
    own = slice(h * HD, (h + 1) * HD)
    scores = jnp.concatenate([right_dot(query[:, own], kv[:, own]) for kv in kvs], -1)
    scores = jnp.where(allowed, scores * HD ** (-0.5), NEGATIVE)
    expo = jnp.exp(scores - jnp.max(scores, -1, keepdims=True))
    return expo / jnp.sum(expo, -1, keepdims=True)


def attend_kernel(nc, wide, query, allowed, w_o, *refs):
    kvs, mixed, out = refs[:nc], refs[nc], refs[nc + 1]
    tok = query.shape[0]
    for h in range(wide // HD):
        value = slice(wide + h * HD, wide + (h + 1) * HD)
        prob = head_probs(query, kvs, allowed[0] > 0.0, h).astype(BF16)
        total = mat_dot(prob[:, :tok], kvs[0][:, value])
        for s in range(1, nc):
            total += mat_dot(prob[:, s * tok : (s + 1) * tok], kvs[s][:, value])
        mixed[:, h * HD : (h + 1) * HD] = total.astype(BF16)
    out[...] = mat_dot(mixed[...], w_o[...]).astype(BF16)


def attend(query, kvs, allowed, w_o):
    m, wide = query.shape
    groups, tok, keys = allowed.shape
    width = w_o.shape[1]
    row = lambda g: (g, 0)
    return pl.pallas_call(
        functools.partial(attend_kernel, len(kvs), wide),
        out_shape=(
            jax.ShapeDtypeStruct((m, wide), BF16),
            jax.ShapeDtypeStruct((m, width), BF16),
        ),
        grid=(groups,),
        in_specs=[
            pl.BlockSpec((tok, wide), row),
            pl.BlockSpec((1, tok, keys), lambda g: (g, 0, 0)),
            pl.BlockSpec((wide, width), lambda g: (0, 0)),
        ]
        + [pl.BlockSpec((tok, 2 * wide), row)] * len(kvs),
        out_specs=[pl.BlockSpec((tok, wide), row), pl.BlockSpec((tok, width), row)],
        compiler_params=params(32),
        cost_estimate=cost(2 * m * width * wide + 4 * m * keys * wide, 8 * MIB),
        name="attend",
    )(query, allowed, w_o, *kvs)


def attend_back_kernel(nc, wide, query, allowed, w_o, grads, cosine, sine, *refs):
    kvs, grad_query, grad_own, grad_far = refs[:nc], refs[nc], refs[nc + 1], refs[nc + 2 :]
    tok = query.shape[0]
    grad_mixed = right_dot(grads[...], w_o[...]).astype(BF16)
    scale = HD ** (-0.5)
    for h in range(wide // HD):
        key = slice(h * HD, (h + 1) * HD)
        value = slice(wide + h * HD, wide + (h + 1) * HD)
        prob = head_probs(query, kvs, allowed[0] > 0.0, h)
        low = prob.astype(BF16)
        mixed = grad_mixed[:, key]
        grad = jnp.concatenate([right_dot(mixed, kv[:, value]) for kv in kvs], -1)
        inner = jnp.sum(grad * prob, -1, keepdims=True)
        grad = (prob * (grad - inner)).astype(BF16)
        total = None
        for s in range(nc):
            block = slice(s * tok, (s + 1) * tok)
            term = mat_dot(grad[:, block], kvs[s][:, key])
            total = term if total is None else total + term
            grad_key = left_dot(grad[:, block], query[:, key]) * scale
            grad_value = left_dot(low[:, block], mixed)
            if s == 0:
                grad_own[:, key] = grad_key
                grad_own[:, value] = grad_value
            else:
                grad_far[s - 1][:, key] = grad_key.astype(BF16)
                grad_far[s - 1][:, value] = grad_value.astype(BF16)
        total = total * scale
        total = total * cosine[...] - turn(total) * sine[...]
        grad_query[:, key] = total.astype(BF16)


def attend_back(query, kvs, allowed, w_o, grads, cosine, sine):
    m, wide = query.shape
    groups, tok, keys = allowed.shape
    width = w_o.shape[1]
    nc = len(kvs)
    row = lambda g: (g, 0)
    both = pl.BlockSpec((tok, 2 * wide), row)
    return pl.pallas_call(
        functools.partial(attend_back_kernel, nc, wide),
        out_shape=(
            jax.ShapeDtypeStruct((m, wide), BF16),
            jax.ShapeDtypeStruct((m, 2 * wide), F32),
            *[jax.ShapeDtypeStruct((m, 2 * wide), BF16)] * (nc - 1),
        ),
        grid=(groups,),
        in_specs=[
            pl.BlockSpec((tok, wide), row),
            pl.BlockSpec((1, tok, keys), lambda g: (g, 0, 0)),
            pl.BlockSpec((wide, width), lambda g: (0, 0)),
            pl.BlockSpec((tok, width), row),
            pl.BlockSpec((tok, HD), row),
            pl.BlockSpec((tok, HD), row),
        ]
        + [both] * nc,
        out_specs=[pl.BlockSpec((tok, wide), row)] + [both] * nc,
        compiler_params=params(32),
        cost_estimate=cost(2 * m * width * wide + 12 * m * keys * wide, 8 * MIB),
        name="attend_back",
    )(query, allowed, w_o, grads, cosine, sine, *kvs)


def join_kernel(wide, grad_query, grad_own, cosine, sine, *refs):
    far, out, sums = refs[:-2], refs[-2], refs[-1]
    total = grad_own[...]
    for ref in far:
        total = total + ref[...].astype(F32)
    out[:, :wide] = grad_query[...]
    for h in range(wide // HD):
        head = total[:, h * HD : (h + 1) * HD]
        head = head * cosine[...] - turn(head) * sine[...]
        out[:, wide + h * HD : wide + (h + 1) * HD] = head.astype(BF16)
    out[:, 2 * wide :] = total[:, wide:].astype(BF16)

    @pl.when(pl.program_id(0) == 0)
    def _():
        sums[...] = jnp.zeros_like(sums)

    sums[...] += jnp.sum(out[...].astype(F32), 0, keepdims=True)


def join(grad_query, grad_own, far, cosine, sine):
    m, wide = grad_query.shape
    step = 256
    row = lambda i: (i, 0)
    both = pl.BlockSpec((step, 2 * wide), row)
    return pl.pallas_call(
        functools.partial(join_kernel, wide),
        out_shape=(
            jax.ShapeDtypeStruct((m, 3 * wide), BF16),
            jax.ShapeDtypeStruct((1, 3 * wide), F32),
        ),
        grid=(m // step,),
        in_specs=[
            pl.BlockSpec((step, wide), row),
            both,
            pl.BlockSpec((step, HD), row),
            pl.BlockSpec((step, HD), row),
        ]
        + [both] * len(far),
        out_specs=[
            pl.BlockSpec((step, 3 * wide), row),
            pl.BlockSpec((1, 3 * wide), lambda i: (0, 0)),
        ],
        compiler_params=params(32),
        cost_estimate=cost(20 * m * wide, 6 * MIB),
        name="join",
    )(grad_query, grad_own, cosine, sine, *far)


def rms_unit(values):
    scaling = lax.rsqrt(jnp.mean(values * values, -1, keepdims=True) + EPSILON)
    return values * scaling, scaling


def body(
    tokens,
    cotangent,
    deal_order,
    seq_lengths,
    expert_ids,
    w_query,
    w_key,
    w_value,
    w_out,
    bias_query,
    bias_key,
    bias_value,
    norm_attn,
    norm_ffn,
    w_router,
    shared_gate,
    shared_up,
    shared_down,
    shared_switch,
    expert_gate,
    expert_up,
    expert_down,
):
    ndp, nc, dp, ctx = plane_blocks()
    planes = ndp * nc
    count = lax.axis_size("expert")
    here = lax.axis_index("expert")
    tok_count, width = tokens.shape[1], tokens.shape[2]
    group_tok = deal_order.shape[1]
    seqs = seq_lengths.shape[1]
    top = expert_ids.shape[2]
    rows_flat = w_query.shape[0]
    part = HD // rows_flat
    heads = planes // part
    runs = count // part
    run, member = here // part, lax.rem(here, part)
    fe_width = expert_gate.shape[2]
    fs_width = shared_gate.shape[1]
    pad = -(fe_width + fs_width) % LANES
    capacity = min(tok_count, 5 * tok_count * top // (4 * count))
    wide = heads * HD
    all_rows = count * tok_count
    block = width // planes

    token_rows = tokens[0]

    def by_head(w):
        w = w.reshape(rows_flat, part, heads, runs, HD).transpose(3, 1, 0, 2, 4)
        return w.reshape(count, rows_flat, wide)

    qkv_out = jnp.concatenate([by_head(w) for w in (w_query, w_key, w_value)], -1)
    all_tokens = lax.all_gather(token_rows, "expert", axis=0, tiled=True)
    qkv_rows = lax.all_to_all(qkv_out, "expert", split_axis=0, concat_axis=0, tiled=True)
    small = jnp.concatenate(
        [
            v.astype(F32).reshape(-1)
            for v in (
                bias_query,
                bias_key,
                bias_value,
                norm_attn,
                norm_ffn,
                shared_switch,
                w_router,
                deal_order,
                seq_lengths,
                expert_ids,
            )
        ]
    )
    small_plane = small_gather(small[None], ("context", "dp"))

    def stacked(routed, shared):
        none = jnp.zeros((routed.shape[0], pad), BF16)
        return jnp.concatenate([routed, shared, none], 1)

    def turned(routed, shared, h):
        columns = slice(h * block // 2, (h + 1) * block // 2)
        return stacked(routed[:, columns].T, shared[:, columns].T)

    def rows_half(x, h):
        return x[h * block // 2 : (h + 1) * block // 2]

    gate = Gather(stacked(expert_gate[0], shared_gate))
    up = Gather(
        *[stacked(rows_half(expert_up[0], h), rows_half(shared_up, h)) for h in range(2)]
    )
    down = Gather(*[turned(expert_down[0], shared_down, h) for h in range(2)])
    out_w = Gather(w_out)
    out_w.direct()
    gate.direct()
    qkv_own = qkv_rows.reshape(count * rows_flat, 3 * wide)
    qkv_own, (gate.across, gate.along, up.own, down.own, small_plane) = tie(
        qkv_own, (gate.across, gate.along, up.own, down.own, small_plane)
    )
    all_grads = lax.all_gather(
        tie(cotangent[0], qkv_own)[0], "expert", axis=0, tiled=True
    )
    qkv_w = Gather(qkv_own)
    qkv_w.direct()
    small_all = small_gather(small_plane.reshape(1, -1), ("expert",))
    small_all = small_all.reshape(count, ndp * nc, -1).transpose(1, 0, 2)
    small_all = small_all.reshape(ndp * nc * count, -1)
    qkv_w.far()
    qkv_pieces = Pieces(qkv_w)
    (out_w.across, out_w.along, gate.across, gate.along, down.own), _ = tie(
        (out_w.across, out_w.along, gate.across, gate.along, down.own),
        (qkv_w.far_top, qkv_w.far_bottom),
    )
    out_w.far()
    gate.far()
    down.send_along(0)
    wo_pieces = Pieces(out_w)
    wo_planes = jnp.zeros((2 * planes, rows_flat // 2, width), BF16)
    for key, number in zip(wo_pieces.keys, list(wo_pieces.places)):
        array, row = wo_pieces.found[key]
        array = wo_pieces.arrays[array][row : row + rows_flat // 2]
        wo_planes = lax.dynamic_update_slice_in_dim(wo_planes, array[None], number, 0)
    wo_mine = core_exchange(wo_planes.reshape(part, heads, rows_flat, width), part)
    w_o = wo_mine.transpose(1, 0, 2, 3).reshape(wide, width)

    columns = {}
    place = 0
    for name in ("bq", "bk", "bv", "na", "nf", "sw"):
        columns[name] = small_all[:, place : place + rows_flat].reshape(-1)
        place += rows_flat
    router = small_all[:, place : place + rows_flat * count].reshape(-1, count).astype(BF16)
    place += rows_flat * count
    plane_small = lax.dynamic_index_in_dim(
        small_all.reshape(ndp, nc, count, -1), dp, 0, keepdims=False
    )
    order = plane_small[0, :, place : place + group_tok].astype(jnp.int32)
    place += group_tok
    lengths = plane_small[0, :, place : place + seqs].astype(jnp.int32)
    place += seqs
    ids = plane_small[..., place:].reshape(nc, count, tok_count, top).astype(jnp.int32)
    gain_attn, gain_ffn = columns["na"], columns["nf"]
    router_switch = jnp.concatenate(
        [
            router,
            columns["sw"].astype(BF16)[:, None],
            jnp.zeros((width, LANES - count - 1), BF16),
        ],
        1,
    )

    local_index = ctx * tok_count + jnp.arange(tok_count, dtype=jnp.int32)
    ends = jnp.cumsum(lengths, 1)
    starts = ends - lengths

    def segments(index):
        segment = jnp.sum((index[None, :, None] >= ends[:, None, :]).astype(jnp.int32), -1)
        hot = segment[..., None] == jnp.arange(seqs, dtype=jnp.int32)
        return segment, index[None, :] - jnp.sum(jnp.where(hot, starts[:, None, :], 0), -1)

    query_segment, position = segments(local_index)
    allowed = []
    for s in range(nc):
        key_index = local_index - s * tok_count
        key_segment, _ = segments(key_index)
        allowed.append(
            (query_segment[:, :, None] == key_segment[:, None, :])
            & (key_index[None, None, :] <= local_index[None, :, None])
            & (key_index >= 0)[None, None, :]
        )
    allowed = jnp.concatenate(allowed, -1).astype(F32)
    frequency = ROPE_BASE ** (-2.0 * jnp.arange(HD // 2, dtype=F32) / HD)
    angles = position.reshape(-1).astype(F32)[:, None] * frequency[None, :]
    cosine = jnp.concatenate([jnp.cos(angles)] * 2, -1)
    sine = jnp.sin(angles)
    sine_table = jnp.concatenate([-sine, sine], -1)

    def own_heads(row):
        row = row.reshape(part, heads, runs, HD)
        row = lax.dynamic_index_in_dim(row, member, 0, keepdims=False)
        return lax.dynamic_index_in_dim(row, run, 1, keepdims=False).reshape(-1)

    bias = jnp.concatenate([own_heads(columns[k]) for k in ("bq", "bk", "bv")])
    normed, queries, key_value, inverse = qkv_project(
        all_tokens, gain_attn[None], bias[None], cosine, sine_table, qkv_pieces, wide
    )
    kvs = [key_value] + [
        lax.ppermute(key_value, "context", [(i, i + s) for i in range(nc - s)])
        for s in range(1, nc)
    ]
    kvs, (gate.far_top, gate.far_bottom, down.along, down.own, all_grads) = tie(
        kvs, (gate.far_top, gate.far_bottom, down.along, down.own, all_grads)
    )
    down.send_across(0)
    down.send_along(1)
    down.send_across(1)
    up.send_along(0)
    mixed, attn_part = attend(queries, kvs, allowed, w_o)
    attn_out = lax.psum_scatter(attn_part, "expert", scatter_dimension=0, tiled=True)
    attn_out, (down.across, down.along, up.along, up.own) = tie(
        attn_out, (down.across, down.along, up.along, up.own)
    )
    up.send_across(0)
    up.send_along(1)
    down.send_far_along()
    up.send_across(1)
    residual = token_rows.astype(F32) + attn_out.astype(F32)
    unit_two, scale_two = rms_unit(residual)
    rows = lax.all_gather(
        (unit_two * gain_ffn).astype(BF16), "expert", axis=0, tiled=True
    )
    rows, (up.across, up.along, down.far_top) = tie(
        rows, (up.across, up.along, down.far_top)
    )
    down.send_far_across()
    up.far()

    (ids, order), _ = tie((ids, order), key_value)
    hit = jnp.any(ids == here, -1)
    below = jnp.arange(tok_count)[:, None] < jnp.arange(tok_count)[None, :]
    slot = mat_dot(hit.reshape(nc * count, tok_count).astype(BF16), below.astype(BF16))
    kept = (hit & (slot.reshape(nc, count, tok_count) < capacity)).astype(F32)
    kept = kept.transpose(1, 0, 2).reshape(count, group_tok)
    kept_rows = jnp.sum(
        jnp.where(order[:, None, :] == local_index[None, :, None], kept[:, None, :], 0.0), -1
    ).reshape(all_rows)

    gate_pieces, up_pieces, down_pieces = Pieces(gate), Pieces(up), Pieces(down)
    gh = hidden_grad(all_grads, down_pieces)
    scaled, grad_gate, grad_up, grad_small = ffn(
        rows,
        router_switch,
        kept_rows[:, None],
        gh,
        here.astype(jnp.int32)[None],
        gate_pieces,
        up_pieces,
        fe_width,
        count,
    )
    def halves_of(acts, grads):
        return lambda numbers, dtype: weight_grad(acts, grads, numbers, block // 2, dtype)

    down_sum = Scatter(halves_of(all_grads, scaled))
    gate_sum = Scatter(halves_of(rows, grad_gate))
    up_sum = Scatter(halves_of(rows, grad_up))
    down_far, down_free = down_sum.far(), down_sum.free()
    grad_rows = spread([(grad_gate, gate_pieces), (grad_up, up_pieces)], (grad_small, router_switch))
    grad_rows, down_far = tie(grad_rows, down_far)
    grad_normed_two = lax.psum_scatter(
        grad_rows, "expert", scatter_dimension=0, tiled=True
    ).astype(F32)
    down_last = down_sum.last(down_far)
    grad_normed_two, (down_free, down_last) = tie(
        grad_normed_two, (down_free, down_last)
    )
    gate_free, gate_far = gate_sum.free(), gate_sum.far()
    grad_router_switch = left_dot(rows, grad_small)

    grad_unit = grad_normed_two * gain_ffn
    grad_residual = cotangent[0].astype(F32) + scale_two * (
        grad_unit - unit_two * jnp.mean(grad_unit * unit_two, -1, keepdims=True)
    )
    grad_gain_ffn = jnp.sum(grad_normed_two * unit_two, 0)
    attn_own = grad_residual.astype(BF16)
    grad_attn = lax.all_gather(attn_own, "expert", axis=0, tiled=True)
    output = lax.psum_scatter(
        spread([(tie(scaled, attn_own)[0], down_pieces)]),
        "expert",
        scatter_dimension=0,
        tiled=True,
    )
    grad_attn, (gate_free, gate_far) = tie(grad_attn, (gate_free, gate_far))
    gate_last = gate_sum.last(gate_far)
    up_free = up_sum.free()
    grad_query, grad_own, *grad_far = attend_back(
        queries, kvs, allowed, w_o, grad_attn, cosine, sine_table
    )
    grad_far, (up_free, gate_last, down_last) = tie(
        grad_far, (up_free, gate_last, down_last)
    )
    grad_down_w = down_sum.finish(down_free, down_last)
    grad_far = [
        lax.ppermute(piece, "context", [(i + s, i) for i in range(nc - s)])
        for s, piece in enumerate(grad_far, 1)
    ]
    up_far = up_sum.far()
    grad_qkv, bias_sums = join(grad_query, grad_own, grad_far, cosine, sine_table)
    grad_qkv, (output, gate_last, mixed) = tie(grad_qkv, (output, gate_last, mixed))
    grad_gate_w = gate_sum.finish(gate_free, gate_last)
    out_tokens = (residual + output.astype(F32)).astype(BF16)
    grad_normed = spread([(grad_qkv, qkv_pieces)])
    grad_normed_own = lax.psum_scatter(
        grad_normed, "expert", scatter_dimension=0, tiled=True
    ).astype(F32)

    qkv_sum = Scatter(halves_of(normed, grad_qkv))
    qkv_far, qkv_free = qkv_sum.far(), qkv_sum.free()
    qkv_far, up_far = tie(qkv_far, up_far)
    qkv_last = qkv_sum.last(qkv_far)
    qkv_last, up_far = tie(qkv_last, up_far)
    up_last = up_sum.last(up_far)
    qkv_grad_rows = qkv_sum.finish(qkv_free, qkv_last)
    grad_up_w = up_sum.finish(up_free, up_last)
    qkv_back = lax.all_to_all(
        qkv_grad_rows.astype(BF16).reshape(count, rows_flat, 3 * wide),
        "expert",
        split_axis=0,
        concat_axis=0,
        tiled=True,
    )

    def from_heads(i):
        w = qkv_back[..., i * wide : (i + 1) * wide].astype(F32)
        w = w.reshape(runs, part, rows_flat, heads, HD).transpose(2, 1, 3, 0, 4)
        return w.reshape(rows_flat, width)

    grad_wo = left_dot(mixed, grad_attn).astype(BF16).reshape(heads, part, rows_flat, width)
    wo_back = core_exchange(grad_wo.transpose(1, 0, 2, 3), part)
    wo_back = wo_back.reshape(2 * planes, rows_flat // 2, width)
    wo_sum = Scatter(
        lambda numbers, dtype: [
            lax.dynamic_index_in_dim(wo_back, i, 0, keepdims=False).astype(dtype)
            for i in numbers
        ]
    )
    grad_w_out = wo_sum.finish(wo_sum.free(), wo_sum.last(wo_sum.far()))

    def to_heads(row):
        full = jnp.zeros((part, heads, runs, HD), F32)
        full = lax.dynamic_update_slice(
            full, row.reshape(1, heads, 1, HD), (member, 0, run, 0)
        )
        return full.reshape(planes * count, rows_flat)

    bias_sums = bias_sums[0]
    grad_gain_attn = jnp.sum(
        grad_normed.astype(F32) * (all_tokens.astype(F32) * inverse), 0
    )
    small_grads = jnp.concatenate(
        [to_heads(bias_sums[i * wide : (i + 1) * wide]) for i in range(3)]
        + [
            grad_gain_attn.reshape(-1, rows_flat),
            grad_gain_ffn.reshape(-1, rows_flat),
            grad_router_switch[:, count].reshape(-1, rows_flat),
            grad_router_switch[:, :count].reshape(planes * count, rows_flat * count),
        ],
        1,
    )
    small_sum = small_scatter(small_grads)
    pieces = [small_sum[i * rows_flat : (i + 1) * rows_flat] for i in range(6)]
    grad_router = small_sum[6 * rows_flat :].reshape(rows_flat, count)

    unit_one, scale_one = rms_unit(token_rows.astype(F32))
    grad_unit = grad_normed_own * gain_attn
    grad_tokens = grad_residual + scale_one * (
        grad_unit - unit_one * jnp.mean(grad_unit * unit_one, -1, keepdims=True)
    )
    return (
        out_tokens[None],
        grad_tokens.astype(BF16)[None],
        from_heads(0),
        from_heads(1),
        from_heads(2),
        grad_w_out,
        pieces[0],
        pieces[1],
        pieces[2],
        pieces[3],
        pieces[4],
        grad_router,
        grad_gate_w[:, fe_width : fe_width + fs_width],
        grad_up_w[:, fe_width : fe_width + fs_width],
        grad_down_w[:, fe_width : fe_width + fs_width].T,
        pieces[5],
        grad_gate_w[None, :, :fe_width],
        grad_up_w[None, :, :fe_width],
        grad_down_w[:, :fe_width].T[None],
    )


def solution(mesh):
    every = ("dp", "context", "expert")
    plane = ("dp", "context")
    rows = P(("dp", "expert"), "context", None)
    groups = P(("dp", "expert"), None)
    return jax.shard_map(
        body,
        mesh=mesh,
        in_specs=(
            rows,
            rows,
            groups,
            groups,
            rows,
            *[P(every, None)] * 4,
            *[P(every)] * 5,
            P(every, None),
            P(plane, "expert"),
            P(plane, "expert"),
            P("expert", plane),
            P(every),
            P("expert", plane, None),
            P("expert", plane, None),
            P("expert", None, plane),
        ),
        out_specs=(
            rows,
            rows,
            *[P(every, None)] * 4,
            *[P(every)] * 5,
            P(every, None),
            P(plane, "expert"),
            P(plane, "expert"),
            P("expert", plane),
            P(every),
            P("expert", plane, None),
            P("expert", plane, None),
            P("expert", None, plane),
        ),
        check_vma=False,
    )
```

time: 1100 us -> 827 us (0.75)
  waiting for transfers between devices: 568 us -> 267 us
  Pallas kernels: 0 us -> 233 us
  matrix products: 185 us -> 6.76 us
  other arithmetic: 105 us -> 78.2 us
  local copies, waits for them, and re-layouts: 137 us -> 122 us
  starting transfers between devices: 80.8 us -> 93.4 us
    pallas_call x0 -> x21, Pallas kernels: none -> 233 us  [the longest x12 84.1 us: weight_grad(): pl.pallas_call(functools.partial(weight_grad_kernel, n, half), out_shape=...]
    ppermute x50 -> x54, waiting for transfers between devices: 320 us -> 193 us  [shift(): return lax.ppermute(x, axis, [(i, (i + step) % n) for i in range(n)])]
    dot_general x11 -> x0, matrix products: 76.2 us -> none  [the longest x6 68.5 us: right_dot(): lax.dot_general(left_mat, right_mat, (((1,), (1,)), ((), ())), preferred_...]
    reduce_scatter x4, waiting for transfers between devices: 100 us -> 24.4 us  [the longest x1 22 us: body(): lax.psum_scatter(grad_rows, 'expert', scatter_dimension=0, tiled=True)]
    dot_general x7 -> x1, matrix products: 55.6 us -> 0.19 us  [mat_dot(): return jnp.dot(left_mat, right_mat, preferred_element_type=F32)]
    all_gather x2, waiting for transfers between devices: 45.4 us -> 0.01 us  [the longest x1 0.01 us: body(): lax.all_gather(tie(cotangent[0], qkv_own)[0], 'expert', axis=0, tiled=True)]
    dot_general x18 -> x2, matrix products: 51.2 us -> 6.57 us  [left_dot(): lax.dot_general(left_mat, right_mat, (((0,), (0,)), ((), ())), preferred_...]
    unnamed x187 -> x191, local copies, waits for them, and re-layouts: 27.5 us -> 54.8 us
  transfers between devices with their start and end apart: 74 -> 78, of which waited for: 34 -> 34; matrix products, arithmetic and copies ran while one was open for 23% -> 20% of each run, Pallas kernels for 0% -> 22%
where the time goes in v1:
time: 827 us; the launch traced here: 816 us
  waiting for transfers between devices  267 us (32%)
  Pallas kernels  233 us (28%)
  local copies, waits for them, and re-layouts  122 us (15%)
  starting transfers between devices  93.4 us (11%)
  other arithmetic  78.2 us (9%)
  between operations  16.1 us (2%)
    ppermute x54, waiting for transfers between devices, shift(): return lax.ppermute(x, axis, [(i, (i + step) % n) for i in range(n)])  193 us
    pallas_call x12, Pallas kernels, weight_grad(): pl.pallas_call(functools.partial(weight_grad_kernel, n, half), out_shape=...  84.1 us
    pallas_call x3, Pallas kernels, spread(): pl.pallas_call(functools.partial(spread_kernel, tuple(arrays), half, extr...  62.7 us
    ppermute x54, starting transfers between devices, shift(): return lax.ppermute(x, axis, [(i, (i + step) % n) for i in range(n)])  60.9 us
    unnamed x191, local copies, waits for them, and re-layouts  54.8 us
    ppermute x5, waiting for transfers between devices, small_gather(): other = lax.ppermute(x, axis, pairs)  37.6 us
    pallas_call x1, Pallas kernels, ffn(): pl.pallas_call(functools.partial(ffn_kernel, gates.counts, ups.counts, ga...  35.6 us
    reduce_scatter x1, waiting for transfers between devices, body(): lax.psum_scatter(grad_rows, 'expert', scatter_dimension=0, tiled=True)  22 us
  transfers between devices with their start and end apart: 78, of which 34 were waited for; matrix products, arithmetic and copies ran while one was open for 20% of the time, Pallas kernels for 22%

profile of v1, /device:TPU:0, one launch (start us, length us, event | category | flops | bytes accessed | tf_op | source)
XLA Modules:
  0.0 816.2 jit_solution(14750347757524137926)
XLA Ops:
  34.6 31.9 %collective-permute-done.2 = f32[1,1666]{1,0:T(1,128)S(1)} collective-permute-done((f32[1,1666]{1,0:T(1,128)S(1)}, f32[1,1666]{1,0:T(1,128)S(1)}, u32[]{:S(2)}, u32[]{:S(2)}) %collective-permute-start.2) | collective-permute-done | bytes 6696 | tf_op jit(solution)/shard_map/ppermute | solution.py:186
  108.2 6.4 collective-permute-done.8.refs_2_.refs_4_
  147.3 7.2 qkv_project.1
  163.5 18.5 %collective-permute-done.19.refs_2_.refs_4_ = bf16[256,2176]{1,0:T(8,128)(2,1)} collective-permute-done((bf16[256,2176]{1,0:T(8,128)(2,1)}, bf16[256,2176]{1,0:T(8,128)(2,1)}, u32[]{:S(2)}, u32[]{:S(2)}) %collective-permute-start.19) | collective-permute-done | bytes 1114144 | tf_op jit(solution)/shard_map/ppermute | solution.py:37
  186.5 8.8 %attend.1 = (bf16[1024,256]{1,0:T(8,128)(2,1)S(1)}, bf16[1024,2048]{1,0:T(8,128)(2,1)S(1)}) custom-call(bf16[1024,256]{1,0:T(8,128)(2,1)S(1)} %copy-done.26, f32[8,128,256]{2,1,0:T(8,128)S(1)} %add_convert_fusion.7.allowed, bf16[256,2048]{1,0:T(8,128)(2,1)S(1)} %bitcast.185, bf16[1024,512]{1,0:T(8,128)(2,1)S(1)} %copy-done.17, bf16[1024,512]{1,0:T(8,128)(2,1)S(1)} %copy-done.20), custom_call_target="tpu_custom_call" | custom-call | flops 1342177280 | bytes 8388608 | tf_op jit(solution)/shard_map/attend/pallas_call | solution.py:594
  202.5 23.7 %collective-permute-done.23.refs_14_.refs_10_ = bf16[256,2176]{1,0:T(8,128)(2,1)} collective-permute-done((bf16[256,2176]{1,0:T(8,128)(2,1)}, bf16[256,2176]{1,0:T(8,128)(2,1)}, u32[]{:S(2)}, u32[]{:S(2)}) %collective-permute-start.23) | collective-permute-done | bytes 1114144 | tf_op jit(solution)/shard_map/ppermute | solution.py:37
  227.0 17.0 %collective-permute-done.22.refs_5_.refs_7_ = bf16[256,2176]{1,0:T(8,128)(2,1)} collective-permute-done((bf16[256,2176]{1,0:T(8,128)(2,1)}, bf16[256,2176]{1,0:T(8,128)(2,1)}, u32[]{:S(2)}, u32[]{:S(2)}) %collective-permute-start.22) | collective-permute-done | bytes 1114144 | tf_op jit(solution)/shard_map/ppermute | solution.py:37
  265.1 13.5 %collective-permute-done.24.refs_13_.refs_9_ = bf16[256,2176]{1,0:T(8,128)(2,1)} collective-permute-done((bf16[256,2176]{1,0:T(8,128)(2,1)}, bf16[256,2176]{1,0:T(8,128)(2,1)}, u32[]{:S(2)}, u32[]{:S(2)}) %collective-permute-start.24) | collective-permute-done | bytes 1114144 | tf_op jit(solution)/shard_map/ppermute | solution.py:37
  280.0 20.8 %collective-permute-done.26.refs_17_.refs_13_ = bf16[256,2176]{1,0:T(8,128)(2,1)} collective-permute-done((bf16[256,2176]{1,0:T(8,128)(2,1)}, bf16[256,2176]{1,0:T(8,128)(2,1)}, u32[]{:S(2)}, u32[]{:S(2)}) %collective-permute-start.26) | collective-permute-done | bytes 1114144 | tf_op jit(solution)/shard_map/ppermute | solution.py:37
  308.4 17.8 %collective-permute-done.28.refs_7_.refs_9_ = bf16[256,2176]{1,0:T(8,128)(2,1)} collective-permute-done((bf16[256,2176]{1,0:T(8,128)(2,1)}, bf16[256,2176]{1,0:T(8,128)(2,1)}, u32[]{:S(2)}, u32[]{:S(2)}) %collective-permute-start.28) | collective-permute-done | bytes 1114144 | tf_op jit(solution)/shard_map/ppermute | solution.py:37
  327.5 16.8 %hidden_grad.1.refs_6_ = f32[1024,2176]{1,0:T(8,128)} custom-call(s32[8]{0:T(128)S(1)} %stack.47.places.refs_1_.refs_0_, bf16[1024,2048]{1,0:T(8,128)(2,1)} %all-gather.6.cloned.1.call-done.acts.refs_0_.refs_1_.refs_2_.refs_3_, bf16[256,2176]{1,0:T(8,128)(2,1)} %concatenate.74.refs_0_.refs_2_, bf16[256,2176]{1,0:T(8,128)(2,1)} %collective-permute-done.20.refs_1_.refs_3_, ...), custom_call_target="tpu_custom_call" | custom-call | flops 9126805504 | bytes 20971520 | tf_op jit(solution)/shard_map/hidden_grad/pallas_call | solution.py:300
  346.8 35.6 %ffn.1 = (bf16[1024,2176]{1,0:T(8,128)(2,1)}, bf16[1024,2176]{1,0:T(8,128)(2,1)}, bf16[1024,2176]{1,0:T(8,128)(2,1)}, bf16[1024,128]{1,0:T(8,128)(2,1)S(1)}) custom-call(s32[8]{0:T(128)S(1)} %stack.46.places.refs_0_, s32[8]{0:T(128)S(1)} %stack.47.places.refs_1_.refs_0_, s32[1]{0:T(128)} %bitcast.44.refs_2_, ...), custom_call_target="tpu_custom_call" | custom-call | flops 18253611008 | bytes 41943040 | tf_op jit(solution)/shard_map/ffn/pallas_call | solution.py:408
  382.4 7.0 weight_grad.12
  392.4 34.3 %spread.3 = bf16[1024,2048]{1,0:T(8,128)(2,1)} custom-call(s32[8]{0:T(128)} %copy-done.37, bf16[1024,2176]{1,0:T(8,128)(2,1)} %get-tuple-element.181.refs_1_.refs_2_.refs_4_, bf16[1024,2176]{1,0:T(8,128)(2,1)} %get-tuple-element.182.refs_2_.refs_4_, bf16[512,2176]{1,0:T(8,128)(2,1)} %concatenate.71.refs_7_.refs_3_, ...), custom_call_target="tpu_custom_call" | custom-call | flops 18253611008 | bytes 20971520 | tf_op jit(solution)/shard_map/spread/pallas_call | solution.py:488
  426.8 7.5 weight_grad.13
  435.4 10.3 %weight_grad.14 = (f32[256,2176]{1,0:T(8,128)S(1)}, f32[256,2176]{1,0:T(8,128)S(1)}, f32[256,2176]{1,0:T(8,128)}, f32[256,2176]{1,0:T(8,128)}) custom-call(s32[4]{0:T(128)S(1)} %pad_add_fusion.2.numbers, bf16[1024,2048]{1,0:T(8,128)(2,1)} %all-gather.6.cloned.1.call-done.acts.refs_0_.refs_1_.refs_2_.refs_3_, ...), custom_call_target="tpu_custom_call" | custom-call | flops 4563402752 | bytes 12582912 | tf_op jit(solution)/shard_map/weight_grad/pallas_call | solution.py:260
  453.6 22.0 %reduce-scatter.7.cloned.1.call-done = bf16[128,2048]{1,0:T(8,128)(2,1)} async-done(((bf16[1024,2048]{1,0:T(8,128)(2,1)}), bf16[128,2048]{1,0:T(8,128)(2,1)}) %reduce-scatter.7.cloned.1.call-update) | async-done | bytes 524304 | tf_op jit(solution)/shard_map/reduce_scatter | solution.py:975
  484.5 18.8 %spread.4 = bf16[1024,2048]{1,0:T(8,128)(2,1)} custom-call(s32[8]{0:T(128)} %copy-done.38, bf16[1024,2176]{1,0:T(8,128)(2,1)} %get-tuple-element.213.refs_2_.refs_4_.refs_1_, bf16[256,2176]{1,0:T(8,128)(2,1)} %concatenate.74.refs_0_.refs_2_, bf16[256,2176]{1,0:T(8,128)(2,1)} %collective-permute-done.20.refs_1_.refs_3_, ...), custom_call_target="tpu_custom_call" | custom-call | flops 9126805504 | bytes 20971520 | tf_op jit(solution)/shard_map/spread/pallas_call | solution.py:488
  503.4 7.2 weight_grad.16
  512.1 7.0 weight_grad.15
  527.0 7.1 weight_grad.17
  535.6 10.3 %weight_grad.18 = (f32[256,2176]{1,0:T(8,128)S(1)}, f32[256,2176]{1,0:T(8,128)S(1)}, f32[256,2176]{1,0:T(8,128)}, f32[256,2176]{1,0:T(8,128)}) custom-call(s32[4]{0:T(128)S(1)} %pad_add_fusion.2.numbers, bf16[1024,2048]{1,0:T(8,128)(2,1)} %all-gather.8.cloned.1.call-done.refs_3_.refs_0_.refs_1_.refs_2_, ...), custom_call_target="tpu_custom_call" | custom-call | flops 4563402752 | bytes 12582912 | tf_op jit(solution)/shard_map/weight_grad/pallas_call | solution.py:260
  549.2 13.2 %collective-permute-done.37 = bf16[256,2176]{1,0:T(8,128)(2,1)} collective-permute-done((bf16[256,2176]{1,0:T(8,128)(2,1)}, bf16[256,2176]{1,0:T(8,128)(2,1)}, u32[]{:S(2)}, u32[]{:S(2)}) %collective-permute-start.37) | collective-permute-done | bytes 1114144 | tf_op jit(solution)/shard_map/ppermute | solution.py:37
  562.3 8.5 %collective-permute-done.38 = bf16[256,2176]{1,0:T(8,128)(2,1)} collective-permute-done((bf16[256,2176]{1,0:T(8,128)(2,1)}, bf16[256,2176]{1,0:T(8,128)(2,1)}, u32[]{:S(2)}, u32[]{:S(2)}) %collective-permute-start.38) | collective-permute-done | bytes 1114144 | tf_op jit(solution)/shard_map/ppermute | solution.py:37
  581.1 7.1 weight_grad.22
  589.6 10.3 %weight_grad.23 = (f32[256,2176]{1,0:T(8,128)S(1)}, f32[256,2176]{1,0:T(8,128)S(1)}, f32[256,2176]{1,0:T(8,128)}, f32[256,2176]{1,0:T(8,128)}) custom-call(s32[4]{0:T(128)S(1)} %pad_add_fusion.2.numbers, bf16[1024,2048]{1,0:T(8,128)(2,1)} %all-gather.8.cloned.1.call-done.refs_3_.refs_0_.refs_1_.refs_2_, ...), custom_call_target="tpu_custom_call" | custom-call | flops 4563402752 | bytes 12582912 | tf_op jit(solution)/shard_map/weight_grad/pallas_call | solution.py:260
  608.5 15.0 %attend_back.1 = (bf16[1024,256]{1,0:T(8,128)(2,1)S(1)}, f32[1024,512]{1,0:T(8,128)S(1)}, bf16[1024,512]{1,0:T(8,128)(2,1)}) custom-call(bf16[1024,256]{1,0:T(8,128)(2,1)S(1)} %copy-done.27, f32[8,128,256]{2,1,0:T(8,128)S(1)} %add_convert_fusion.7.allowed, bf16[256,2048]{1,0:T(8,128)(2,1)S(1)} %bitcast.186, bf16[1024,2048]{1,0:T(8,128)(2,1)S(1)} %copy-done.4, ...), custom_call_target="tpu_custom_call" | custom-call | flops 1879048192 | bytes 8388608 | tf_op jit(solution)/shard_map/attend_back/pallas_call | solution.py:653
  643.0 7.4 collective-permute-done.45.refs_0_
  659.4 9.7 %spread.5 = bf16[1024,2048]{1,0:T(8,128)(2,1)} custom-call(s32[8]{0:T(128)} %copy-done.37, bf16[1024,768]{1,0:T(8,128)(2,1)} %copy-done.1, bf16[512,768]{1,0:T(8,128)(2,1)} %bitcast.191, bf16[512,768]{1,0:T(8,128)(2,1)} %copy-done.36, bf16[512,768]{1,0:T(8,128)(2,1)} %copy-done.35, bf16[256,768]{1,0:T(8,128)(2,1)} %collective-permute-done.9.refs_3_.refs_5_, ...), custom_call_target="tpu_custom_call" | custom-call | flops 3221225472 | bytes 20971520 | tf_op jit(solution)/shard_map/spread/pallas_call | solution.py:488
  686.1 9.3 %collective-permute-start.63 = (f32[4,896]{1,0:T(4,128)S(1)}, f32[4,896]{1,0:T(4,128)S(1)}, u32[]{:S(2)}, u32[]{:S(2)}) collective-permute-start(f32[4,896]{1,0:T(4,128)S(1)} %slice_select_fusion.2), channel_id=1, source_target_pairs={{0,4},{1,5},{2,6},{3,7},{4,0},{5,1},{6,2},{7,3},{8,12},{9,13},{10,... | collective-permute-start | bytes 43016 | tf_op jit(solution)/shard_map/ppermute | solution.py:199
  742.7 5.0 collective-permute-done.51
  761.6 21.4 %collective-permute-done.66 = bf16[256,2176]{1,0:T(8,128)(2,1)S(1)} collective-permute-done((bf16[256,2176]{1,0:T(8,128)(2,1)S(1)}, bf16[256,2176]{1,0:T(8,128)(2,1)S(1)}, u32[]{:S(2)}, u32[]{:S(2)}) %collective-permute-start.66) | collective-permute-done | bytes 1114144 | tf_op jit(solution)/shard_map/ppermute | solution.py:37
  (542 shorter events, 344.0 us)
Async XLA Ops:
  7.2 137.9 %all-gather.12.cloned.1.call-start = ((), (), s32[]{:S(2)}) async-start(), calls=%async_computation.13 | async-start | bytes 4718592 | tf_op jit(solution)/shard_map/all_gather | solution.py:782
  7.2 112.5 %collective-permute-start.12 = (bf16[64,2048]{1,0:T(8,128)(2,1)}, bf16[64,2048]{1,0:T(8,128)(2,1)}, u32[]{:S(2)}, u32[]{:S(2)}) collective-permute-start(bf16[64,2048]{1,0:T(8,128)(2,1)} %param.30), channel_id=1, source_target_pairs={{0,16},{16,0},{1,17},{17,1},{2,18},{18,2},{3,19},{19,3},{4,20},{20... | collective-permute-start | bytes 786440 | tf_op jit(solution)/shard_map/ppermute | solution.py:37
  10.3 109.5 %collective-permute-start.11 = (bf16[64,2048]{1,0:T(8,128)(2,1)}, bf16[64,2048]{1,0:T(8,128)(2,1)}, u32[]{:S(2)}, u32[]{:S(2)}) collective-permute-start(bf16[64,2048]{1,0:T(8,128)(2,1)} %param.30), channel_id=1, source_target_pairs={{0,8},{8,0},{1,9},{9,1},{2,10},{10,2},{3,11},{11,3},{4,12},{12,4},... | collective-permute-start | bytes 786440 | tf_op jit(solution)/shard_map/ppermute | solution.py:37
  16.2 71.6 %collective-permute-start.1 = (bf16[512,2176]{1,0:T(8,128)(2,1)}, bf16[512,2176]{1,0:T(8,128)(2,1)}, u32[]{:S(2)}, u32[]{:S(2)}) collective-permute-start(bf16[512,2176]{1,0:T(8,128)(2,1)} %concatenate.71.refs_7_.refs_3_), channel_id=1, source_target_pairs={{0,16},{16,0},{1,17},{17,1},{2,18},{18,2},{3,19},{19,3},{4,20},{20... | collective-permute-start | bytes 6684680 | tf_op jit(solution)/shard_map/ppermute | solution.py:37
  16.7 71.1 %collective-permute-start = (bf16[512,2176]{1,0:T(8,128)(2,1)}, bf16[512,2176]{1,0:T(8,128)(2,1)}, u32[]{:S(2)}, u32[]{:S(2)}) collective-permute-start(bf16[512,2176]{1,0:T(8,128)(2,1)} %concatenate.71.refs_7_.refs_3_), channel_id=1, source_target_pairs={{0,8},{8,0},{1,9},{9,1},{2,10},{10,2},{3,11},{11,3},{4,12},{12,4},... | collective-permute-start | bytes 6684680 | tf_op jit(solution)/shard_map/ppermute | solution.py:37
  17.5 49.0 %collective-permute-start.2 = (f32[1,1666]{1,0:T(1,128)S(1)}, f32[1,1666]{1,0:T(1,128)S(1)}, u32[]{:S(2)}, u32[]{:S(2)}) collective-permute-start(f32[1,1666]{1,0:T(1,128)S(1)} %broadcast_in_dim.118), channel_id=1, source_target_pairs={{0,8},{8,0},{1,9},{9,1},{2,10},{10,2},{3,11},{11,3},{4,12},{12,4},... | collective-permute-start | bytes 20000 | tf_op jit(solution)/shard_map/ppermute | solution.py:186
  22.1 65.7 %all-to-all-start = ((bf16[8,64,768]{2,1,0:T(8,128)(2,1)}), bf16[8,64,768]{2,1,0:T(8,128)(2,1)S(1)}, u32[]{:S(2)}, u32[]{:S(2)}) async-start(bf16[8,64,768]{2,1,0:T(8,128)(2,1)} %pad_maximum_fusion.5), calls=%async_computation | async-start | bytes 1572864 | tf_op jit(solution)/shard_map/all_to_all | solution.py:783
  27.0 156.0 %all-gather.6.cloned.1.call-start = ((), (), s32[]{:S(2)}) async-start(), calls=%async_computation.6 | async-start | bytes 4718592 | tf_op jit(solution)/shard_map/all_gather | solution.py:826
  98.1 148.8 %reduce-scatter.5.cloned.1.call-start = ((), (), s32[]{:S(2)}) async-start(), calls=%async_computation.7 | async-start | bytes 4718592 | tf_op jit(solution)/shard_map/reduce_scatter | solution.py:924
  136.3 45.7 %collective-permute-start.19 = (bf16[256,2176]{1,0:T(8,128)(2,1)}, bf16[256,2176]{1,0:T(8,128)(2,1)}, u32[]{:S(2)}, u32[]{:S(2)}) collective-permute-start(bf16[256,2176]{1,0:T(8,128)(2,1)} %concatenate.74.refs_0_.refs_2_), channel_id=1, source_target_pairs={{0,16},{16,0},{1,17},{17,1},{2,18},{18,2},{3,19},{19,3},{4,20},{20... | collective-permute-start | bytes 3342344 | tf_op jit(solution)/shard_map/ppermute | solution.py:37
  198.2 104.2 %all-gather.8.cloned.1.call-start = ((), (), s32[]{:S(2)}) async-start(), calls=%async_computation.8 | async-start | bytes 4718592 | tf_op jit(solution)/shard_map/all_gather | solution.py:934
  200.7 43.3 %collective-permute-start.22 = (bf16[256,2176]{1,0:T(8,128)(2,1)}, bf16[256,2176]{1,0:T(8,128)(2,1)}, u32[]{:S(2)}, u32[]{:S(2)}) collective-permute-start(bf16[256,2176]{1,0:T(8,128)(2,1)} %concatenate.75.refs_3_.refs_5_), channel_id=1, source_target_pairs={{0,16},{16,0},{1,17},{17,1},{2,18},{18,2},{3,19},{19,3},{4,20},{20... | collective-permute-start | bytes 3342344 | tf_op jit(solution)/shard_map/ppermute | solution.py:37
  201.2 43.3 %collective-permute-start.21 = (bf16[256,2176]{1,0:T(8,128)(2,1)}, bf16[256,2176]{1,0:T(8,128)(2,1)}, u32[]{:S(2)}, u32[]{:S(2)}) collective-permute-start(bf16[256,2176]{1,0:T(8,128)(2,1)} %concatenate.75.refs_3_.refs_5_), channel_id=1, source_target_pairs={{0,8},{8,0},{1,9},{9,1},{2,10},{10,2},{3,11},{11,3},{4,12},{12,4},... | collective-permute-start | bytes 3342344 | tf_op jit(solution)/shard_map/ppermute | solution.py:37
  250.6 225.0 %reduce-scatter.7.cloned.1.call-start = ((), (), s32[]{:S(2)}) async-start(), calls=%async_computation.9 | async-start | bytes 4718592 | tf_op jit(solution)/shard_map/reduce_scatter | solution.py:975
  253.6 47.1 %collective-permute-start.26 = (bf16[256,2176]{1,0:T(8,128)(2,1)}, bf16[256,2176]{1,0:T(8,128)(2,1)}, u32[]{:S(2)}, u32[]{:S(2)}) collective-permute-start(bf16[256,2176]{1,0:T(8,128)(2,1)} %concatenate.73.refs_15_.refs_11_), channel_id=1, source_target_pairs={{0,16},{16,0},{1,17},{17,1},{2,18},{18,2},{3,19},{19,3},{4,20},{20... | collective-permute-start | bytes 3342344 | tf_op jit(solution)/shard_map/ppermute | solution.py:37
  254.2 48.2 %collective-permute-start.25 = (bf16[256,2176]{1,0:T(8,128)(2,1)}, bf16[256,2176]{1,0:T(8,128)(2,1)}, u32[]{:S(2)}, u32[]{:S(2)}) collective-permute-start(bf16[256,2176]{1,0:T(8,128)(2,1)} %concatenate.73.refs_15_.refs_11_), channel_id=1, source_target_pairs={{0,8},{8,0},{1,9},{9,1},{2,10},{10,2},{3,11},{11,3},{4,12},{12,4},... | collective-permute-start | bytes 3342344 | tf_op jit(solution)/shard_map/ppermute | solution.py:37
  255.0 71.3 %collective-permute-start.28 = (bf16[256,2176]{1,0:T(8,128)(2,1)}, bf16[256,2176]{1,0:T(8,128)(2,1)}, u32[]{:S(2)}, u32[]{:S(2)}) collective-permute-start(bf16[256,2176]{1,0:T(8,128)(2,1)} %collective-permute-done.22.refs_5_.refs_7_), channel_id=1, source_target_pairs={{0,8},{8,0},{1,9},{9,1},{2,10},{10,2},{3,11},{11,3},{4,12},{12,4},... | collective-permute-start | bytes 3342344 | tf_op jit(solution)/shard_map/ppermute | solution.py:37
  303.9 42.9 %collective-permute-start.30 = (bf16[256,2176]{1,0:T(8,128)(2,1)}, bf16[256,2176]{1,0:T(8,128)(2,1)}, u32[]{:S(2)}, u32[]{:S(2)}) collective-permute-start(bf16[256,2176]{1,0:T(8,128)(2,1)} %collective-permute-done.26.refs_17_.refs_13_), channel_id=1, source_target_pairs={{0,8},{8,0},{1,9},{9,1},{2,10},{10,2},{3,11},{11,3},{4,12},{12,4},... | collective-permute-start | bytes 3342344 | tf_op jit(solution)/shard_map/ppermute | solution.py:37
  426.7 144.1 %all-gather.10.cloned.1.call-start = ((), (), s32[]{:S(2)}) async-start(), calls=%async_computation.10 | async-start | bytes 4718592 | tf_op jit(solution)/shard_map/all_gather | solution.py:991
  434.3 42.5 %collective-permute-start.33 = (bf16[256,2176]{1,0:T(8,128)(2,1)}, bf16[256,2176]{1,0:T(8,128)(2,1)}, u32[]{:S(2)}, u32[]{:S(2)}) collective-permute-start(bf16[256,2176]{1,0:T(8,128)(2,1)} %get-tuple-element.188), channel_id=1, source_target_pairs={{0,8},{8,0},{1,9},{9,1},{2,10},{10,2},{3,11},{11,3},{4,12},{12,4},... | collective-permute-start | bytes 3342344 | tf_op jit(solution)/shard_map/ppermute | solution.py:37
  434.8 42.0 %collective-permute-start.34 = (bf16[256,2176]{1,0:T(8,128)(2,1)}, bf16[256,2176]{1,0:T(8,128)(2,1)}, u32[]{:S(2)}, u32[]{:S(2)}) collective-permute-start(bf16[256,2176]{1,0:T(8,128)(2,1)} %get-tuple-element.189), channel_id=1, source_target_pairs={{0,16},{16,0},{1,17},{17,1},{2,18},{18,2},{3,19},{19,3},{4,20},{20... | collective-permute-start | bytes 3342344 | tf_op jit(solution)/shard_map/ppermute | solution.py:37
  484.5 170.9 %reduce-scatter.9.cloned.1.call-start = ((), (), s32[]{:S(2)}) async-start(), calls=%async_computation.11 | async-start | bytes 4718592 | tf_op jit(solution)/shard_map/reduce_scatter | solution.py:992
  503.3 301.4 %reduce-scatter.11.cloned.1.call-start = ((), (), s32[]{:S(2)}) async-start(), calls=%async_computation.12 | async-start | bytes 4718592 | tf_op jit(solution)/shard_map/reduce_scatter | solution.py:1018
  519.7 42.6 %collective-permute-start.37 = (bf16[256,2176]{1,0:T(8,128)(2,1)}, bf16[256,2176]{1,0:T(8,128)(2,1)}, u32[]{:S(2)}, u32[]{:S(2)}) collective-permute-start(bf16[256,2176]{1,0:T(8,128)(2,1)} %get-tuple-element.195), channel_id=1, source_target_pairs={{0,8},{8,0},{1,9},{9,1},{2,10},{10,2},{3,11},{11,3},{4,12},{12,4},... | collective-permute-start | bytes 3342344 | tf_op jit(solution)/shard_map/ppermute | solution.py:37
  520.3 50.5 %collective-permute-start.38 = (bf16[256,2176]{1,0:T(8,128)(2,1)}, bf16[256,2176]{1,0:T(8,128)(2,1)}, u32[]{:S(2)}, u32[]{:S(2)}) collective-permute-start(bf16[256,2176]{1,0:T(8,128)(2,1)} %get-tuple-element.196), channel_id=1, source_target_pairs={{0,16},{16,0},{1,17},{17,1},{2,18},{18,2},{3,19},{19,3},{4,20},{20... | collective-permute-start | bytes 3342344 | tf_op jit(solution)/shard_map/ppermute | solution.py:37
  534.1 89.4 %collective-permute-start.41 = (bf16[256,2176]{1,0:T(8,128)(2,1)}, bf16[256,2176]{1,0:T(8,128)(2,1)}, u32[]{:S(2)}, u32[]{:S(2)}) collective-permute-start(bf16[256,2176]{1,0:T(8,128)(2,1)} %get-tuple-element.203), channel_id=1, source_target_pairs={{0,8},{8,0},{1,9},{9,1},{2,10},{10,2},{3,11},{11,3},{4,12},{12,4},... | collective-permute-start | bytes 3342344 | tf_op jit(solution)/shard_map/ppermute | solution.py:37
  548.6 76.5 %collective-permute-start.42 = (bf16[256,2176]{1,0:T(8,128)(2,1)}, bf16[256,2176]{1,0:T(8,128)(2,1)}, u32[]{:S(2)}, u32[]{:S(2)}) collective-permute-start(bf16[256,2176]{1,0:T(8,128)(2,1)} %get-tuple-element.204), channel_id=1, source_target_pairs={{0,16},{16,0},{1,17},{17,1},{2,18},{18,2},{3,19},{19,3},{4,20},{20... | collective-permute-start | bytes 3342344 | tf_op jit(solution)/shard_map/ppermute | solution.py:37
  574.1 51.0 %collective-permute-start.43 = (bf16[256,2176]{1,0:T(8,128)(2,1)}, bf16[256,2176]{1,0:T(8,128)(2,1)}, u32[]{:S(2)}, u32[]{:S(2)}) collective-permute-start(bf16[256,2176]{1,0:T(8,128)(2,1)} %add_convert_fusion.3), channel_id=1, source_target_pairs={{0,16},{16,0},{1,17},{17,1},{2,18},{18,2},{3,19},{19,3},{4,20},{20... | collective-permute-start | bytes 3342344 | tf_op jit(solution)/shard_map/ppermute | solution.py:37
  577.3 47.8 %collective-permute-start.44 = (bf16[256,2176]{1,0:T(8,128)(2,1)}, bf16[256,2176]{1,0:T(8,128)(2,1)}, u32[]{:S(2)}, u32[]{:S(2)}) collective-permute-start(bf16[256,2176]{1,0:T(8,128)(2,1)} %add_convert_fusion.2), channel_id=1, source_target_pairs={{0,8},{8,0},{1,9},{9,1},{2,10},{10,2},{3,11},{11,3},{4,12},{12,4},... | collective-permute-start | bytes 3342344 | tf_op jit(solution)/shard_map/ppermute | solution.py:37
  588.2 126.2 %collective-permute-start.49 = (bf16[256,2176]{1,0:T(8,128)(2,1)}, bf16[256,2176]{1,0:T(8,128)(2,1)}, u32[]{:S(2)}, u32[]{:S(2)}) collective-permute-start(bf16[256,2176]{1,0:T(8,128)(2,1)} %get-tuple-element.225), channel_id=1, source_target_pairs={{0,8},{8,0},{1,9},{9,1},{2,10},{10,2},{3,11},{11,3},{4,12},{12,4},... | collective-permute-start | bytes 3342344 | tf_op jit(solution)/shard_map/ppermute | solution.py:37
  623.5 92.9 %collective-permute-start.50 = (bf16[256,2176]{1,0:T(8,128)(2,1)}, bf16[256,2176]{1,0:T(8,128)(2,1)}, u32[]{:S(2)}, u32[]{:S(2)}) collective-permute-start(bf16[256,2176]{1,0:T(8,128)(2,1)} %get-tuple-element.226), channel_id=1, source_target_pairs={{0,16},{16,0},{1,17},{17,1},{2,18},{18,2},{3,19},{19,3},{4,20},{20... | collective-permute-start | bytes 3342344 | tf_op jit(solution)/shard_map/ppermute | solution.py:37
  750.5 45.2 %all-to-all-start.1 = ((bf16[8,64,768]{2,1,0:T(8,128)(2,1)}), bf16[8,64,768]{2,1,0:T(8,128)(2,1)S(1)}, u32[]{:S(2)}, u32[]{:S(2)}) async-start(bf16[8,64,768]{2,1,0:T(8,128)(2,1)} %bitcast.60), calls=%async_computation.5 | async-start | bytes 1572864 | tf_op jit(solution)/shard_map/all_to_all | solution.py:1030
  (137 other events, 2480.2 us)
Sparse Core Ops, SparseCore 0:
  17.0 65.5 all-gather.11
  98.2 45.7 all-gather.5
  198.3 48.5 reduce-scatter.4
  250.7 45.2 all-gather.7
  426.8 48.6 reduce-scatter.6
  484.6 49.7 all-gather.9
  536.6 48.7 reduce-scatter.8
  669.2 55.2 reduce-scatter.10

commit v2 on v1

--- a/solution.py
+++ b/solution.py
@@ -50,125 +50,141 @@
     )
 
 
-class Gather:
-    def __init__(self, *own):
-        self.own = list(own)
-        self.half = own[0].shape[0] * len(own) // 2
-        self.across, self.along = [{} for _ in own], [{} for _ in own]
-
-    def send_across(self, h):
-        nc = lax.axis_size("context")
-        self.across[h] = {s: shift(self.own[h], "context", s) for s in range(1, nc)}
-
-    def send_along(self, h):
-        ndp = lax.axis_size("dp")
-        self.along[h] = {d: shift(self.own[h], "dp", d) for d in range(1, ndp)}
-
-    def send_far_along(self):
-        ndp = lax.axis_size("dp")
-        self.far_top = {
-            (d, s): shift(x[: self.half], "dp", d)
-            for s, x in self.across[0].items()
-            for d in range(1, ndp)
+def by_context(block_of):
+    nc = lax.axis_size("context")
+    return {s: shift(block_of(s), "context", s) for s in range(1, nc)}
+
+
+def by_dp(block_of):
+    ndp = lax.axis_size("dp")
+    return {d: shift(block_of(d), "dp", d) for d in range(1, ndp)}
+
+
+class Pieces:
+    def __init__(self, found, half):
+        ndp, nc, dp, ctx = plane_blocks()
+        keys = sorted(found)
+        self.parts = [found[key] for key in keys]
+        self.arrays = [array for array, _ in self.parts]
+        self.half, self.columns = half, self.arrays[0].shape[1]
+        self.places = jnp.stack(
+            [
+                2 * (lax.rem(dp - d + ndp, ndp) * nc + lax.rem(ctx - s + nc, nc)) + h
+                for d, s, h in keys
+            ]
+        ).astype(jnp.int32)
+
+
+def gather_plain(own):
+    half = own.shape[0] // 2
+    across, along = by_context(lambda s: own), by_dp(lambda d: own)
+
+    def far(after=None):
+        tops = [x[:half] for x in across.values()]
+        bottoms = [x[half:] for x in along.values()]
+        if after is not None:
+            (tops, bottoms), _ = tie((tops, bottoms), after)
+        far_x = by_context(lambda s: jnp.concatenate(bottoms, 0))
+        far_y = by_dp(lambda d: jnp.concatenate(tops, 0))
+        found = {(0, 0, h): (own, h) for h in range(2)}
+        for s, x in across.items():
+            found.update({(0, s, h): (x, h) for h in range(2)})
+        for d, x in along.items():
+            found.update({(d, 0, h): (x, h) for h in range(2)})
+            found.update({(d, s, 0): (far_y[d], s - 1) for s in across})
+            found.update({(d, s, 1): (far_x[s], d - 1) for s in across})
+        return found, (far_x, far_y)
+
+    return across, along, far
+
+
+class Scatter:
+    def __init__(self, halves_of, half):
+        self.halves_of, self.half = halves_of, half
+
+    def make(self, first=True, last=True):
+        ndp, nc, dp, ctx = plane_blocks()
+        across, along = range(1, nc), range(1, ndp)
+
+        def group(keys, dtype):
+            return [
+                2 * (lax.rem(dp + d, ndp) * nc + lax.rem(ctx + s, nc)) + h for d, s, h in keys
+            ], dtype
+
+        groups = []
+        if first:
+            groups += [group([*((d, s, 0) for d in along), (0, s, 0)], BF16) for s in across]
+            groups += [group([*((d, s, 1) for s in across), (d, 0, 1)], BF16) for d in along]
+        if last:
+            groups += [group([(0, s, 1)], F32) for s in across]
+            groups += [group([(d, 0, 0)], F32) for d in along]
+            groups.append(group([(0, 0, 0), (0, 0, 1)], F32))
+        made = list(self.halves_of(groups))
+        if first:
+            self.to_across = dict(zip(across, made))
+            self.to_along = dict(zip(along, made[nc - 1 :]))
+            made = made[nc - 1 + ndp - 1 :]
+        if last:
+            self.near_across = dict(zip(across, made))
+            self.near_along = dict(zip(along, made[nc - 1 :]))
+            self.own = made[-1]
+        return made
+
+    def send_first(self, after=()):
+        (across, along), _ = tie((self.to_across, self.to_along), after)
+        self.across = by_context(lambda s: across[s])
+        self.along = by_dp(lambda d: along[d])
+        return self.across, self.along
+
+    def row(self, x, i):
+        return x[i * self.half : (i + 1) * self.half].astype(F32)
+
+    def sums(self):
+        across = {
+            s: (x + sum(self.row(y, s - 1) for y in self.along.values())).astype(BF16)
+            for s, x in self.near_across.items()
         }
-
-    def send_far_across(self):
-        nc = lax.axis_size("context")
-        self.far_bottom = {
-            (d, s): shift(x[-self.half :], "context", s)
-            for d, x in self.along[-1].items()
-            for s in range(1, nc)
+        along = {
+            d: (x + sum(self.row(y, d - 1) for y in self.across.values())).astype(BF16)
+            for d, x in self.near_along.items()
         }
-
-    def direct(self):
-        for h in range(len(self.own)):
-            self.send_across(h)
-            self.send_along(h)
-
-    def far(self):
-        self.send_far_along()
-        self.send_far_across()
-
-
-class Pieces:
-    def __init__(self, gather):
-        ndp, nc, dp, ctx = plane_blocks()
-        found = []
-        for h in range(len(gather.own)):
-            found.append((0, 0, h, gather.own[h]))
-            found += [(0, s, h, x) for s, x in gather.across[h].items()]
-            found += [(d, 0, h, x) for d, x in gather.along[h].items()]
-        found += [(*k, 0, x) for k, x in gather.far_top.items()]
-        found += [(*k, 1, x) for k, x in gather.far_bottom.items()]
-        self.half, self.columns = gather.half, gather.own[0].shape[1]
-        self.arrays, self.counts, self.keys, self.found, places = [], [], [], {}, []
-        for d, s, h, x in found:
-            plane = lax.rem(dp - d + ndp, ndp) * nc + lax.rem(ctx - s + nc, nc)
-            n = x.shape[0] // self.half
-            self.arrays.append(x)
-            self.counts.append(n)
-            for i in range(n):
-                self.keys.append((d, s, h + i))
-                self.found[d, s, h + i] = (len(self.arrays) - 1, i * self.half)
-                places.append(2 * plane + h + i)
-        self.places = jnp.stack(places).astype(jnp.int32)
-
-
-class Scatter:
-    def __init__(self, halves_of):
-        self.halves_of = halves_of
-
-    def terms(self, keys, dtype):
-        ndp, nc, dp, ctx = plane_blocks()
-        numbers = [
-            2 * (lax.rem(dp + d, ndp) * nc + lax.rem(ctx + s, nc)) + h for d, s, h in keys
-        ]
-        return dict(zip(keys, self.halves_of(numbers, dtype)))
-
-    def far(self):
+        return across, along
+
+    def finish(self, last):
         ndp, nc, _, _ = plane_blocks()
-        pairs = [(d, s) for d in range(1, ndp) for s in range(1, nc)]
-        terms = self.terms([(*k, h) for k in pairs for h in range(2)], BF16)
-        return (
-            {k: shift(terms[*k, 0], "context", k[1]) for k in pairs},
-            {k: shift(terms[*k, 1], "dp", k[0]) for k in pairs},
+        across, along = last
+        top, bottom = self.own[: self.half], self.own[self.half :]
+        for x in self.across.values():
+            top = top + self.row(x, ndp - 1)
+        for x in along.values():
+            top = top + x.astype(F32)
+        for x in self.along.values():
+            bottom = bottom + self.row(x, nc - 1)
+        for x in across.values():
+            bottom = bottom + x.astype(F32)
+        return jnp.concatenate([top, bottom], 0)
+
+
+def join_last(scatters):
+    sums = [scatter.sums() for scatter in scatters]
+    return (
+        {s: jnp.concatenate([x[0][s] for x in sums], 0) for s in sums[0][0]},
+        {d: jnp.concatenate([x[1][d] for x in sums], 0) for d in sums[0][1]},
+    )
+
+
+def send_last(scatters, blocks=None):
+    to_across, to_along = join_last(scatters) if blocks is None else blocks
+    across = by_context(lambda s: to_across[s])
+    along = by_dp(lambda d: to_along[d])
+    split, start = [], 0
+    for scatter in scatters:
+        rows = slice(start, start + scatter.half)
+        split.append(
+            ({s: x[rows] for s, x in across.items()}, {d: x[rows] for d, x in along.items()})
         )
-
-    def free(self):
-        ndp, nc, _, _ = plane_blocks()
-        keys = [(0, s, 0) for s in range(1, nc)] + [(d, 0, 1) for d in range(1, ndp)]
-        terms = self.terms(keys, BF16)
-        return (
-            [shift(terms[0, s, 0], "context", s) for s in range(1, nc)],
-            [shift(terms[d, 0, 1], "dp", d) for d in range(1, ndp)],
-        )
-
-    def last(self, far):
-        ndp, nc, _, _ = plane_blocks()
-        keys = [(d, 0, 0) for d in range(1, ndp)] + [(0, s, 1) for s in range(1, nc)]
-        terms = self.terms(keys + [(0, 0, 0), (0, 0, 1)], F32)
-        self.own = [terms[0, 0, h] for h in range(2)]
-        along, across = [], []
-        for d in range(1, ndp):
-            total = terms[d, 0, 0]
-            for s in range(1, nc):
-                total = total + far[0][d, s].astype(F32)
-            along.append(shift(total.astype(BF16), "dp", d))
-        for s in range(1, nc):
-            total = terms[0, s, 1]
-            for d in range(1, ndp):
-                total = total + far[1][d, s].astype(F32)
-            across.append(shift(total.astype(BF16), "context", s))
-        return along, across
-
-    def finish(self, free, last):
-        out = []
-        for h, pieces in enumerate((free[0] + last[0], free[1] + last[1])):
-            total = self.own[h]
-            for piece in pieces:
-                total = total + piece.astype(F32)
-            out.append(total)
-        return jnp.concatenate(out, 0)
+        start += scatter.half
+    return split
 
 
 def doubling_steps(axis):
@@ -189,8 +205,8 @@
     return x
 
 
-def small_scatter(x):
-    for axis in ("dp", "context", "expert"):
+def small_scatter(x, axes):
+    for axis in axes:
         place = lax.axis_index(axis)
         for step, pairs in reversed(list(doubling_steps(axis))):
             half = x.shape[0] // 2
@@ -198,7 +214,7 @@
             low_part, high_part = x[:half], x[half:]
             other = lax.ppermute(jnp.where(high, low_part, high_part), axis, pairs)
             x = jnp.where(high, high_part, low_part) + other
-    return x[0]
+    return x
 
 
 def core_exchange(x, group):
@@ -214,6 +230,7 @@
 
 
 LANES = 128
+SCALE = 2
 MIB = 1 << 20
 
 
@@ -224,54 +241,62 @@
 
 
 def cost(flops, nbytes):
-    return pl.CostEstimate(flops=flops, bytes_accessed=nbytes, transcendentals=0)
-
-
-def assemble(places, full, refs, counts, half):
-    i = 0
-    for ref, n in zip(refs, counts):
-        for k in range(n):
-            start = pl.multiple_of(places[i] * half, half)
-            full[pl.ds(start, half), :] = ref[k * half : (k + 1) * half, :]
-            i += 1
-
-
-def weight_grad_kernel(n, half, numbers, *refs):
+    return pl.CostEstimate(
+        flops=flops // SCALE, bytes_accessed=nbytes // SCALE, transcendentals=0
+    )
+
+
+def assemble(places, full, refs, half):
+    for i, ref in enumerate(refs):
+        full[pl.ds(pl.multiple_of(places[i] * half, half), half), :] = ref[...]
+
+
+def weight_grad_kernel(counts, half, numbers, *refs):
+    n = sum(counts)
     acts, grads, outs, turned = refs[:n], refs[n], refs[n + 1 : -1], refs[-1]
+    spots = [(out, i) for out, c in zip(outs, counts) for i in range(c)]
 
     @pl.when(pl.program_id(0) == 0)
     def _():
         for k in range(n):
             turned[k * half : (k + 1) * half, :] = acts[k][...].T
 
-    total = mat_dot(turned[...], grads[...])
-    for k in range(n):
-        outs[k][...] = total[k * half : (k + 1) * half].astype(outs[k].dtype)
-
-
-def weight_grad(acts, grads, numbers, half, dtype):
+    step = min(n, max(1, 1024 // half))
+    for first in range(0, n, step):
+        some = spots[first : first + step]
+        total = mat_dot(turned[first * half : (first + len(some)) * half, :], grads[...])
+        for i, (out, at) in enumerate(some):
+            out[at * half : (at + 1) * half, :] = total[i * half : (i + 1) * half].astype(
+                out.dtype
+            )
+
+
+def weight_grad(acts, grads, groups, half):
     m, columns = grads.shape
-    n = len(numbers)
+    numbers = [number for some, _ in groups for number in some]
+    counts = tuple(len(some) for some, _ in groups)
     tile = tile_of(m)
 
     def block(k):
         return pl.BlockSpec((m, half), lambda j, p: (0, p[k]))
 
     return pl.pallas_call(
-        functools.partial(weight_grad_kernel, n, half),
-        out_shape=[jax.ShapeDtypeStruct((half, columns), dtype)] * n,
+        functools.partial(weight_grad_kernel, counts, half),
+        out_shape=[
+            jax.ShapeDtypeStruct((len(some) * half, columns), dtype) for some, dtype in groups
+        ],
         grid_spec=pltpu.PrefetchScalarGridSpec(
             num_scalar_prefetch=1,
             grid=(pl.cdiv(columns, tile),),
-            in_specs=[block(k) for k in range(n)]
+            in_specs=[block(k) for k in range(len(numbers))]
             + [pl.BlockSpec((m, tile), lambda j, p: (0, j))],
-            out_specs=[pl.BlockSpec((half, tile), lambda j, p: (0, j))] * n,
-            scratch_shapes=[pltpu.VMEM((n * half, m), BF16)],
+            out_specs=[pl.BlockSpec((c * half, tile), lambda j, p: (0, j)) for c in counts],
+            scratch_shapes=[pltpu.VMEM((len(numbers) * half, m), BF16)],
         ),
-        compiler_params=params(48),
-        cost_estimate=cost(2 * m * n * half * columns, 12 * MIB),
+        compiler_params=params(52),
+        cost_estimate=cost(2 * m * len(numbers) * half * columns, 12 * MIB),
         name="weight_grad",
-    )(jnp.stack(numbers).astype(jnp.int32), *[acts] * n, grads)
+    )(jnp.stack(numbers).astype(jnp.int32), *[acts] * len(numbers), grads)
 
 
 def chunk(m):
@@ -282,9 +307,9 @@
     return 768 if m <= 1024 else 256
 
 
-def hidden_grad_kernel(counts, half, places, acts, *refs):
+def hidden_grad_kernel(half, places, acts, *refs):
     out, full = refs[-2], refs[-1]
-    assemble(places, full, refs[:-2], counts, half)
+    assemble(places, full, refs[:-2], half)
     step = chunk(acts.shape[0])
 
     @pl.loop(0, acts.shape[0] // step)
@@ -298,13 +323,16 @@
     tile_size = tile_of(m)
     tiles = pl.cdiv(pieces.columns, tile_size)
     return pl.pallas_call(
-        functools.partial(hidden_grad_kernel, pieces.counts, pieces.half),
+        functools.partial(hidden_grad_kernel, pieces.half),
         out_shape=jax.ShapeDtypeStruct((m, pieces.columns), F32),
         grid_spec=pltpu.PrefetchScalarGridSpec(
             num_scalar_prefetch=1,
             grid=(tiles,),
             in_specs=[pl.BlockSpec((m, width), lambda j, p: (0, 0))]
-            + [pl.BlockSpec((a.shape[0], tile_size), lambda j, p: (0, j)) for a in pieces.arrays],
+            + [
+                pl.BlockSpec((pieces.half, tile_size), lambda j, p, r=r: (r, j))
+                for _, r in pieces.parts
+            ],
             out_specs=pl.BlockSpec((m, tile_size), lambda j, p: (0, j)),
             scratch_shapes=[pltpu.VMEM((width, tile_size), BF16)],
         ),
@@ -321,11 +349,9 @@
     return total
 
 
-def ffn_kernel(g_counts, u_counts, half, tile, fe, count, columns, *refs):
-    g_places, u_places, here, acts, router, kept, gh = refs[:7]
-    refs, n = refs[7:], len(g_counts)
-    gates, refs = refs[:n], refs[n:]
-    ups, refs = refs[: len(u_counts)], refs[len(u_counts) :]
+def ffn_kernel(n, half, tile, fe, count, columns, *refs):
+    places, here, acts, router, kept, gh = refs[:6]
+    gates, ups, refs = refs[6 : 6 + n], refs[6 + n : 6 + 2 * n], refs[6 + 2 * n :]
     scaled, gate_out, up_out, small = refs[:4]
     prob, share, switch, sum_e, sum_s, gate_full, up_full = refs[4:]
     step = chunk(acts.shape[0])
@@ -357,8 +383,8 @@
     column = j * tile + lax.broadcasted_iota(jnp.int32, (1, tile), 1)
     routed = column < fe
     shared = (column >= fe) & (column < columns)
-    assemble(g_places, gate_full, gates, g_counts, half)
-    assemble(u_places, up_full, ups, u_counts, half)
+    assemble(places, gate_full, gates, half)
+    assemble(places, up_full, ups, half)
 
     @pl.loop(0, chunks)
     def _(c):
@@ -398,20 +424,20 @@
     columns = gates.columns
     tile_size = tile_of(m)
     tiles = pl.cdiv(columns, tile_size)
-    whole = lambda j, g, u, h: (0, 0)
-    tile = pl.BlockSpec((m, tile_size), lambda j, g, u, h: (0, j))
+    whole = lambda j, p, h: (0, 0)
+    tile = pl.BlockSpec((m, tile_size), lambda j, p, h: (0, j))
     weights = [
-        pl.BlockSpec((a.shape[0], tile_size), lambda j, g, u, h: (0, j))
-        for a in gates.arrays + ups.arrays
+        pl.BlockSpec((gates.half, tile_size), lambda j, p, h, r=r: (r, j))
+        for _, r in gates.parts + ups.parts
     ]
     hid = jax.ShapeDtypeStruct((m, columns), BF16)
     return pl.pallas_call(
         functools.partial(
-            ffn_kernel, gates.counts, ups.counts, gates.half, tile_size, fe, count, columns
+            ffn_kernel, len(gates.parts), gates.half, tile_size, fe, count, columns
         ),
         out_shape=(hid, hid, hid, jax.ShapeDtypeStruct((m, LANES), BF16)),
         grid_spec=pltpu.PrefetchScalarGridSpec(
-            num_scalar_prefetch=3,
+            num_scalar_prefetch=2,
             grid=(tiles,),
             in_specs=[
                 pl.BlockSpec((m, width), whole),
@@ -434,28 +460,21 @@
         compiler_params=params(52),
         cost_estimate=cost(4 * m * width * columns, 40 * MIB),
         name="ffn",
-    )(gates.places, ups.places, here, acts, router, kept, gh, *gates.arrays, *ups.arrays)
-
-
-def spread_kernel(arrays, half, extra, *refs):
-    pairs = len(arrays)
-    places, refs = refs[0], refs[1:]
+    )(gates.places, here, acts, router, kept, gh, *gates.arrays, *ups.arrays)
+
+
+def spread_kernel(n, pairs, extra, places, *refs):
     i = pl.program_id(0)
     acts, refs = refs[:pairs], refs[pairs:]
-    weights = []
-    for found in arrays:
-        n = max(array for array, _ in found) + 1
-        weights.append(refs[:n])
-        refs = refs[n:]
+    weights, refs = [refs[k * n : (k + 1) * n] for k in range(pairs)], refs[pairs * n :]
     out, held = refs[-1 - pairs], refs[-pairs:]
     step = min(out.shape[0], 1024)
-    for k in range(len(arrays[0])):
+    for k in range(n):
 
         @pl.when(i == k)
         def _(k=k):
             for pair in range(pairs):
-                array, row = arrays[pair][k]
-                held[pair][...] = weights[pair][array][row : row + half, :]
+                held[pair][...] = weights[pair][k][...]
 
     @pl.loop(0, out.shape[0] // step)
     def _(c):
@@ -468,25 +487,27 @@
         out[rows, :] = total.astype(BF16)
 
 
-def spread(pairs, extra=None):
+def spread(pairs, extra=None, weight=1):
     acts = [a for a, _ in pairs]
     first = pairs[0][1]
-    half, steps = first.half, sum(first.counts)
+    half, steps = first.half, len(first.parts)
     m = acts[0].shape[0]
     width = steps * half
     whole = lambda i, p: (0, 0)
     specs = [pl.BlockSpec(a.shape, whole) for a in acts]
-    operands, arrays = list(acts), []
+    operands = list(acts)
     for _, pieces in pairs:
-        specs += [pl.BlockSpec(a.shape, whole) for a in pieces.arrays]
+        specs += [
+            pl.BlockSpec((half, pieces.columns), lambda i, p, r=r: (r, 0))
+            for _, r in pieces.parts
+        ]
         operands += pieces.arrays
-        arrays.append(tuple(pieces.found[k] for k in first.keys))
     if extra is not None:
         specs.append(pl.BlockSpec(extra[0].shape, whole))
         specs.append(pl.BlockSpec((half, LANES), lambda i, p: (p[i], 0)))
         operands += list(extra)
     return pl.pallas_call(
-        functools.partial(spread_kernel, tuple(arrays), half, extra is not None),
+        functools.partial(spread_kernel, steps, len(pairs), extra is not None),
         out_shape=jax.ShapeDtypeStruct((m, width), BF16),
         grid_spec=pltpu.PrefetchScalarGridSpec(
             num_scalar_prefetch=1,
@@ -496,7 +517,7 @@
             scratch_shapes=[pltpu.VMEM((half, first.columns), BF16)] * len(pairs),
         ),
         compiler_params=params(60),
-        cost_estimate=cost(2 * m * width * first.columns * len(pairs), 20 * MIB),
+        cost_estimate=cost(2 * weight * m * width * first.columns * len(pairs), 20 * MIB),
         name="spread",
     )(first.places, *operands)
 
@@ -505,16 +526,15 @@
     return pltpu.roll(x, HD // 2, 1)
 
 
-def qkv_kernel(counts, half, wide, places, tok, gain, bias, cosine, sine, *refs):
-    normed, query, key_value, inverse, full = refs[-5:]
+def qkv_kernel(half, wide, places, tok, gain, bias, cosine, sine, *refs):
+    normed, query, key_value, full = refs[-4:]
 
     @pl.when(pl.program_id(0) == 0)
     def _():
-        assemble(places, full, refs[:-5], counts, half)
+        assemble(places, full, refs[:-4], half)
 
     values = tok[...].astype(F32)
     inv = lax.rsqrt(jnp.mean(values * values, -1, keepdims=True) + EPSILON)
-    inverse[...] = inv
     normed[...] = (values * inv * gain[...]).astype(BF16)
     out = mat_dot(normed[...], full[...]) + bias[...]
     for h in range(2 * wide // HD):
@@ -533,12 +553,11 @@
     row = lambda i, p: (i, 0)
     whole = lambda i, p: (0, 0)
     return pl.pallas_call(
-        functools.partial(qkv_kernel, pieces.counts, pieces.half, wide),
+        functools.partial(qkv_kernel, pieces.half, wide),
         out_shape=(
             jax.ShapeDtypeStruct((m, width), BF16),
             jax.ShapeDtypeStruct((m, wide), BF16),
             jax.ShapeDtypeStruct((m, 2 * wide), BF16),
-            jax.ShapeDtypeStruct((m, 1), F32),
         ),
         grid_spec=pltpu.PrefetchScalarGridSpec(
             num_scalar_prefetch=1,
@@ -550,12 +569,14 @@
                 pl.BlockSpec((step, HD), row),
                 pl.BlockSpec((step, HD), row),
             ]
-            + [pl.BlockSpec(a.shape, whole) for a in pieces.arrays],
+            + [
+                pl.BlockSpec((pieces.half, 3 * wide), lambda i, p, r=r: (r, 0))
+                for _, r in pieces.parts
+            ],
             out_specs=[
                 pl.BlockSpec((step, width), row),
                 pl.BlockSpec((step, wide), row),
                 pl.BlockSpec((step, 2 * wide), row),
-                pl.BlockSpec((step, 1), row),
             ],
             scratch_shapes=[pltpu.VMEM((width, 3 * wide), BF16)],
         ),
@@ -798,7 +819,9 @@
             )
         ]
     )
-    small_plane = small_gather(small[None], ("context", "dp"))
+
+    weights, _ = tie((expert_up, shared_up, expert_down, shared_down), qkv_out)
+    expert_up, shared_up, expert_down, shared_down = weights
 
     def stacked(routed, shared):
         none = jnp.zeros((routed.shape[0], pad), BF16)
@@ -811,44 +834,30 @@
     def rows_half(x, h):
         return x[h * block // 2 : (h + 1) * block // 2]
 
-    gate = Gather(stacked(expert_gate[0], shared_gate))
-    up = Gather(
-        *[stacked(rows_half(expert_up[0], h), rows_half(shared_up, h)) for h in range(2)]
-    )
-    down = Gather(*[turned(expert_down[0], shared_down, h) for h in range(2)])
-    out_w = Gather(w_out)
-    out_w.direct()
-    gate.direct()
+    hb = block // 2
+    gate_own = stacked(expert_gate[0], shared_gate)
+    d_top, d_low = [turned(expert_down[0], shared_down, h) for h in range(2)]
+    u_top, u_low = [stacked(rows_half(expert_up[0], h), rows_half(shared_up, h)) for h in range(2)]
+    pair_own = jnp.concatenate([d_top, d_low, u_top, u_low], 0)
+    wo_across, wo_along, wo_far = gather_plain(w_out)
+    gate_across, gate_along, gate_far = gather_plain(gate_own)
+    small, pair_own = tie(small, pair_own)
+    small_plane = small_gather(small[None], ("context", "dp"))
     qkv_own = qkv_rows.reshape(count * rows_flat, 3 * wide)
-    qkv_own, (gate.across, gate.along, up.own, down.own, small_plane) = tie(
-        qkv_own, (gate.across, gate.along, up.own, down.own, small_plane)
-    )
+    qkv_own, _ = tie(qkv_own, (gate_across, gate_along, pair_own))
+    small_plane, _ = tie(small_plane, qkv_own)
     all_grads = lax.all_gather(
         tie(cotangent[0], qkv_own)[0], "expert", axis=0, tiled=True
     )
-    qkv_w = Gather(qkv_own)
-    qkv_w.direct()
+    _, _, qkv_far = gather_plain(qkv_own)
     small_all = small_gather(small_plane.reshape(1, -1), ("expert",))
     small_all = small_all.reshape(count, ndp * nc, -1).transpose(1, 0, 2)
     small_all = small_all.reshape(ndp * nc * count, -1)
-    qkv_w.far()
-    qkv_pieces = Pieces(qkv_w)
-    (out_w.across, out_w.along, gate.across, gate.along, down.own), _ = tie(
-        (out_w.across, out_w.along, gate.across, gate.along, down.own),
-        (qkv_w.far_top, qkv_w.far_bottom),
-    )
-    out_w.far()
-    gate.far()
-    down.send_along(0)
-    wo_pieces = Pieces(out_w)
-    wo_planes = jnp.zeros((2 * planes, rows_flat // 2, width), BF16)
-    for key, number in zip(wo_pieces.keys, list(wo_pieces.places)):
-        array, row = wo_pieces.found[key]
-        array = wo_pieces.arrays[array][row : row + rows_flat // 2]
-        wo_planes = lax.dynamic_update_slice_in_dim(wo_planes, array[None], number, 0)
-    wo_mine = core_exchange(wo_planes.reshape(part, heads, rows_flat, width), part)
-    w_o = wo_mine.transpose(1, 0, 2, 3).reshape(wide, width)
-
+    qkv_found, qkv_sent = qkv_far()
+    qkv_pieces = Pieces(qkv_found, qkv_own.shape[0] // 2)
+    wo_found, _ = wo_far(qkv_sent)
+    gate_found, gate_sent = gate_far(qkv_sent)
+    gate_pieces = Pieces(gate_found, hb)
     columns = {}
     place = 0
     for name in ("bq", "bk", "bv", "na", "nf", "sw"):
@@ -906,39 +915,54 @@
         return lax.dynamic_index_in_dim(row, run, 1, keepdims=False).reshape(-1)
 
     bias = jnp.concatenate([own_heads(columns[k]) for k in ("bq", "bk", "bv")])
-    normed, queries, key_value, inverse = qkv_project(
+    normed, queries, key_value = qkv_project(
         all_tokens, gain_attn[None], bias[None], cosine, sine_table, qkv_pieces, wide
     )
     kvs = [key_value] + [
         lax.ppermute(key_value, "context", [(i, i + s) for i in range(nc - s)])
         for s in range(1, nc)
     ]
-    kvs, (gate.far_top, gate.far_bottom, down.along, down.own, all_grads) = tie(
-        kvs, (gate.far_top, gate.far_bottom, down.along, down.own, all_grads)
-    )
-    down.send_across(0)
-    down.send_along(1)
-    down.send_across(1)
-    up.send_along(0)
+    wo_arrays, _ = tie({k: array for k, (array, _) in wo_found.items()}, key_value)
+    wo_found = {k: (wo_arrays[k], row) for k, (_, row) in wo_found.items()}
+    wo_pieces = Pieces(wo_found, rows_flat // 2)
+    wo_planes = jnp.zeros((2 * planes, rows_flat // 2, width), BF16)
+    for (array, row), number in zip(wo_pieces.parts, list(wo_pieces.places)):
+        array = array[row * rows_flat // 2 : (row + 1) * rows_flat // 2]
+        wo_planes = lax.dynamic_update_slice_in_dim(wo_planes, array[None], number, 0)
+    wo_mine = core_exchange(wo_planes.reshape(part, heads, rows_flat, width), part)
+    w_o = wo_mine.transpose(1, 0, 2, 3).reshape(wide, width)
+
+    kvs, (pair_own, _) = tie(kvs, (pair_own, (gate_sent, all_grads)))
+    x_one, y_one = by_context(lambda s: pair_own), by_dp(lambda d: pair_own)
     mixed, attn_part = attend(queries, kvs, allowed, w_o)
     attn_out = lax.psum_scatter(attn_part, "expert", scatter_dimension=0, tiled=True)
-    attn_out, (down.across, down.along, up.along, up.own) = tie(
-        attn_out, (down.across, down.along, up.along, up.own)
-    )
-    up.send_across(0)
-    up.send_along(1)
-    down.send_far_along()
-    up.send_across(1)
+    attn_out, _ = tie(attn_out, (x_one, y_one))
+    x_two = by_context(
+        lambda s: jnp.concatenate([y[hb : 2 * hb] for y in y_one.values()], 0)
+    )
+    y_two = by_dp(lambda d: jnp.concatenate([x[:hb] for x in x_one.values()], 0))
     residual = token_rows.astype(F32) + attn_out.astype(F32)
     unit_two, scale_two = rms_unit(residual)
     rows = lax.all_gather(
         (unit_two * gain_ffn).astype(BF16), "expert", axis=0, tiled=True
     )
-    rows, (up.across, up.along, down.far_top) = tie(
-        rows, (up.across, up.along, down.far_top)
-    )
-    down.send_far_across()
-    up.far()
+    rows, _ = tie(rows, (x_two, y_two))
+    x_far = [y[3 * hb :] for y in y_one.values()]
+    y_far = [x[2 * hb : 3 * hb] for x in x_one.values()]
+    x_three = by_context(lambda s: jnp.concatenate(x_far, 0))
+    y_three = by_dp(lambda d: jnp.concatenate(y_far, 0))
+    down_found = {(0, 0, h): (pair_own, h) for h in range(2)}
+    up_found = {(0, 0, h): (pair_own, 2 + h) for h in range(2)}
+    for s, x in x_one.items():
+        down_found.update({(0, s, h): (x, h) for h in range(2)})
+        up_found.update({(0, s, h): (x, 2 + h) for h in range(2)})
+    for d, y in y_one.items():
+        down_found.update({(d, 0, h): (y, h) for h in range(2)})
+        up_found.update({(d, 0, h): (y, 2 + h) for h in range(2)})
+        for s in x_one:
+            down_found.update({(d, s, 0): (y_two[d], s - 1), (d, s, 1): (x_two[s], d - 1)})
+            up_found.update({(d, s, 0): (y_three[d], s - 1), (d, s, 1): (x_three[s], d - 1)})
+    down_pieces, up_pieces = Pieces(down_found, hb), Pieces(up_found, hb)
 
     (ids, order), _ = tie((ids, order), key_value)
     hit = jnp.any(ids == here, -1)
@@ -950,7 +974,6 @@
         jnp.where(order[:, None, :] == local_index[None, :, None], kept[:, None, :], 0.0), -1
     ).reshape(all_rows)
 
-    gate_pieces, up_pieces, down_pieces = Pieces(gate), Pieces(up), Pieces(down)
     gh = hidden_grad(all_grads, down_pieces)
     scaled, grad_gate, grad_up, grad_small = ffn(
         rows,
@@ -963,23 +986,25 @@
         fe_width,
         count,
     )
-    def halves_of(acts, grads):
-        return lambda numbers, dtype: weight_grad(acts, grads, numbers, block // 2, dtype)
-
-    down_sum = Scatter(halves_of(all_grads, scaled))
-    gate_sum = Scatter(halves_of(rows, grad_gate))
-    up_sum = Scatter(halves_of(rows, grad_up))
-    down_far, down_free = down_sum.far(), down_sum.free()
+    def scatter_of(acts, grads):
+        return Scatter(lambda groups: weight_grad(acts, grads, groups, hb), hb)
+
+    down_sum = scatter_of(all_grads, scaled)
+    gate_sum = scatter_of(rows, grad_gate)
+    down_sum.make(last=False)
+    down_sent = down_sum.send_first()
     grad_rows = spread([(grad_gate, gate_pieces), (grad_up, up_pieces)], (grad_small, router_switch))
-    grad_rows, down_far = tie(grad_rows, down_far)
+    grad_rows, _ = tie(grad_rows, down_sent)
     grad_normed_two = lax.psum_scatter(
         grad_rows, "expert", scatter_dimension=0, tiled=True
     ).astype(F32)
-    down_last = down_sum.last(down_far)
-    grad_normed_two, (down_free, down_last) = tie(
-        grad_normed_two, (down_free, down_last)
-    )
-    gate_free, gate_far = gate_sum.free(), gate_sum.far()
+    gate_sum.make(last=False)
+    gate_sent = gate_sum.send_first()
+    terms = [down_sum.make(first=False), gate_sum.make(first=False)]
+    up_sum = scatter_of(rows, grad_up)
+    terms.append(up_sum.make())
+    grad_normed_two, _ = tie(grad_normed_two, (gate_sent, terms))
+    up_sent = up_sum.send_first()
     grad_router_switch = left_dot(rows, grad_small)
 
     grad_unit = grad_normed_two * gain_ffn
@@ -989,44 +1014,74 @@
     grad_gain_ffn = jnp.sum(grad_normed_two * unit_two, 0)
     attn_own = grad_residual.astype(BF16)
     grad_attn = lax.all_gather(attn_own, "expert", axis=0, tiled=True)
-    output = lax.psum_scatter(
-        spread([(tie(scaled, attn_own)[0], down_pieces)]),
-        "expert",
-        scatter_dimension=0,
-        tiled=True,
-    )
-    grad_attn, (gate_free, gate_far) = tie(grad_attn, (gate_free, gate_far))
-    gate_last = gate_sum.last(gate_far)
-    up_free = up_sum.free()
+    grad_attn, _ = tie(grad_attn, up_sent)
     grad_query, grad_own, *grad_far = attend_back(
         queries, kvs, allowed, w_o, grad_attn, cosine, sine_table
     )
-    grad_far, (up_free, gate_last, down_last) = tie(
-        grad_far, (up_free, gate_last, down_last)
-    )
-    grad_down_w = down_sum.finish(down_free, down_last)
+    (mixed, scaled), _ = tie((mixed, scaled), grad_query)
+    out_part = spread([(scaled, down_pieces)], weight=4)
+    three = [down_sum, gate_sum, up_sum]
+    blocks = join_last(three)
+    grad_own, _ = tie(grad_own, (out_part, blocks))
+    output = lax.psum_scatter(out_part, "expert", scatter_dimension=0, tiled=True)
+    grad_wo = left_dot(mixed, grad_attn).astype(BF16).reshape(heads, part, rows_flat, width)
+    wo_back = core_exchange(grad_wo.transpose(1, 0, 2, 3), part)
+    wo_back = wo_back.reshape(2 * planes, rows_flat // 2, width)
     grad_far = [
         lax.ppermute(piece, "context", [(i + s, i) for i in range(nc - s)])
         for s, piece in enumerate(grad_far, 1)
     ]
-    up_far = up_sum.far()
     grad_qkv, bias_sums = join(grad_query, grad_own, grad_far, cosine, sine_table)
-    grad_qkv, (output, gate_last, mixed) = tie(grad_qkv, (output, gate_last, mixed))
-    grad_gate_w = gate_sum.finish(gate_free, gate_last)
+    grad_qkv, wo_back = tie(grad_qkv, wo_back)
     out_tokens = (residual + output.astype(F32)).astype(BF16)
+    def to_heads(row):
+        full = jnp.zeros((part, heads, runs, HD), F32)
+        full = lax.dynamic_update_slice(
+            full, row.reshape(1, heads, 1, HD), (member, 0, run, 0)
+        )
+        return full.reshape(planes * count, rows_flat)
+
+    bias_sums = bias_sums[0]
+    small_grads = jnp.concatenate(
+        [to_heads(bias_sums[i * wide : (i + 1) * wide]) for i in range(3)]
+        + [
+            grad_gain_ffn.reshape(-1, rows_flat),
+            grad_router_switch[:, count].reshape(-1, rows_flat),
+            grad_router_switch[:, :count].reshape(planes * count, rows_flat * count),
+        ],
+        1,
+    )
+
+    wo_sum = Scatter(
+        lambda groups: [
+            jnp.concatenate(
+                [lax.dynamic_index_in_dim(wo_back, i, 0, keepdims=False) for i in some], 0
+            ).astype(dtype)
+            for some, dtype in groups
+        ],
+        rows_flat // 2,
+    )
+    wo_sum.make()
+    qkv_sum = scatter_of(normed, grad_qkv)
+    lasts = send_last(three, tie(blocks, grad_far)[0])
+    down_last, gate_last, up_last = lasts
+    qkv_sum.make()
+    qkv_sent = qkv_sum.send_first(lasts)
+    wo_sum.send_first(lasts)
+    small_sum = small_scatter(tie(small_grads, lasts)[0], ("dp", "context"))
+    (wo_last,) = send_last([wo_sum])
+    (qkv_last,) = send_last([qkv_sum])
     grad_normed = spread([(grad_qkv, qkv_pieces)])
     grad_normed_own = lax.psum_scatter(
         grad_normed, "expert", scatter_dimension=0, tiled=True
     ).astype(F32)
-
-    qkv_sum = Scatter(halves_of(normed, grad_qkv))
-    qkv_far, qkv_free = qkv_sum.far(), qkv_sum.free()
-    qkv_far, up_far = tie(qkv_far, up_far)
-    qkv_last = qkv_sum.last(qkv_far)
-    qkv_last, up_far = tie(qkv_last, up_far)
-    up_last = up_sum.last(up_far)
-    qkv_grad_rows = qkv_sum.finish(qkv_free, qkv_last)
-    grad_up_w = up_sum.finish(up_free, up_last)
+    grad_normed_own, _ = tie(grad_normed_own, (qkv_last, up_last))
+
+    qkv_grad_rows = qkv_sum.finish(qkv_last)
+    grad_gate_w = gate_sum.finish(gate_last)
+    grad_down_w = down_sum.finish(down_last)
+    grad_w_out = wo_sum.finish(wo_last)
+    grad_up_w = up_sum.finish(up_last)
     qkv_back = lax.all_to_all(
         qkv_grad_rows.astype(BF16).reshape(count, rows_flat, 3 * wide),
         "expert",
@@ -1040,41 +1095,16 @@
         w = w.reshape(runs, part, rows_flat, heads, HD).transpose(2, 1, 3, 0, 4)
         return w.reshape(rows_flat, width)
 
-    grad_wo = left_dot(mixed, grad_attn).astype(BF16).reshape(heads, part, rows_flat, width)
-    wo_back = core_exchange(grad_wo.transpose(1, 0, 2, 3), part)
-    wo_back = wo_back.reshape(2 * planes, rows_flat // 2, width)
-    wo_sum = Scatter(
-        lambda numbers, dtype: [
-            lax.dynamic_index_in_dim(wo_back, i, 0, keepdims=False).astype(dtype)
-            for i in numbers
-        ]
-    )
-    grad_w_out = wo_sum.finish(wo_sum.free(), wo_sum.last(wo_sum.far()))
-
-    def to_heads(row):
-        full = jnp.zeros((part, heads, runs, HD), F32)
-        full = lax.dynamic_update_slice(
-            full, row.reshape(1, heads, 1, HD), (member, 0, run, 0)
-        )
-        return full.reshape(planes * count, rows_flat)
-
-    bias_sums = bias_sums[0]
-    grad_gain_attn = jnp.sum(
-        grad_normed.astype(F32) * (all_tokens.astype(F32) * inverse), 0
-    )
-    small_grads = jnp.concatenate(
-        [to_heads(bias_sums[i * wide : (i + 1) * wide]) for i in range(3)]
-        + [
-            grad_gain_attn.reshape(-1, rows_flat),
-            grad_gain_ffn.reshape(-1, rows_flat),
-            grad_router_switch[:, count].reshape(-1, rows_flat),
-            grad_router_switch[:, :count].reshape(planes * count, rows_flat * count),
-        ],
-        1,
-    )
-    small_sum = small_scatter(small_grads)
-    pieces = [small_sum[i * rows_flat : (i + 1) * rows_flat] for i in range(6)]
-    grad_router = small_sum[6 * rows_flat :].reshape(rows_flat, count)
+    small_sum, _ = tie(small_sum, (qkv_last, up_last))
+    small_sum = small_scatter(small_sum, ("expert",))[0]
+    pieces = [small_sum[i * rows_flat : (i + 1) * rows_flat] for i in range(5)]
+    grad_router = small_sum[5 * rows_flat :].reshape(rows_flat, count)
+
+    w_grads = [from_heads(i) for i in range(3)]
+    grad_gain_attn = sum(
+        jnp.sum(w.astype(F32) * grad, 1)
+        for w, grad in zip((w_query, w_key, w_value), w_grads)
+    ) / norm_attn.astype(F32)
 
     unit_one, scale_one = rms_unit(token_rows.astype(F32))
     grad_unit = grad_normed_own * gain_attn
@@ -1084,20 +1114,18 @@
     return (
         out_tokens[None],
         grad_tokens.astype(BF16)[None],
-        from_heads(0),
-        from_heads(1),
-        from_heads(2),
+        *w_grads,
         grad_w_out,
         pieces[0],
         pieces[1],
         pieces[2],
+        grad_gain_attn,
         pieces[3],
-        pieces[4],
         grad_router,
         grad_gate_w[:, fe_width : fe_width + fs_width],
         grad_up_w[:, fe_width : fe_width + fs_width],
         grad_down_w[:, fe_width : fe_width + fs_width].T,
-        pieces[5],
+        pieces[4],
         grad_gate_w[None, :, :fe_width],
         grad_up_w[None, :, :fe_width],
         grad_down_w[:, :fe_width].T[None],

time: 827 us -> 789 us (0.954)
  waiting for transfers between devices: 267 us -> 291 us
  starting transfers between devices: 93.4 us -> 70.1 us
  Pallas kernels: 233 us -> 214 us
    ppermute x54 -> x34, waiting for transfers between devices: 193 us -> 245 us  [shift(): return lax.ppermute(x, axis, [(i, (i + step) % n) for i in range(n)])]
    ppermute x5, waiting for transfers between devices: 37.6 us -> 10.9 us  [small_gather(): other = lax.ppermute(x, axis, pairs)]
    reduce_scatter x1, waiting for transfers between devices: 22 us -> 0.01 us  [body(): lax.psum_scatter(grad_rows, 'expert', scatter_dimension=0, tiled=True)]
    pallas_call x18 -> x12, Pallas kernels: 206 us -> 187 us  [the longest x6 66.9 us: weight_grad(): pl.pallas_call(functools.partial(weight_grad_kernel, counts, half), out_s...]
    ppermute x1, waiting for transfers between devices: 0.01 us -> 18.5 us  [body(): lax.ppermute(key_value, 'context', [(i, i + s) for i in range(nc - s)])]
    ppermute x54 -> x34, starting transfers between devices: 60.9 us -> 45.9 us  [shift(): return lax.ppermute(x, axis, [(i, (i + step) % n) for i in range(n)])]
    concatenate x3 -> x7, other arithmetic: 2.72 us -> 12.5 us  [the longest x1 5.4 us: body(): pair_own = jnp.concatenate([d_top, d_low, u_top, u_low], 0)]
    ppermute x5, waiting for transfers between devices: 2.6 us -> 11.1 us  [small_scatter(): other = lax.ppermute(jnp.where(high, low_part, high_part), axis, pairs)]
  transfers between devices with their start and end apart: 78 -> 58, of which waited for: 34 -> 25; matrix products, arithmetic and copies ran while one was open for 20% -> 18% of each run, Pallas kernels for 22% -> 17%
where the time goes in v2:
time: 789 us; the launch traced here: 781 us
  waiting for transfers between devices  291 us (37%)
  Pallas kernels  214 us (27%)
  local copies, waits for them, and re-layouts  114 us (14%)
  other arithmetic  70.6 us (9%)
  starting transfers between devices  70.1 us (9%)
  between operations  16.1 us (2%)
    ppermute x34, waiting for transfers between devices, shift(): return lax.ppermute(x, axis, [(i, (i + step) % n) for i in range(n)])  245 us
    pallas_call x6, Pallas kernels, weight_grad(): pl.pallas_call(functools.partial(weight_grad_kernel, counts, half), out_s...  66.9 us
    pallas_call x3, Pallas kernels, spread(): pl.pallas_call(functools.partial(spread_kernel, steps, len(pairs), extra...  62.7 us
    unnamed x178, local copies, waits for them, and re-layouts  47.2 us
    ppermute x34, starting transfers between devices, shift(): return lax.ppermute(x, axis, [(i, (i + step) % n) for i in range(n)])  45.9 us
    pallas_call x1, Pallas kernels, ffn(): pl.pallas_call(functools.partial(ffn_kernel, len(gates.parts), gates.half...  35.7 us
    ppermute x1, waiting for transfers between devices, body(): lax.ppermute(key_value, 'context', [(i, i + s) for i in range(nc - s)])  18.5 us
    pallas_call x1, Pallas kernels, hidden_grad(): pl.pallas_call(functools.partial(hidden_grad_kernel, pieces.half), out_sh...  16.1 us
  transfers between devices with their start and end apart: 58, of which 25 were waited for; matrix products, arithmetic and copies ran while one was open for 18% of the time, Pallas kernels for 17%

profile of v2, /device:TPU:0, one launch (start us, length us, event | category | flops | bytes accessed | tf_op | source)
XLA Modules:
  0.0 781.0 jit_solution(5797390483183490326)
XLA Ops:
  20.6 4.9 all-to-all-start
  54.2 5.4 pad_maximum_fusion.refs_0_.refs_1_.refs_14_.refs_15_.refs_10_.refs_11_.refs_2_
  73.1 6.0 collective-permute-done.5
  93.0 7.2 collective-permute-done.7.refs_2_.refs_3_.refs_4_
  105.1 4.6 collective-permute-done.9.refs_6_.refs_7_
  119.6 6.1 qkv_project.1
  134.4 6.4 collective-permute-done.17.refs_13_.refs_9_
  140.8 18.5 %collective-permute-done.16.refs_1_ = bf16[1024,512]{1,0:T(8,128)(2,1)S(1)} collective-permute-done((bf16[1024,512]{1,0:T(8,128)(2,1)S(1)}, bf16[1024,512]{1,0:T(8,128)(2,1)S(1)}, u32[]{:S(2)}, u32[]{:S(2)}) %collective-permute-start.16) | collective-permute-done | bytes 1048608 | tf_op jit(solution)/shard_map/ppermute | solution.py:922
  163.8 8.8 %attend.1 = (bf16[1024,256]{1,0:T(8,128)(2,1)S(1)}, bf16[1024,2048]{1,0:T(8,128)(2,1)S(1)}) custom-call(bf16[1024,256]{1,0:T(8,128)(2,1)S(1)} %copy-done.18, f32[8,128,256]{2,1,0:T(8,128)S(1)} %add_convert_fusion.7.allowed, bf16[256,2048]{1,0:T(8,128)(2,1)S(1)} %bitcast.188, bf16[1024,512]{1,0:T(8,128)(2,1)S(1)} %copy-done.11, bf16[1024,512]{1,0:T(8,128)(2,1)S(1)} %copy-done.14), custom_call_target="tpu_custom_call" | custom-call | flops 671088640 | bytes 4194304 | tf_op jit(solution)/shard_map/attend/pallas_call | solution.py:615
  179.8 91.1 %collective-permute-done.19.refs_2_.refs_3_.refs_16_.refs_17_.refs_12_.refs_13_.refs_4_ = bf16[1024,2176]{1,0:T(8,128)(2,1)} collective-permute-done((bf16[1024,2176]{1,0:T(8,128)(2,1)}, bf16[1024,2176]{1,0:T(8,128)(2,1)}, u32[]{:S(2)}, u32[]{:S(2)}) %collective-permute-start.19) | collective-permute-done | bytes 4456480 | tf_op jit(solution)/shard_map/ppermute | solution.py:37
  295.9 15.3 %collective-permute-done.21.refs_7_.refs_8_ = bf16[256,2176]{1,0:T(8,128)(2,1)} collective-permute-done((bf16[256,2176]{1,0:T(8,128)(2,1)}, bf16[256,2176]{1,0:T(8,128)(2,1)}, u32[]{:S(2)}, u32[]{:S(2)}) %collective-permute-start.21) | collective-permute-done | bytes 1114144 | tf_op jit(solution)/shard_map/ppermute | solution.py:37
  317.0 16.1 %hidden_grad.1.refs_5_ = f32[1024,2176]{1,0:T(8,128)} custom-call(s32[8]{0:T(128)S(1)} %stack.44.places.refs_0_, bf16[1024,2048]{1,0:T(8,128)(2,1)S(1)} %copy-done, bf16[1024,2176]{1,0:T(8,128)(2,1)} %pad_maximum_fusion.refs_0_.refs_1_.refs_14_.refs_15_.refs_10_.refs_11_.refs_2_, ...), custom_call_target="tpu_custom_call" | custom-call | flops 4563402752 | bytes 10485760 | tf_op jit(solution)/shard_map/hidden_grad/pallas_call | solution.py:325
  335.2 35.7 %ffn.1 = (bf16[1024,2176]{1,0:T(8,128)(2,1)}, bf16[1024,2176]{1,0:T(8,128)(2,1)}, bf16[1024,2176]{1,0:T(8,128)(2,1)}, bf16[1024,128]{1,0:T(8,128)(2,1)S(1)}) custom-call(s32[8]{0:T(128)S(1)} %stack.44.places.refs_0_, s32[1]{0:T(128)} %bitcast.44.refs_1_, ...), custom_call_target="tpu_custom_call" | custom-call | flops 9126805504 | bytes 20971520 | tf_op jit(solution)/shard_map/ffn/pallas_call | solution.py:434
  370.9 9.8 %weight_grad.6 = (bf16[512,2176]{1,0:T(8,128)(2,1)}, bf16[512,2176]{1,0:T(8,128)(2,1)}) custom-call(s32[4]{0:T(128)S(1)} %get-tuple-element.358.numbers, bf16[1024,2048]{1,0:T(8,128)(2,1)} %all-gather.6.cloned.1.call-done.acts.refs_0_.refs_1_.refs_2_.refs_3_, bf16[1024,2048]{1,0:T(8,128)(2,1)} %all-gather.6.cloned.1.call-done.acts.refs_0_.refs_1_.refs_2_.refs_3_, ...), custom_call_target="tpu_custom_call" | custom-call | flops 2281701376 | bytes 6291456 | tf_op jit(solution)/shard_map/weight_grad/pallas_call | solution.py:283
  384.0 34.2 %spread.3 = bf16[1024,2048]{1,0:T(8,128)(2,1)} custom-call(s32[8]{0:T(128)} %copy-done.30, bf16[1024,2176]{1,0:T(8,128)(2,1)} %get-tuple-element.133.refs_0_.refs_4_, bf16[1024,2176]{1,0:T(8,128)(2,1)} %get-tuple-element.134.refs_1_.refs_8_, bf16[512,2176]{1,0:T(8,128)(2,1)} %copy-done.33, bf16[512,2176]{1,0:T(8,128)(2,1)} %copy-done.33, ...), custom_call_target="tpu_custom_call" | custom-call | flops 9126805504 | bytes 10485760 | tf_op jit(solution)/shard_map/spread/pallas_call | solution.py:509
  418.2 7.6 collective-permute-done.25
  426.8 10.1 %weight_grad.7 = (bf16[512,2176]{1,0:T(8,128)(2,1)}, bf16[512,2176]{1,0:T(8,128)(2,1)}) custom-call(s32[4]{0:T(128)S(1)} %get-tuple-element.358.numbers, bf16[1024,2048]{1,0:T(8,128)(2,1)} %all-gather.8.cloned.1.call-done.refs_2_.refs_0_.refs_1_.refs_3_.refs_4_.refs_5_.refs_6_.refs_7_, ...), custom_call_target="tpu_custom_call" | custom-call | flops 2281701376 | bytes 6291456 | tf_op jit(solution)/shard_map/weight_grad/pallas_call | solution.py:283
  439.5 10.8 %weight_grad.9 = (f32[256,2176]{1,0:T(8,128)}, f32[256,2176]{1,0:T(8,128)}, f32[512,2176]{1,0:T(8,128)}) custom-call(s32[4]{0:T(128)S(1)} %get-tuple-element.359.numbers, bf16[1024,2048]{1,0:T(8,128)(2,1)} %all-gather.8.cloned.1.call-done.refs_2_.refs_0_.refs_1_.refs_3_.refs_4_.refs_5_.refs_6_.refs_7_, ...), custom_call_target="tpu_custom_call" | custom-call | flops 2281701376 | bytes 6291456 | tf_op jit(solution)/shard_map/weight_grad/pallas_call | solution.py:283
  450.3 10.9 %weight_grad.8 = (f32[256,2176]{1,0:T(8,128)}, f32[256,2176]{1,0:T(8,128)}, f32[512,2176]{1,0:T(8,128)}) custom-call(s32[4]{0:T(128)S(1)} %get-tuple-element.359.numbers, bf16[1024,2048]{1,0:T(8,128)(2,1)} %all-gather.6.cloned.1.call-done.acts.refs_0_.refs_1_.refs_2_.refs_3_, ...), custom_call_target="tpu_custom_call" | custom-call | flops 2281701376 | bytes 6291456 | tf_op jit(solution)/shard_map/weight_grad/pallas_call | solution.py:283
  461.2 17.1 %weight_grad.10 = (bf16[512,2176]{1,0:T(8,128)(2,1)}, bf16[512,2176]{1,0:T(8,128)(2,1)}, f32[256,2176]{1,0:T(8,128)}, f32[256,2176]{1,0:T(8,128)}, f32[512,2176]{1,0:T(8,128)}) custom-call(s32[8]{0:T(128)S(1)} %stack.53.numbers, bf16[1024,2048]{1,0:T(8,128)(2,1)} %all-gather.8.cloned.1.call-done.refs_2_.refs_0_.refs_1_.refs_3_.refs_4_.refs_5_.refs_6_.refs_7_, ...), custom_call_target="tpu_custom_call" | custom-call | flops 4563402752 | bytes 6291456 | tf_op jit(solution)/shard_map/weight_grad/pallas_call | solution.py:283
  490.4 39.7 %collective-permute-done.30 = bf16[512,2176]{1,0:T(8,128)(2,1)S(1)} collective-permute-done((bf16[512,2176]{1,0:T(8,128)(2,1)}, bf16[512,2176]{1,0:T(8,128)(2,1)S(1)}, u32[]{:S(2)}, u32[]{:S(2)}) %collective-permute-start.30) | collective-permute-done | bytes 2228256 | tf_op jit(solution)/shard_map/ppermute | solution.py:37
  547.1 15.2 %attend_back.1 = (bf16[1024,256]{1,0:T(8,128)(2,1)S(1)}, f32[1024,512]{1,0:T(8,128)S(1)}, bf16[1024,512]{1,0:T(8,128)(2,1)}) custom-call(bf16[1024,256]{1,0:T(8,128)(2,1)S(1)} %copy-done.19, f32[8,128,256]{2,1,0:T(8,128)S(1)} %add_convert_fusion.7.allowed, bf16[256,2048]{1,0:T(8,128)(2,1)S(1)} %bitcast.189, bf16[1024,2048]{1,0:T(8,128)(2,1)S(1)} %copy-done.8, ...), custom_call_target="tpu_custom_call" | custom-call | flops 939524096 | bytes 4194304 | tf_op jit(solution)/shard_map/attend_back/pallas_call | solution.py:674
  566.8 18.8 %spread.4 = bf16[1024,2048]{1,0:T(8,128)(2,1)} custom-call(s32[8]{0:T(128)} %copy-done.30, bf16[1024,2176]{1,0:T(8,128)(2,1)} %get-tuple-element.157.refs_4_.refs_0_, bf16[1024,2176]{1,0:T(8,128)(2,1)} %pad_maximum_fusion.refs_0_.refs_1_.refs_14_.refs_15_.refs_10_.refs_11_.refs_2_, ...), custom_call_target="tpu_custom_call" | custom-call | flops 18253611008 | bytes 10485760 | tf_op jit(solution)/shard_map/spread/pallas_call | solution.py:509
  593.8 9.7 %spread.5 = bf16[1024,2048]{1,0:T(8,128)(2,1)} custom-call(s32[8]{0:T(128)} %copy-done.30, bf16[1024,768]{1,0:T(8,128)(2,1)} %copy-done.5, bf16[512,768]{1,0:T(8,128)(2,1)} %bitcast.186, bf16[512,768]{1,0:T(8,128)(2,1)} %bitcast.187, bf16[512,768]{1,0:T(8,128)(2,1)} %copy-done.3, bf16[512,768]{1,0:T(8,128)(2,1)} %copy-done.3, bf16[512,768]{1,0:T(8,128)(2,1)} %copy-done.4, ...), custom_call_target="tpu_custom_call" | custom-call | flops 1610612736 | bytes 10485760 | tf_op jit(solution)/shard_map/spread/pallas_call | solution.py:509
  603.6 3.7 collective-permute-start.33
  613.3 8.2 %weight_grad.11 = (bf16[512,768]{1,0:T(8,128)(2,1)S(1)}, bf16[512,768]{1,0:T(8,128)(2,1)S(1)}, f32[256,768]{1,0:T(8,128)}, f32[256,768]{1,0:T(8,128)}, f32[512,768]{1,0:T(8,128)}) custom-call(s32[8]{0:T(128)S(1)} %stack.53.numbers, bf16[1024,2048]{1,0:T(8,128)(2,1)} %copy-done.1, bf16[1024,2048]{1,0:T(8,128)(2,1)} %copy-done.1, ...), custom_call_target="tpu_custom_call" | custom-call | flops 1610612736 | bytes 6291456 | tf_op jit(solution)/shard_map/weight_grad/pallas_call | solution.py:283
  623.9 56.7 %collective-permute-done.33 = bf16[768,2176]{1,0:T(8,128)(2,1)} collective-permute-done((bf16[768,2176]{1,0:T(8,128)(2,1)}, bf16[768,2176]{1,0:T(8,128)(2,1)}, u32[]{:S(2)}, u32[]{:S(2)}) %collective-permute-start.33) | collective-permute-done | bytes 3342368 | tf_op jit(solution)/shard_map/ppermute | solution.py:37
  684.5 11.4 %convert_add_fusion.5 = (f32[256,2176]{1,0:T(8,128)S(1)}, f32[256,2176]{1,0:T(8,128)S(1)}, f32[256,2176]{1,0:T(8,128)S(1)}, f32[256,2176]{1,0:T(8,128)S(1)}, f32[256,2176]{1,0:T(8,128)S(1)}, /*index=5*/f32[256,2176]{1,0:T(8,128)}) fusion(f32[512,2176]{1,0:T(8,128)} %get-tuple-element.146, bf16[512,2176]{1,0:T(8,128)(2,1)} %collective-permute-done.27, ...), kind=kLoop, calls=%fused_computation.15 | loop fusion | flops 13369344 | bytes 40108032 | tf_op jit(solution)/shard_map/add | solution.py:160
  727.9 4.0 collective-permute-done.36
  737.8 4.9 all-to-all-start.1
  745.8 10.8 %collective-permute-done.46 = f32[2,832]{1,0:T(2,128)S(1)} collective-permute-done((f32[2,832]{1,0:T(2,128)S(1)}, f32[2,832]{1,0:T(2,128)S(1)}, u32[]{:S(2)}, u32[]{:S(2)}) %collective-permute-start.46) | collective-permute-done | bytes 6688 | tf_op jit(solution)/shard_map/ppermute | solution.py:215
  759.3 4.3 all-to-all-done.1
  (487 shorter events, 251.0 us)
Async XLA Ops:
  7.2 108.2 %all-gather.12.cloned.1.call-start = ((), (), s32[]{:S(2)}) async-start(), calls=%async_computation.13 | async-start | bytes 4718592 | tf_op jit(solution)/shard_map/all_gather | solution.py:803
  12.2 55.7 %collective-permute-start.2 = (bf16[512,2176]{1,0:T(8,128)(2,1)S(1)}, bf16[512,2176]{1,0:T(8,128)(2,1)}, u32[]{:S(2)}, u32[]{:S(2)}) collective-permute-start(bf16[512,2176]{1,0:T(8,128)(2,1)S(1)} %concatenate.97.refs_6_.refs_7_.refs_2_.refs_3_), channel_id=1, source_target_pairs={{0,8},{8,0},{1,9},{9,1},{2,10},{10,2},{3,11},{11,3},{4,12},{12,4},... | collective-permute-start | bytes 6684680 | tf_op jit(solution)/shard_map/ppermute | solution.py:37
  15.2 52.7 %collective-permute-start.3 = (bf16[512,2176]{1,0:T(8,128)(2,1)S(1)}, bf16[512,2176]{1,0:T(8,128)(2,1)}, u32[]{:S(2)}, u32[]{:S(2)}) collective-permute-start(bf16[512,2176]{1,0:T(8,128)(2,1)S(1)} %concatenate.97.refs_6_.refs_7_.refs_2_.refs_3_), channel_id=1, source_target_pairs={{0,16},{16,0},{1,17},{17,1},{2,18},{18,2},{3,19},{19,3},{4,20},{20... | collective-permute-start | bytes 6684680 | tf_op jit(solution)/shard_map/ppermute | solution.py:37
  20.6 47.3 %all-to-all-start = ((bf16[8,64,768]{2,1,0:T(8,128)(2,1)}), bf16[8,64,768]{2,1,0:T(8,128)(2,1)S(1)}, u32[]{:S(2)}, u32[]{:S(2)}) async-start(bf16[8,64,768]{2,1,0:T(8,128)(2,1)} %constant_dynamic-update-slice_fusion), calls=%async_computation | async-start | bytes 1572864 | tf_op jit(solution)/shard_map/all_to_all | solution.py:804
  25.5 134.8 %all-gather.6.cloned.1.call-start = ((), (), s32[]{:S(2)}) async-start(), calls=%async_computation.6 | async-start | bytes 4718592 | tf_op jit(solution)/shard_map/all_gather | solution.py:849
  83.8 189.1 %reduce-scatter.5.cloned.1.call-start = ((), (), s32[]{:S(2)}) async-start(), calls=%async_computation.7 | async-start | bytes 4718592 | tf_op jit(solution)/shard_map/reduce_scatter | solution.py:938
  112.7 28.1 %collective-permute-start.17 = (bf16[256,2176]{1,0:T(8,128)(2,1)}, bf16[256,2176]{1,0:T(8,128)(2,1)}, u32[]{:S(2)}, u32[]{:S(2)}) collective-permute-start(bf16[256,2176]{1,0:T(8,128)(2,1)} %slice.450), channel_id=1, source_target_pairs={{0,8},{8,0},{1,9},{9,1},{2,10},{10,2},{3,11},{11,3},{4,12},{12,4},... | collective-permute-start | bytes 3342344 | tf_op jit(solution)/shard_map/ppermute | solution.py:37
  114.4 26.4 %collective-permute-start.18 = (bf16[256,2176]{1,0:T(8,128)(2,1)}, bf16[256,2176]{1,0:T(8,128)(2,1)}, u32[]{:S(2)}, u32[]{:S(2)}) collective-permute-start(bf16[256,2176]{1,0:T(8,128)(2,1)} %slice.449), channel_id=1, source_target_pairs={{0,16},{16,0},{1,17},{17,1},{2,18},{18,2},{3,19},{19,3},{4,20},{20... | collective-permute-start | bytes 3342344 | tf_op jit(solution)/shard_map/ppermute | solution.py:37
  126.5 32.8 %collective-permute-start.16 = (bf16[1024,512]{1,0:T(8,128)(2,1)S(1)}, bf16[1024,512]{1,0:T(8,128)(2,1)S(1)}, u32[]{:S(2)}, u32[]{:S(2)}) collective-permute-start(bf16[1024,512]{1,0:T(8,128)(2,1)S(1)} %get-tuple-element.123.refs_0_), channel_id=1, source_target_pairs={{0,8},{1,9},{2,10},{3,11},{4,12},{5,13},{6,14},{7,15},{16,24},{17,... | collective-permute-start | bytes 3145736 | tf_op jit(solution)/shard_map/ppermute | solution.py:922
  175.4 157.7 %all-gather.8.cloned.1.call-start = ((), (), s32[]{:S(2)}) async-start(), calls=%async_computation.8 | async-start | bytes 4718592 | tf_op jit(solution)/shard_map/all_gather | solution.py:946
  175.4 95.4 %collective-permute-start.19 = (bf16[1024,2176]{1,0:T(8,128)(2,1)}, bf16[1024,2176]{1,0:T(8,128)(2,1)}, u32[]{:S(2)}, u32[]{:S(2)}) collective-permute-start(bf16[1024,2176]{1,0:T(8,128)(2,1)} %pad_maximum_fusion.refs_0_.refs_1_.refs_14_.refs_15_.refs_10_.refs_11_.refs_2_), channel_id=1, source_target_pairs={{0,8},{8,0},{1,9},{9,1},{2,10},{10,2},{3,11},{11,3},{4,12},{12,4},... | collective-permute-start | bytes 13369352 | tf_op jit(solution)/shard_map/ppermute | solution.py:37
  178.0 94.9 %collective-permute-start.20 = (bf16[1024,2176]{1,0:T(8,128)(2,1)}, bf16[1024,2176]{1,0:T(8,128)(2,1)}, u32[]{:S(2)}, u32[]{:S(2)}) collective-permute-start(bf16[1024,2176]{1,0:T(8,128)(2,1)} %pad_maximum_fusion.refs_0_.refs_1_.refs_14_.refs_15_.refs_10_.refs_11_.refs_2_), channel_id=1, source_target_pairs={{0,16},{16,0},{1,17},{17,1},{2,18},{18,2},{3,19},{19,3},{4,20},{20... | collective-permute-start | bytes 13369352 | tf_op jit(solution)/shard_map/ppermute | solution.py:37
  276.6 201.7 %reduce-scatter.7.cloned.1.call-start = ((), (), s32[]{:S(2)}) async-start(), calls=%async_computation.9 | async-start | bytes 4718592 | tf_op jit(solution)/shard_map/reduce_scatter | solution.py:998
  283.4 27.8 %collective-permute-start.21 = (bf16[256,2176]{1,0:T(8,128)(2,1)}, bf16[256,2176]{1,0:T(8,128)(2,1)}, u32[]{:S(2)}, u32[]{:S(2)}) collective-permute-start(bf16[256,2176]{1,0:T(8,128)(2,1)} %get-tuple-element.294), channel_id=1, source_target_pairs={{0,8},{8,0},{1,9},{9,1},{2,10},{10,2},{3,11},{11,3},{4,12},{12,4},... | collective-permute-start | bytes 3342344 | tf_op jit(solution)/shard_map/ppermute | solution.py:37
  286.9 27.8 %collective-permute-start.22 = (bf16[256,2176]{1,0:T(8,128)(2,1)}, bf16[256,2176]{1,0:T(8,128)(2,1)}, u32[]{:S(2)}, u32[]{:S(2)}) collective-permute-start(bf16[256,2176]{1,0:T(8,128)(2,1)} %get-tuple-element.296), channel_id=1, source_target_pairs={{0,16},{16,0},{1,17},{17,1},{2,18},{18,2},{3,19},{19,3},{4,20},{20... | collective-permute-start | bytes 3342344 | tf_op jit(solution)/shard_map/ppermute | solution.py:37
  289.8 43.3 %collective-permute-start.23 = (bf16[256,2176]{1,0:T(8,128)(2,1)}, bf16[256,2176]{1,0:T(8,128)(2,1)}, u32[]{:S(2)}, u32[]{:S(2)}) collective-permute-start(bf16[256,2176]{1,0:T(8,128)(2,1)} %get-tuple-element.295), channel_id=1, source_target_pairs={{0,16},{16,0},{1,17},{17,1},{2,18},{18,2},{3,19},{19,3},{4,20},{20... | collective-permute-start | bytes 3342344 | tf_op jit(solution)/shard_map/ppermute | solution.py:37
  290.1 43.0 %collective-permute-start.24 = (bf16[256,2176]{1,0:T(8,128)(2,1)}, bf16[256,2176]{1,0:T(8,128)(2,1)}, u32[]{:S(2)}, u32[]{:S(2)}) collective-permute-start(bf16[256,2176]{1,0:T(8,128)(2,1)} %get-tuple-element.293), channel_id=1, source_target_pairs={{0,8},{8,0},{1,9},{9,1},{2,10},{10,2},{3,11},{11,3},{4,12},{12,4},... | collective-permute-start | bytes 3342344 | tf_op jit(solution)/shard_map/ppermute | solution.py:37
  380.7 45.2 %collective-permute-start.25 = (bf16[512,2176]{1,0:T(8,128)(2,1)}, bf16[512,2176]{1,0:T(8,128)(2,1)}, u32[]{:S(2)}, u32[]{:S(2)}) collective-permute-start(bf16[512,2176]{1,0:T(8,128)(2,1)} %get-tuple-element.136), channel_id=1, source_target_pairs={{0,8},{8,0},{1,9},{9,1},{2,10},{10,2},{3,11},{11,3},{4,12},{12,4},... | collective-permute-start | bytes 6684680 | tf_op jit(solution)/shard_map/ppermute | solution.py:37
  382.3 44.3 %collective-permute-start.26 = (bf16[512,2176]{1,0:T(8,128)(2,1)}, bf16[512,2176]{1,0:T(8,128)(2,1)}, u32[]{:S(2)}, u32[]{:S(2)}) collective-permute-start(bf16[512,2176]{1,0:T(8,128)(2,1)} %get-tuple-element.137), channel_id=1, source_target_pairs={{0,16},{16,0},{1,17},{17,1},{2,18},{18,2},{3,19},{19,3},{4,20},{20... | collective-permute-start | bytes 6684680 | tf_op jit(solution)/shard_map/ppermute | solution.py:37
  426.7 114.7 %all-gather.10.cloned.1.call-start = ((), (), s32[]{:S(2)}) async-start(), calls=%async_computation.10 | async-start | bytes 4718592 | tf_op jit(solution)/shard_map/all_gather | solution.py:1016
  436.8 43.4 %collective-permute-start.27 = (bf16[512,2176]{1,0:T(8,128)(2,1)}, bf16[512,2176]{1,0:T(8,128)(2,1)}, u32[]{:S(2)}, u32[]{:S(2)}) collective-permute-start(bf16[512,2176]{1,0:T(8,128)(2,1)} %get-tuple-element.139), channel_id=1, source_target_pairs={{0,8},{8,0},{1,9},{9,1},{2,10},{10,2},{3,11},{11,3},{4,12},{12,4},... | collective-permute-start | bytes 6684680 | tf_op jit(solution)/shard_map/ppermute | solution.py:37
  437.7 43.7 %collective-permute-start.28 = (bf16[512,2176]{1,0:T(8,128)(2,1)}, bf16[512,2176]{1,0:T(8,128)(2,1)}, u32[]{:S(2)}, u32[]{:S(2)}) collective-permute-start(bf16[512,2176]{1,0:T(8,128)(2,1)} %get-tuple-element.140), channel_id=1, source_target_pairs={{0,16},{16,0},{1,17},{17,1},{2,18},{18,2},{3,19},{19,3},{4,20},{20... | collective-permute-start | bytes 6684680 | tf_op jit(solution)/shard_map/ppermute | solution.py:37
  484.4 284.9 %reduce-scatter.11.cloned.1.call-start = ((), (), s32[]{:S(2)}) async-start(), calls=%async_computation.12 | async-start | bytes 4718592 | tf_op jit(solution)/shard_map/reduce_scatter | solution.py:1075
  484.4 45.7 %collective-permute-start.30 = (bf16[512,2176]{1,0:T(8,128)(2,1)}, bf16[512,2176]{1,0:T(8,128)(2,1)S(1)}, u32[]{:S(2)}, u32[]{:S(2)}) collective-permute-start(bf16[512,2176]{1,0:T(8,128)(2,1)} %get-tuple-element.154), channel_id=1, source_target_pairs={{0,16},{16,0},{1,17},{17,1},{2,18},{18,2},{3,19},{19,3},{4,20},{20... | collective-permute-start | bytes 6684680 | tf_op jit(solution)/shard_map/ppermute | solution.py:37
  486.1 51.8 %collective-permute-start.29 = (bf16[512,2176]{1,0:T(8,128)(2,1)}, bf16[512,2176]{1,0:T(8,128)(2,1)S(1)}, u32[]{:S(2)}, u32[]{:S(2)}) collective-permute-start(bf16[512,2176]{1,0:T(8,128)(2,1)} %get-tuple-element.153), channel_id=1, source_target_pairs={{0,8},{8,0},{1,9},{9,1},{2,10},{10,2},{3,11},{11,3},{4,12},{12,4},... | collective-permute-start | bytes 6684680 | tf_op jit(solution)/shard_map/ppermute | solution.py:37
  562.4 27.6 %collective-permute-start.31 = (bf16[1024,512]{1,0:T(8,128)(2,1)}, bf16[1024,512]{1,0:T(8,128)(2,1)}, u32[]{:S(2)}, u32[]{:S(2)}) collective-permute-start(bf16[1024,512]{1,0:T(8,128)(2,1)} %get-tuple-element.160), channel_id=1, source_target_pairs={{8,0},{9,1},{10,2},{11,3},{12,4},{13,5},{14,6},{15,7},{24,16},{25,... | collective-permute-start | bytes 3145736 | tf_op jit(solution)/shard_map/ppermute | solution.py:1031
  603.6 167.2 %reduce-scatter.9.cloned.1.call-start = ((), (), s32[]{:S(2)}) async-start(), calls=%async_computation.11 | async-start | bytes 4718592 | tf_op jit(solution)/shard_map/reduce_scatter | solution.py:1026
  603.6 77.0 %collective-permute-start.33 = (bf16[768,2176]{1,0:T(8,128)(2,1)}, bf16[768,2176]{1,0:T(8,128)(2,1)}, u32[]{:S(2)}, u32[]{:S(2)}) collective-permute-start(bf16[768,2176]{1,0:T(8,128)(2,1)} %pad_maximum_fusion.1), channel_id=1, source_target_pairs={{0,8},{8,0},{1,9},{9,1},{2,10},{10,2},{3,11},{11,3},{4,12},{12,4},... | collective-permute-start | bytes 10027016 | tf_op jit(solution)/shard_map/ppermute | solution.py:37
  607.3 74.8 %collective-permute-start.34 = (bf16[768,2176]{1,0:T(8,128)(2,1)}, bf16[768,2176]{1,0:T(8,128)(2,1)}, u32[]{:S(2)}, u32[]{:S(2)}) collective-permute-start(bf16[768,2176]{1,0:T(8,128)(2,1)} %pad_maximum_fusion.2), channel_id=1, source_target_pairs={{0,16},{16,0},{1,17},{17,1},{2,18},{18,2},{3,19},{19,3},{4,20},{20... | collective-permute-start | bytes 10027016 | tf_op jit(solution)/shard_map/ppermute | solution.py:37
  682.0 38.2 %collective-permute-start.35 = (bf16[512,768]{1,0:T(8,128)(2,1)S(1)}, bf16[512,768]{1,0:T(8,128)(2,1)}, u32[]{:S(2)}, u32[]{:S(2)}) collective-permute-start(bf16[512,768]{1,0:T(8,128)(2,1)S(1)} %get-tuple-element.170), channel_id=1, source_target_pairs={{0,16},{16,0},{1,17},{17,1},{2,18},{18,2},{3,19},{19,3},{4,20},{20... | collective-permute-start | bytes 2359304 | tf_op jit(solution)/shard_map/ppermute | solution.py:37
  683.5 39.7 %collective-permute-start.37 = (bf16[512,768]{1,0:T(8,128)(2,1)S(1)}, bf16[512,768]{1,0:T(8,128)(2,1)}, u32[]{:S(2)}, u32[]{:S(2)}) collective-permute-start(bf16[512,768]{1,0:T(8,128)(2,1)S(1)} %get-tuple-element.172), channel_id=1, source_target_pairs={{0,8},{8,0},{1,9},{9,1},{2,10},{10,2},{3,11},{11,3},{4,12},{12,4},... | collective-permute-start | bytes 2359304 | tf_op jit(solution)/shard_map/ppermute | solution.py:37
  737.8 25.8 %all-to-all-start.1 = ((bf16[8,64,768]{2,1,0:T(8,128)(2,1)}), bf16[8,64,768]{2,1,0:T(8,128)(2,1)S(1)}, u32[]{:S(2)}, u32[]{:S(2)}) async-start(bf16[8,64,768]{2,1,0:T(8,128)(2,1)} %bitcast.64), calls=%async_computation.5 | async-start | bytes 1572864 | tf_op jit(solution)/shard_map/all_to_all | solution.py:1085
  (111 other events, 1130.2 us)
Sparse Core Ops, SparseCore 0:
  16.9 63.3 all-gather.11
  83.9 47.2 all-gather.5
  175.5 52.0 reduce-scatter.4
  276.7 47.0 all-gather.7
  426.8 50.1 reduce-scatter.6
  484.5 46.6 all-gather.9
  603.7 52.7 reduce-scatter.10
  658.8 48.1 reduce-scatter.8

commit v3 on v2

--- a/solution.py
+++ b/solution.py
@@ -1066,11 +1066,11 @@
     lasts = send_last(three, tie(blocks, grad_far)[0])
     down_last, gate_last, up_last = lasts
     qkv_sum.make()
-    qkv_sent = qkv_sum.send_first(lasts)
-    wo_sum.send_first(lasts)
-    small_sum = small_scatter(tie(small_grads, lasts)[0], ("dp", "context"))
+    qkv_sent = qkv_sum.send_first()
+    wo_sum.send_first(qkv_sent)
+    small_sum = small_scatter(tie(small_grads, qkv_sent)[0], ("dp", "context"))
     (wo_last,) = send_last([wo_sum])
-    (qkv_last,) = send_last([qkv_sum])
+    (qkv_last,) = send_last([qkv_sum], tie(join_last([qkv_sum]), lasts)[0])
     grad_normed = spread([(grad_qkv, qkv_pieces)])
     grad_normed_own = lax.psum_scatter(
         grad_normed, "expert", scatter_dimension=0, tiled=True

time: 789 us -> 811 us (1.028)
  waiting for transfers between devices: 291 us -> 308 us
    ppermute x5, waiting for transfers between devices: 11.1 us -> 78.2 us  [small_scatter(): other = lax.ppermute(jnp.where(high, low_part, high_part), axis, pairs)]
    ppermute x34, waiting for transfers between devices: 245 us -> 199 us  [shift(): return lax.ppermute(x, axis, [(i, (i + step) % n) for i in range(n)])]
    unnamed x178 -> x186, local copies, waits for them, and re-layouts: 47.2 us -> 47.5 us
where the time goes in v3:
time: 811 us; the launch traced here: 802 us
  waiting for transfers between devices  308 us (38%)
  Pallas kernels  215 us (27%)
  local copies, waits for them, and re-layouts  119 us (15%)
  starting transfers between devices  71.2 us (9%)
  other arithmetic  67.9 us (8%)
  between operations  16.2 us (2%)
    ppermute x34, waiting for transfers between devices, shift(): return lax.ppermute(x, axis, [(i, (i + step) % n) for i in range(n)])  199 us
    ppermute x5, waiting for transfers between devices, small_scatter(): other = lax.ppermute(jnp.where(high, low_part, high_part), axis, pairs)  78.2 us
    pallas_call x6, Pallas kernels, weight_grad(): pl.pallas_call(functools.partial(weight_grad_kernel, counts, half), out_s...  67.3 us
    pallas_call x3, Pallas kernels, spread(): pl.pallas_call(functools.partial(spread_kernel, steps, len(pairs), extra...  62.8 us
    unnamed x186, local copies, waits for them, and re-layouts  47.5 us
    ppermute x34, starting transfers between devices, shift(): return lax.ppermute(x, axis, [(i, (i + step) % n) for i in range(n)])  43.3 us
    pallas_call x1, Pallas kernels, ffn(): pl.pallas_call(functools.partial(ffn_kernel, len(gates.parts), gates.half...  35.6 us
    ppermute x1, waiting for transfers between devices, body(): lax.ppermute(key_value, 'context', [(i, i + s) for i in range(nc - s)])  18.5 us
  transfers between devices with their start and end apart: 58, of which 25 were waited for; matrix products, arithmetic and copies ran while one was open for 18% of the time, Pallas kernels for 17%

profile of v3, /device:TPU:0, one launch (start us, length us, event | category | flops | bytes accessed | tf_op | source)
XLA Modules:
  0.0 801.9 jit_solution(10618759503345730568)
XLA Ops:
  8.7 3.5 concatenate.97.refs_6_.refs_7_.refs_2_.refs_3_
  20.6 4.9 all-to-all-start
  54.2 5.4 pad_maximum_fusion.refs_0_.refs_1_.refs_14_.refs_15_.refs_10_.refs_11_.refs_2_
  73.1 6.0 collective-permute-done.5
  93.0 7.2 collective-permute-done.7.refs_2_.refs_3_.refs_4_
  105.1 4.6 collective-permute-done.9.refs_6_.refs_7_
  119.6 6.1 qkv_project.1
  134.4 6.5 collective-permute-done.17.refs_13_.refs_9_
  140.8 18.5 %collective-permute-done.16.refs_1_ = bf16[1024,512]{1,0:T(8,128)(2,1)S(1)} collective-permute-done((bf16[1024,512]{1,0:T(8,128)(2,1)S(1)}, bf16[1024,512]{1,0:T(8,128)(2,1)S(1)}, u32[]{:S(2)}, u32[]{:S(2)}) %collective-permute-start.16) | collective-permute-done | bytes 1048608 | tf_op jit(solution)/shard_map/ppermute | solution.py:922
  163.8 8.8 %attend.1 = (bf16[1024,256]{1,0:T(8,128)(2,1)S(1)}, bf16[1024,2048]{1,0:T(8,128)(2,1)S(1)}) custom-call(bf16[1024,256]{1,0:T(8,128)(2,1)S(1)} %copy-done.18, f32[8,128,256]{2,1,0:T(8,128)S(1)} %add_convert_fusion.7.allowed, bf16[256,2048]{1,0:T(8,128)(2,1)S(1)} %bitcast.188, bf16[1024,512]{1,0:T(8,128)(2,1)S(1)} %copy-done.11, bf16[1024,512]{1,0:T(8,128)(2,1)S(1)} %copy-done.14), custom_call_target="tpu_custom_call" | custom-call | flops 671088640 | bytes 4194304 | tf_op jit(solution)/shard_map/attend/pallas_call | solution.py:615
  179.8 91.1 %collective-permute-done.19.refs_2_.refs_3_.refs_16_.refs_17_.refs_12_.refs_13_.refs_4_ = bf16[1024,2176]{1,0:T(8,128)(2,1)} collective-permute-done((bf16[1024,2176]{1,0:T(8,128)(2,1)}, bf16[1024,2176]{1,0:T(8,128)(2,1)}, u32[]{:S(2)}, u32[]{:S(2)}) %collective-permute-start.19) | collective-permute-done | bytes 4456480 | tf_op jit(solution)/shard_map/ppermute | solution.py:37
  295.9 15.3 %collective-permute-done.21.refs_7_.refs_8_ = bf16[256,2176]{1,0:T(8,128)(2,1)} collective-permute-done((bf16[256,2176]{1,0:T(8,128)(2,1)}, bf16[256,2176]{1,0:T(8,128)(2,1)}, u32[]{:S(2)}, u32[]{:S(2)}) %collective-permute-start.21) | collective-permute-done | bytes 1114144 | tf_op jit(solution)/shard_map/ppermute | solution.py:37
  311.2 3.6 collective-permute-done.22.refs_6_.refs_7_
  317.0 16.0 %hidden_grad.1.refs_5_ = f32[1024,2176]{1,0:T(8,128)} custom-call(s32[8]{0:T(128)S(1)} %stack.44.places.refs_0_, bf16[1024,2048]{1,0:T(8,128)(2,1)S(1)} %copy-done, bf16[1024,2176]{1,0:T(8,128)(2,1)} %pad_maximum_fusion.refs_0_.refs_1_.refs_14_.refs_15_.refs_10_.refs_11_.refs_2_, ...), custom_call_target="tpu_custom_call" | custom-call | flops 4563402752 | bytes 10485760 | tf_op jit(solution)/shard_map/hidden_grad/pallas_call | solution.py:325
  335.1 35.6 %ffn.1 = (bf16[1024,2176]{1,0:T(8,128)(2,1)}, bf16[1024,2176]{1,0:T(8,128)(2,1)}, bf16[1024,2176]{1,0:T(8,128)(2,1)}, bf16[1024,128]{1,0:T(8,128)(2,1)S(1)}) custom-call(s32[8]{0:T(128)S(1)} %stack.44.places.refs_0_, s32[1]{0:T(128)} %bitcast.44.refs_1_, ...), custom_call_target="tpu_custom_call" | custom-call | flops 9126805504 | bytes 20971520 | tf_op jit(solution)/shard_map/ffn/pallas_call | solution.py:434
  370.8 9.8 %weight_grad.6 = (bf16[512,2176]{1,0:T(8,128)(2,1)}, bf16[512,2176]{1,0:T(8,128)(2,1)}) custom-call(s32[4]{0:T(128)S(1)} %get-tuple-element.356.numbers, bf16[1024,2048]{1,0:T(8,128)(2,1)} %all-gather.6.cloned.1.call-done.acts.refs_0_.refs_1_.refs_2_.refs_3_, bf16[1024,2048]{1,0:T(8,128)(2,1)} %all-gather.6.cloned.1.call-done.acts.refs_0_.refs_1_.refs_2_.refs_3_, ...), custom_call_target="tpu_custom_call" | custom-call | flops 2281701376 | bytes 6291456 | tf_op jit(solution)/shard_map/weight_grad/pallas_call | solution.py:283
  383.9 34.3 %spread.3 = bf16[1024,2048]{1,0:T(8,128)(2,1)} custom-call(s32[8]{0:T(128)} %copy-done.30, bf16[1024,2176]{1,0:T(8,128)(2,1)} %get-tuple-element.135.refs_0_.refs_4_, bf16[1024,2176]{1,0:T(8,128)(2,1)} %get-tuple-element.136.refs_1_.refs_8_, bf16[512,2176]{1,0:T(8,128)(2,1)} %copy-done.33, bf16[512,2176]{1,0:T(8,128)(2,1)} %copy-done.33, ...), custom_call_target="tpu_custom_call" | custom-call | flops 9126805504 | bytes 10485760 | tf_op jit(solution)/shard_map/spread/pallas_call | solution.py:509
  418.3 7.5 collective-permute-done.25
  426.7 10.1 %weight_grad.7 = (bf16[512,2176]{1,0:T(8,128)(2,1)}, bf16[512,2176]{1,0:T(8,128)(2,1)}) custom-call(s32[4]{0:T(128)S(1)} %get-tuple-element.356.numbers, bf16[1024,2048]{1,0:T(8,128)(2,1)} %all-gather.8.cloned.1.call-done.refs_2_.refs_0_.refs_1_.refs_3_.refs_4_.refs_5_.refs_6_.refs_7_, ...), custom_call_target="tpu_custom_call" | custom-call | flops 2281701376 | bytes 6291456 | tf_op jit(solution)/shard_map/weight_grad/pallas_call | solution.py:283
  439.4 10.8 %weight_grad.9 = (f32[256,2176]{1,0:T(8,128)}, f32[256,2176]{1,0:T(8,128)}, f32[512,2176]{1,0:T(8,128)}) custom-call(s32[4]{0:T(128)S(1)} %get-tuple-element.357.numbers, bf16[1024,2048]{1,0:T(8,128)(2,1)} %all-gather.8.cloned.1.call-done.refs_2_.refs_0_.refs_1_.refs_3_.refs_4_.refs_5_.refs_6_.refs_7_, ...), custom_call_target="tpu_custom_call" | custom-call | flops 2281701376 | bytes 6291456 | tf_op jit(solution)/shard_map/weight_grad/pallas_call | solution.py:283
  450.2 10.9 %weight_grad.8 = (f32[256,2176]{1,0:T(8,128)}, f32[256,2176]{1,0:T(8,128)}, f32[512,2176]{1,0:T(8,128)}) custom-call(s32[4]{0:T(128)S(1)} %get-tuple-element.357.numbers, bf16[1024,2048]{1,0:T(8,128)(2,1)} %all-gather.6.cloned.1.call-done.acts.refs_0_.refs_1_.refs_2_.refs_3_, ...), custom_call_target="tpu_custom_call" | custom-call | flops 2281701376 | bytes 6291456 | tf_op jit(solution)/shard_map/weight_grad/pallas_call | solution.py:283
  461.1 17.1 %weight_grad.10 = (bf16[512,2176]{1,0:T(8,128)(2,1)}, bf16[512,2176]{1,0:T(8,128)(2,1)}, f32[256,2176]{1,0:T(8,128)}, f32[256,2176]{1,0:T(8,128)}, f32[512,2176]{1,0:T(8,128)}) custom-call(s32[8]{0:T(128)S(1)} %stack.53.numbers, bf16[1024,2048]{1,0:T(8,128)(2,1)} %all-gather.8.cloned.1.call-done.refs_2_.refs_0_.refs_1_.refs_3_.refs_4_.refs_5_.refs_6_.refs_7_, ...), custom_call_target="tpu_custom_call" | custom-call | flops 4563402752 | bytes 6291456 | tf_op jit(solution)/shard_map/weight_grad/pallas_call | solution.py:283
  490.4 39.6 %collective-permute-done.30 = bf16[512,2176]{1,0:T(8,128)(2,1)S(1)} collective-permute-done((bf16[512,2176]{1,0:T(8,128)(2,1)}, bf16[512,2176]{1,0:T(8,128)(2,1)S(1)}, u32[]{:S(2)}, u32[]{:S(2)}) %collective-permute-start.30) | collective-permute-done | bytes 2228256 | tf_op jit(solution)/shard_map/ppermute | solution.py:37
  547.1 15.2 %attend_back.1 = (bf16[1024,256]{1,0:T(8,128)(2,1)S(1)}, f32[1024,512]{1,0:T(8,128)S(1)}, bf16[1024,512]{1,0:T(8,128)(2,1)}) custom-call(bf16[1024,256]{1,0:T(8,128)(2,1)S(1)} %copy-done.19, f32[8,128,256]{2,1,0:T(8,128)S(1)} %add_convert_fusion.7.allowed, bf16[256,2048]{1,0:T(8,128)(2,1)S(1)} %bitcast.189, bf16[1024,2048]{1,0:T(8,128)(2,1)S(1)} %copy-done.8, ...), custom_call_target="tpu_custom_call" | custom-call | flops 939524096 | bytes 4194304 | tf_op jit(solution)/shard_map/attend_back/pallas_call | solution.py:674
  566.7 18.8 %spread.4 = bf16[1024,2048]{1,0:T(8,128)(2,1)} custom-call(s32[8]{0:T(128)} %copy-done.30, bf16[1024,2176]{1,0:T(8,128)(2,1)} %get-tuple-element.159.refs_4_.refs_0_, bf16[1024,2176]{1,0:T(8,128)(2,1)} %pad_maximum_fusion.refs_0_.refs_1_.refs_14_.refs_15_.refs_10_.refs_11_.refs_2_, ...), custom_call_target="tpu_custom_call" | custom-call | flops 18253611008 | bytes 10485760 | tf_op jit(solution)/shard_map/spread/pallas_call | solution.py:509
  593.7 9.7 %spread.5 = bf16[1024,2048]{1,0:T(8,128)(2,1)} custom-call(s32[8]{0:T(128)} %copy-done.30, bf16[1024,768]{1,0:T(8,128)(2,1)} %copy-done.5, bf16[512,768]{1,0:T(8,128)(2,1)} %bitcast.186, bf16[512,768]{1,0:T(8,128)(2,1)} %bitcast.187, bf16[512,768]{1,0:T(8,128)(2,1)} %copy-done.3, bf16[512,768]{1,0:T(8,128)(2,1)} %copy-done.3, bf16[512,768]{1,0:T(8,128)(2,1)} %copy-done.4, ...), custom_call_target="tpu_custom_call" | custom-call | flops 1610612736 | bytes 10485760 | tf_op jit(solution)/shard_map/spread/pallas_call | solution.py:509
  610.8 8.6 %weight_grad.11 = (bf16[512,768]{1,0:T(8,128)(2,1)S(1)}, bf16[512,768]{1,0:T(8,128)(2,1)S(1)}, f32[256,768]{1,0:T(8,128)}, f32[256,768]{1,0:T(8,128)}, f32[512,768]{1,0:T(8,128)}) custom-call(s32[8]{0:T(128)S(1)} %stack.53.numbers, bf16[1024,2048]{1,0:T(8,128)(2,1)} %copy-done.1, bf16[1024,2048]{1,0:T(8,128)(2,1)} %copy-done.1, ...), custom_call_target="tpu_custom_call" | custom-call | flops 1610612736 | bytes 6291456 | tf_op jit(solution)/shard_map/weight_grad/pallas_call | solution.py:283
  628.1 11.7 %collective-permute-done.33 = bf16[512,768]{1,0:T(8,128)(2,1)} collective-permute-done((bf16[512,768]{1,0:T(8,128)(2,1)S(1)}, bf16[512,768]{1,0:T(8,128)(2,1)}, u32[]{:S(2)}, u32[]{:S(2)}) %collective-permute-start.33) | collective-permute-done | bytes 786464 | tf_op jit(solution)/shard_map/ppermute | solution.py:37
  649.0 68.7 %collective-permute-done.43 = f32[16,832]{1,0:T(8,128)S(1)} collective-permute-done((f32[16,832]{1,0:T(8,128)S(1)}, f32[16,832]{1,0:T(8,128)S(1)}, u32[]{:S(2)}, u32[]{:S(2)}) %collective-permute-start.43) | collective-permute-done | bytes 53280 | tf_op jit(solution)/shard_map/ppermute | solution.py:215
  729.5 9.8 %convert_add_fusion.5 = (f32[256,2176]{1,0:T(8,128)S(1)}, f32[256,2176]{1,0:T(8,128)S(1)}, f32[256,2176]{1,0:T(8,128)S(1)}, f32[256,2176]{1,0:T(8,128)S(1)}, f32...) fusion(f32[512,2176]{1,0:T(8,128)} %get-tuple-element.148, bf16[512,2176]{1,0:T(8,128)(2,1)} %collective-permute-done.27, ...), kind=kLoop, calls=%fused_computation.15 | loop fusion | flops 13369344 | bytes 40108032 | tf_op jit(solution)/shard_map/add | solution.py:160
  752.4 4.2 all-to-all-start.1
  761.2 9.3 %collective-permute-done.46 = f32[2,832]{1,0:T(2,128)S(1)} collective-permute-done((f32[2,832]{1,0:T(2,128)S(1)}, f32[2,832]{1,0:T(2,128)S(1)}, u32[]{:S(2)}, u32[]{:S(2)}) %collective-permute-start.46) | collective-permute-done | bytes 6688 | tf_op jit(solution)/shard_map/ppermute | solution.py:215
  (495 shorter events, 256.5 us)
Async XLA Ops:
  7.2 108.2 %all-gather.12.cloned.1.call-start = ((), (), s32[]{:S(2)}) async-start(), calls=%async_computation.13 | async-start | bytes 4718592 | tf_op jit(solution)/shard_map/all_gather | solution.py:803
  12.2 55.7 %collective-permute-start.2 = (bf16[512,2176]{1,0:T(8,128)(2,1)S(1)}, bf16[512,2176]{1,0:T(8,128)(2,1)}, u32[]{:S(2)}, u32[]{:S(2)}) collective-permute-start(bf16[512,2176]{1,0:T(8,128)(2,1)S(1)} %concatenate.97.refs_6_.refs_7_.refs_2_.refs_3_), channel_id=1, source_target_pairs={{0,8},{8,0},{1,9},{9,1},{2,10},{10,2},{3,11},{11,3},{4,12},{12,4},... | collective-permute-start | bytes 6684680 | tf_op jit(solution)/shard_map/ppermute | solution.py:37
  15.2 52.7 %collective-permute-start.3 = (bf16[512,2176]{1,0:T(8,128)(2,1)S(1)}, bf16[512,2176]{1,0:T(8,128)(2,1)}, u32[]{:S(2)}, u32[]{:S(2)}) collective-permute-start(bf16[512,2176]{1,0:T(8,128)(2,1)S(1)} %concatenate.97.refs_6_.refs_7_.refs_2_.refs_3_), channel_id=1, source_target_pairs={{0,16},{16,0},{1,17},{17,1},{2,18},{18,2},{3,19},{19,3},{4,20},{20... | collective-permute-start | bytes 6684680 | tf_op jit(solution)/shard_map/ppermute | solution.py:37
  20.6 47.3 %all-to-all-start = ((bf16[8,64,768]{2,1,0:T(8,128)(2,1)}), bf16[8,64,768]{2,1,0:T(8,128)(2,1)S(1)}, u32[]{:S(2)}, u32[]{:S(2)}) async-start(bf16[8,64,768]{2,1,0:T(8,128)(2,1)} %constant_dynamic-update-slice_fusion), calls=%async_computation | async-start | bytes 1572864 | tf_op jit(solution)/shard_map/all_to_all | solution.py:804
  25.5 134.8 %all-gather.6.cloned.1.call-start = ((), (), s32[]{:S(2)}) async-start(), calls=%async_computation.6 | async-start | bytes 4718592 | tf_op jit(solution)/shard_map/all_gather | solution.py:849
  83.7 189.2 %reduce-scatter.5.cloned.1.call-start = ((), (), s32[]{:S(2)}) async-start(), calls=%async_computation.7 | async-start | bytes 4718592 | tf_op jit(solution)/shard_map/reduce_scatter | solution.py:938
  112.7 28.1 %collective-permute-start.17 = (bf16[256,2176]{1,0:T(8,128)(2,1)}, bf16[256,2176]{1,0:T(8,128)(2,1)}, u32[]{:S(2)}, u32[]{:S(2)}) collective-permute-start(bf16[256,2176]{1,0:T(8,128)(2,1)} %slice.450), channel_id=1, source_target_pairs={{0,8},{8,0},{1,9},{9,1},{2,10},{10,2},{3,11},{11,3},{4,12},{12,4},... | collective-permute-start | bytes 3342344 | tf_op jit(solution)/shard_map/ppermute | solution.py:37
  126.5 32.8 %collective-permute-start.16 = (bf16[1024,512]{1,0:T(8,128)(2,1)S(1)}, bf16[1024,512]{1,0:T(8,128)(2,1)S(1)}, u32[]{:S(2)}, u32[]{:S(2)}) collective-permute-start(bf16[1024,512]{1,0:T(8,128)(2,1)S(1)} %get-tuple-element.125.refs_0_), channel_id=1, source_target_pairs={{0,8},{1,9},{2,10},{3,11},{4,12},{5,13},{6,14},{7,15},{16,24},{17,... | collective-permute-start | bytes 3145736 | tf_op jit(solution)/shard_map/ppermute | solution.py:922
  175.4 157.6 %all-gather.8.cloned.1.call-start = ((), (), s32[]{:S(2)}) async-start(), calls=%async_computation.8 | async-start | bytes 4718592 | tf_op jit(solution)/shard_map/all_gather | solution.py:946
  175.4 95.4 %collective-permute-start.19 = (bf16[1024,2176]{1,0:T(8,128)(2,1)}, bf16[1024,2176]{1,0:T(8,128)(2,1)}, u32[]{:S(2)}, u32[]{:S(2)}) collective-permute-start(bf16[1024,2176]{1,0:T(8,128)(2,1)} %pad_maximum_fusion.refs_0_.refs_1_.refs_14_.refs_15_.refs_10_.refs_11_.refs_2_), channel_id=1, source_target_pairs={{0,8},{8,0},{1,9},{9,1},{2,10},{10,2},{3,11},{11,3},{4,12},{12,4},... | collective-permute-start | bytes 13369352 | tf_op jit(solution)/shard_map/ppermute | solution.py:37
  178.0 94.9 %collective-permute-start.20 = (bf16[1024,2176]{1,0:T(8,128)(2,1)}, bf16[1024,2176]{1,0:T(8,128)(2,1)}, u32[]{:S(2)}, u32[]{:S(2)}) collective-permute-start(bf16[1024,2176]{1,0:T(8,128)(2,1)} %pad_maximum_fusion.refs_0_.refs_1_.refs_14_.refs_15_.refs_10_.refs_11_.refs_2_), channel_id=1, source_target_pairs={{0,16},{16,0},{1,17},{17,1},{2,18},{18,2},{3,19},{19,3},{4,20},{20... | collective-permute-start | bytes 13369352 | tf_op jit(solution)/shard_map/ppermute | solution.py:37
  276.6 201.6 %reduce-scatter.7.cloned.1.call-start = ((), (), s32[]{:S(2)}) async-start(), calls=%async_computation.9 | async-start | bytes 4718592 | tf_op jit(solution)/shard_map/reduce_scatter | solution.py:998
  283.3 27.8 %collective-permute-start.21 = (bf16[256,2176]{1,0:T(8,128)(2,1)}, bf16[256,2176]{1,0:T(8,128)(2,1)}, u32[]{:S(2)}, u32[]{:S(2)}) collective-permute-start(bf16[256,2176]{1,0:T(8,128)(2,1)} %get-tuple-element.298), channel_id=1, source_target_pairs={{0,8},{8,0},{1,9},{9,1},{2,10},{10,2},{3,11},{11,3},{4,12},{12,4},... | collective-permute-start | bytes 3342344 | tf_op jit(solution)/shard_map/ppermute | solution.py:37
  286.9 27.8 %collective-permute-start.22 = (bf16[256,2176]{1,0:T(8,128)(2,1)}, bf16[256,2176]{1,0:T(8,128)(2,1)}, u32[]{:S(2)}, u32[]{:S(2)}) collective-permute-start(bf16[256,2176]{1,0:T(8,128)(2,1)} %get-tuple-element.300), channel_id=1, source_target_pairs={{0,16},{16,0},{1,17},{17,1},{2,18},{18,2},{3,19},{19,3},{4,20},{20... | collective-permute-start | bytes 3342344 | tf_op jit(solution)/shard_map/ppermute | solution.py:37
  289.8 43.3 %collective-permute-start.23 = (bf16[256,2176]{1,0:T(8,128)(2,1)}, bf16[256,2176]{1,0:T(8,128)(2,1)}, u32[]{:S(2)}, u32[]{:S(2)}) collective-permute-start(bf16[256,2176]{1,0:T(8,128)(2,1)} %get-tuple-element.299), channel_id=1, source_target_pairs={{0,16},{16,0},{1,17},{17,1},{2,18},{18,2},{3,19},{19,3},{4,20},{20... | collective-permute-start | bytes 3342344 | tf_op jit(solution)/shard_map/ppermute | solution.py:37
  290.1 43.0 %collective-permute-start.24 = (bf16[256,2176]{1,0:T(8,128)(2,1)}, bf16[256,2176]{1,0:T(8,128)(2,1)}, u32[]{:S(2)}, u32[]{:S(2)}) collective-permute-start(bf16[256,2176]{1,0:T(8,128)(2,1)} %get-tuple-element.297), channel_id=1, source_target_pairs={{0,8},{8,0},{1,9},{9,1},{2,10},{10,2},{3,11},{11,3},{4,12},{12,4},... | collective-permute-start | bytes 3342344 | tf_op jit(solution)/shard_map/ppermute | solution.py:37
  380.6 45.2 %collective-permute-start.25 = (bf16[512,2176]{1,0:T(8,128)(2,1)}, bf16[512,2176]{1,0:T(8,128)(2,1)}, u32[]{:S(2)}, u32[]{:S(2)}) collective-permute-start(bf16[512,2176]{1,0:T(8,128)(2,1)} %get-tuple-element.138), channel_id=1, source_target_pairs={{0,8},{8,0},{1,9},{9,1},{2,10},{10,2},{3,11},{11,3},{4,12},{12,4},... | collective-permute-start | bytes 6684680 | tf_op jit(solution)/shard_map/ppermute | solution.py:37
  382.2 44.4 %collective-permute-start.26 = (bf16[512,2176]{1,0:T(8,128)(2,1)}, bf16[512,2176]{1,0:T(8,128)(2,1)}, u32[]{:S(2)}, u32[]{:S(2)}) collective-permute-start(bf16[512,2176]{1,0:T(8,128)(2,1)} %get-tuple-element.139), channel_id=1, source_target_pairs={{0,16},{16,0},{1,17},{17,1},{2,18},{18,2},{3,19},{19,3},{4,20},{20... | collective-permute-start | bytes 6684680 | tf_op jit(solution)/shard_map/ppermute | solution.py:37
  426.6 114.8 %all-gather.10.cloned.1.call-start = ((), (), s32[]{:S(2)}) async-start(), calls=%async_computation.10 | async-start | bytes 4718592 | tf_op jit(solution)/shard_map/all_gather | solution.py:1016
  436.7 43.4 %collective-permute-start.27 = (bf16[512,2176]{1,0:T(8,128)(2,1)}, bf16[512,2176]{1,0:T(8,128)(2,1)}, u32[]{:S(2)}, u32[]{:S(2)}) collective-permute-start(bf16[512,2176]{1,0:T(8,128)(2,1)} %get-tuple-element.141), channel_id=1, source_target_pairs={{0,8},{8,0},{1,9},{9,1},{2,10},{10,2},{3,11},{11,3},{4,12},{12,4},... | collective-permute-start | bytes 6684680 | tf_op jit(solution)/shard_map/ppermute | solution.py:37
  437.6 43.7 %collective-permute-start.28 = (bf16[512,2176]{1,0:T(8,128)(2,1)}, bf16[512,2176]{1,0:T(8,128)(2,1)}, u32[]{:S(2)}, u32[]{:S(2)}) collective-permute-start(bf16[512,2176]{1,0:T(8,128)(2,1)} %get-tuple-element.142), channel_id=1, source_target_pairs={{0,16},{16,0},{1,17},{17,1},{2,18},{18,2},{3,19},{19,3},{4,20},{20... | collective-permute-start | bytes 6684680 | tf_op jit(solution)/shard_map/ppermute | solution.py:37
  484.3 305.8 %reduce-scatter.11.cloned.1.call-start = ((), (), s32[]{:S(2)}) async-start(), calls=%async_computation.12 | async-start | bytes 4718592 | tf_op jit(solution)/shard_map/reduce_scatter | solution.py:1075
  484.4 45.7 %collective-permute-start.30 = (bf16[512,2176]{1,0:T(8,128)(2,1)}, bf16[512,2176]{1,0:T(8,128)(2,1)S(1)}, u32[]{:S(2)}, u32[]{:S(2)}) collective-permute-start(bf16[512,2176]{1,0:T(8,128)(2,1)} %get-tuple-element.156), channel_id=1, source_target_pairs={{0,16},{16,0},{1,17},{17,1},{2,18},{18,2},{3,19},{19,3},{4,20},{20... | collective-permute-start | bytes 6684680 | tf_op jit(solution)/shard_map/ppermute | solution.py:37
  486.0 51.8 %collective-permute-start.29 = (bf16[512,2176]{1,0:T(8,128)(2,1)}, bf16[512,2176]{1,0:T(8,128)(2,1)S(1)}, u32[]{:S(2)}, u32[]{:S(2)}) collective-permute-start(bf16[512,2176]{1,0:T(8,128)(2,1)} %get-tuple-element.155), channel_id=1, source_target_pairs={{0,8},{8,0},{1,9},{9,1},{2,10},{10,2},{3,11},{11,3},{4,12},{12,4},... | collective-permute-start | bytes 6684680 | tf_op jit(solution)/shard_map/ppermute | solution.py:37
  562.3 27.5 %collective-permute-start.31 = (bf16[1024,512]{1,0:T(8,128)(2,1)}, bf16[1024,512]{1,0:T(8,128)(2,1)}, u32[]{:S(2)}, u32[]{:S(2)}) collective-permute-start(bf16[1024,512]{1,0:T(8,128)(2,1)} %get-tuple-element.162), channel_id=1, source_target_pairs={{8,0},{9,1},{10,2},{11,3},{12,4},{13,5},{14,6},{15,7},{24,16},{25,... | collective-permute-start | bytes 3145736 | tf_op jit(solution)/shard_map/ppermute | solution.py:1031
  603.4 188.2 %reduce-scatter.9.cloned.1.call-start = ((), (), s32[]{:S(2)}) async-start(), calls=%async_computation.11 | async-start | bytes 4718592 | tf_op jit(solution)/shard_map/reduce_scatter | solution.py:1026
  624.1 104.6 %collective-permute-start.35 = (bf16[768,2176]{1,0:T(8,128)(2,1)}, bf16[768,2176]{1,0:T(8,128)(2,1)}, u32[]{:S(2)}, u32[]{:S(2)}) collective-permute-start(bf16[768,2176]{1,0:T(8,128)(2,1)} %pad_maximum_fusion.1), channel_id=1, source_target_pairs={{0,8},{8,0},{1,9},{9,1},{2,10},{10,2},{3,11},{11,3},{4,12},{12,4},... | collective-permute-start | bytes 10027016 | tf_op jit(solution)/shard_map/ppermute | solution.py:37
  624.1 104.5 %collective-permute-start.36 = (bf16[768,2176]{1,0:T(8,128)(2,1)}, bf16[768,2176]{1,0:T(8,128)(2,1)}, u32[]{:S(2)}, u32[]{:S(2)}) collective-permute-start(bf16[768,2176]{1,0:T(8,128)(2,1)} %pad_maximum_fusion.2), channel_id=1, source_target_pairs={{0,16},{16,0},{1,17},{17,1},{2,18},{18,2},{3,19},{19,3},{4,20},{20... | collective-permute-start | bytes 10027016 | tf_op jit(solution)/shard_map/ppermute | solution.py:37
  642.5 78.7 %collective-permute-start.39 = (bf16[64,2048]{1,0:T(8,128)(2,1)S(1)}, bf16[64,2048]{1,0:T(8,128)(2,1)S(1)}, u32[]{:S(2)}, u32[]{:S(2)}) collective-permute-start(bf16[64,2048]{1,0:T(8,128)(2,1)S(1)} %pad_maximum_fusion.12), channel_id=1, source_target_pairs={{0,8},{8,0},{1,9},{9,1},{2,10},{10,2},{3,11},{11,3},{4,12},{12,4},... | collective-permute-start | bytes 786440 | tf_op jit(solution)/shard_map/ppermute | solution.py:37
  644.5 76.7 %collective-permute-start.41 = (bf16[64,2048]{1,0:T(8,128)(2,1)S(1)}, bf16[64,2048]{1,0:T(8,128)(2,1)S(1)}, u32[]{:S(2)}, u32[]{:S(2)}) collective-permute-start(bf16[64,2048]{1,0:T(8,128)(2,1)S(1)} %pad_maximum_fusion.13), channel_id=1, source_target_pairs={{0,16},{16,0},{1,17},{17,1},{2,18},{18,2},{3,19},{19,3},{4,20},{20... | collective-permute-start | bytes 786440 | tf_op jit(solution)/shard_map/ppermute | solution.py:37
  645.2 72.5 %collective-permute-start.43 = (f32[16,832]{1,0:T(8,128)S(1)}, f32[16,832]{1,0:T(8,128)S(1)}, u32[]{:S(2)}, u32[]{:S(2)}) collective-permute-start(f32[16,832]{1,0:T(8,128)S(1)} %slice_select_fusion), channel_id=1, source_target_pairs={{0,16},{16,0},{1,17},{17,1},{2,18},{18,2},{3,19},{19,3},{4,20},{20... | collective-permute-start | bytes 159752 | tf_op jit(solution)/shard_map/ppermute | solution.py:215
  752.4 30.9 %all-to-all-start.1 = ((bf16[8,64,768]{2,1,0:T(8,128)(2,1)}), bf16[8,64,768]{2,1,0:T(8,128)(2,1)}, u32[]{:S(2)}, u32[]{:S(2)}) async-start(bf16[8,64,768]{2,1,0:T(8,128)(2,1)} %bitcast.64), calls=%async_computation.5 | async-start | bytes 1572864 | tf_op jit(solution)/shard_map/all_to_all | solution.py:1085
  (115 other events, 1157.9 us)
Sparse Core Ops, SparseCore 0:
  16.9 63.3 all-gather.11
  83.9 47.2 all-gather.5
  175.5 52.0 reduce-scatter.4
  276.7 47.0 all-gather.7
  426.7 50.1 reduce-scatter.6
  484.4 46.6 all-gather.9
  603.5 52.7 reduce-scatter.10
  658.6 48.1 reduce-scatter.8

commit v4 on v3

--- a/solution.py
+++ b/solution.py
@@ -130,11 +130,30 @@
             self.own = made[-1]
         return made
 
-    def send_first(self, after=()):
+    def send_first(self):
+        self.across = by_context(lambda s: self.to_across[s])
+        self.along = by_dp(lambda d: self.to_along[d])
+        return self.across, self.along
+
+    def send_free(self, after):
         (across, along), _ = tie((self.to_across, self.to_along), after)
-        self.across = by_context(lambda s: across[s])
-        self.along = by_dp(lambda d: along[d])
-        return self.across, self.along
+        self.free = (
+            by_context(lambda s: across[s][-self.half :]),
+            by_dp(lambda d: along[d][-self.half :]),
+        )
+        return self.free
+
+    def send_far(self, after):
+        across, _ = tie(self.to_across, after)
+        far_across = by_context(lambda s: across[s][: -self.half])
+        far_along = by_dp(lambda d: self.to_along[d][: -self.half])
+        self.across = {
+            s: jnp.concatenate([x, self.free[0][s]], 0) for s, x in far_across.items()
+        }
+        self.along = {
+            d: jnp.concatenate([x, self.free[1][d]], 0) for d, x in far_along.items()
+        }
+        return far_across, far_along
 
     def row(self, x, i):
         return x[i * self.half : (i + 1) * self.half].astype(F32)
@@ -165,18 +184,12 @@
         return jnp.concatenate([top, bottom], 0)
 
 
-def join_last(scatters):
+def send_last(scatters, after=None):
     sums = [scatter.sums() for scatter in scatters]
-    return (
-        {s: jnp.concatenate([x[0][s] for x in sums], 0) for s in sums[0][0]},
-        {d: jnp.concatenate([x[1][d] for x in sums], 0) for d in sums[0][1]},
-    )
-
-
-def send_last(scatters, blocks=None):
-    to_across, to_along = join_last(scatters) if blocks is None else blocks
-    across = by_context(lambda s: to_across[s])
-    along = by_dp(lambda d: to_along[d])
+    if after is not None:
+        sums, _ = tie(sums, after)
+    across = by_context(lambda s: jnp.concatenate([x[0][s] for x in sums], 0))
+    along = by_dp(lambda d: jnp.concatenate([x[1][d] for x in sums], 0))
     split, start = [], 0
     for scatter in scatters:
         rows = slice(start, start + scatter.half)
@@ -487,7 +500,7 @@
         out[rows, :] = total.astype(BF16)
 
 
-def spread(pairs, extra=None, weight=1):
+def spread(pairs, extra=None):
     acts = [a for a, _ in pairs]
     first = pairs[0][1]
     half, steps = first.half, len(first.parts)
@@ -517,7 +530,7 @@
             scratch_shapes=[pltpu.VMEM((half, first.columns), BF16)] * len(pairs),
         ),
         compiler_params=params(60),
-        cost_estimate=cost(2 * weight * m * width * first.columns * len(pairs), 20 * MIB),
+        cost_estimate=cost(2 * m * width * first.columns * len(pairs), 20 * MIB),
         name="spread",
     )(first.places, *operands)
 
@@ -527,14 +540,15 @@
 
 
 def qkv_kernel(half, wide, places, tok, gain, bias, cosine, sine, *refs):
-    normed, query, key_value, full = refs[-4:]
+    normed, query, key_value, inverse, full = refs[-5:]
 
     @pl.when(pl.program_id(0) == 0)
     def _():
-        assemble(places, full, refs[:-4], half)
+        assemble(places, full, refs[:-5], half)
 
     values = tok[...].astype(F32)
     inv = lax.rsqrt(jnp.mean(values * values, -1, keepdims=True) + EPSILON)
+    inverse[...] = inv
     normed[...] = (values * inv * gain[...]).astype(BF16)
     out = mat_dot(normed[...], full[...]) + bias[...]
     for h in range(2 * wide // HD):
@@ -558,6 +572,7 @@
             jax.ShapeDtypeStruct((m, width), BF16),
             jax.ShapeDtypeStruct((m, wide), BF16),
             jax.ShapeDtypeStruct((m, 2 * wide), BF16),
+            jax.ShapeDtypeStruct((m, 1), F32),
         ),
         grid_spec=pltpu.PrefetchScalarGridSpec(
             num_scalar_prefetch=1,
@@ -577,6 +592,7 @@
                 pl.BlockSpec((step, width), row),
                 pl.BlockSpec((step, wide), row),
                 pl.BlockSpec((step, 2 * wide), row),
+                pl.BlockSpec((step, 1), row),
             ],
             scratch_shapes=[pltpu.VMEM((width, 3 * wide), BF16)],
         ),
@@ -915,7 +931,7 @@
         return lax.dynamic_index_in_dim(row, run, 1, keepdims=False).reshape(-1)
 
     bias = jnp.concatenate([own_heads(columns[k]) for k in ("bq", "bk", "bv")])
-    normed, queries, key_value = qkv_project(
+    normed, queries, key_value, inverse = qkv_project(
         all_tokens, gain_attn[None], bias[None], cosine, sine_table, qkv_pieces, wide
     )
     kvs = [key_value] + [
@@ -1001,10 +1017,13 @@
     gate_sum.make(last=False)
     gate_sent = gate_sum.send_first()
     terms = [down_sum.make(first=False), gate_sum.make(first=False)]
+    out_part = spread([(scaled, down_pieces)])
+    grad_normed_two, _ = tie(grad_normed_two, (gate_sent, terms, out_part))
+    both = send_last([down_sum, gate_sum])
+    down_last, gate_last = both
+    grad_up, _ = tie(grad_up, grad_normed_two)
     up_sum = scatter_of(rows, grad_up)
-    terms.append(up_sum.make())
-    grad_normed_two, _ = tie(grad_normed_two, (gate_sent, terms))
-    up_sent = up_sum.send_first()
+    up_sum.make()
     grad_router_switch = left_dot(rows, grad_small)
 
     grad_unit = grad_normed_two * gain_ffn
@@ -1014,16 +1033,17 @@
     grad_gain_ffn = jnp.sum(grad_normed_two * unit_two, 0)
     attn_own = grad_residual.astype(BF16)
     grad_attn = lax.all_gather(attn_own, "expert", axis=0, tiled=True)
-    grad_attn, _ = tie(grad_attn, up_sent)
+    output = lax.psum_scatter(
+        tie(out_part, attn_own)[0], "expert", scatter_dimension=0, tiled=True
+    )
+    grad_attn, _ = tie(grad_attn, both)
+    up_sent = up_sum.send_free(both)
     grad_query, grad_own, *grad_far = attend_back(
         queries, kvs, allowed, w_o, grad_attn, cosine, sine_table
     )
-    (mixed, scaled), _ = tie((mixed, scaled), grad_query)
-    out_part = spread([(scaled, down_pieces)], weight=4)
-    three = [down_sum, gate_sum, up_sum]
-    blocks = join_last(three)
-    grad_own, _ = tie(grad_own, (out_part, blocks))
-    output = lax.psum_scatter(out_part, "expert", scatter_dimension=0, tiled=True)
+    grad_far, (down_last, _) = tie(grad_far, (down_last, up_sent))
+    grad_down_w = down_sum.finish(down_last)
+    mixed, _ = tie(mixed, grad_query)
     grad_wo = left_dot(mixed, grad_attn).astype(BF16).reshape(heads, part, rows_flat, width)
     wo_back = core_exchange(grad_wo.transpose(1, 0, 2, 3), part)
     wo_back = wo_back.reshape(2 * planes, rows_flat // 2, width)
@@ -1032,26 +1052,38 @@
         for s, piece in enumerate(grad_far, 1)
     ]
     grad_qkv, bias_sums = join(grad_query, grad_own, grad_far, cosine, sine_table)
-    grad_qkv, wo_back = tie(grad_qkv, wo_back)
+    grad_qkv, (output, gate_last, wo_back) = tie(grad_qkv, (output, gate_last, wo_back))
+    grad_gate_w = gate_sum.finish(gate_last)
     out_tokens = (residual + output.astype(F32)).astype(BF16)
-    def to_heads(row):
-        full = jnp.zeros((part, heads, runs, HD), F32)
-        full = lax.dynamic_update_slice(
-            full, row.reshape(1, heads, 1, HD), (member, 0, run, 0)
-        )
-        return full.reshape(planes * count, rows_flat)
-
-    bias_sums = bias_sums[0]
-    small_grads = jnp.concatenate(
-        [to_heads(bias_sums[i * wide : (i + 1) * wide]) for i in range(3)]
-        + [
-            grad_gain_ffn.reshape(-1, rows_flat),
-            grad_router_switch[:, count].reshape(-1, rows_flat),
-            grad_router_switch[:, :count].reshape(planes * count, rows_flat * count),
-        ],
-        1,
-    )
-
+    up_far_sent = up_sum.send_far(grad_far)
+    qkv_sum = scatter_of(normed, grad_qkv)
+    grad_qkv, _ = tie(grad_qkv, qkv_sum.make())
+    qkv_sent = qkv_sum.send_first()
+    grad_normed = spread([(grad_qkv, qkv_pieces)])
+    grad_normed, _ = tie(grad_normed, up_far_sent)
+    grad_normed_own = lax.psum_scatter(
+        grad_normed, "expert", scatter_dimension=0, tiled=True
+    ).astype(F32)
+    (qkv_last,) = send_last([qkv_sum])
+    grad_normed_own, _ = tie(grad_normed_own, qkv_last)
+
+    qkv_grad_rows = qkv_sum.finish(qkv_last)
+    (up_last,) = send_last([up_sum], qkv_sent)
+    grad_up_w = up_sum.finish(up_last)
+    qkv_back = lax.all_to_all(
+        qkv_grad_rows.astype(BF16).reshape(count, rows_flat, 3 * wide),
+        "expert",
+        split_axis=0,
+        concat_axis=0,
+        tiled=True,
+    )
+
+    def from_heads(i):
+        w = qkv_back[..., i * wide : (i + 1) * wide].astype(F32)
+        w = w.reshape(runs, part, rows_flat, heads, HD).transpose(2, 1, 3, 0, 4)
+        return w.reshape(rows_flat, width)
+
+    wo_back, _ = tie(wo_back, qkv_last)
     wo_sum = Scatter(
         lambda groups: [
             jnp.concatenate(
@@ -1062,49 +1094,35 @@
         rows_flat // 2,
     )
     wo_sum.make()
-    qkv_sum = scatter_of(normed, grad_qkv)
-    lasts = send_last(three, tie(blocks, grad_far)[0])
-    down_last, gate_last, up_last = lasts
-    qkv_sum.make()
-    qkv_sent = qkv_sum.send_first()
-    wo_sum.send_first(qkv_sent)
-    small_sum = small_scatter(tie(small_grads, qkv_sent)[0], ("dp", "context"))
-    (wo_last,) = send_last([wo_sum])
-    (qkv_last,) = send_last([qkv_sum], tie(join_last([qkv_sum]), lasts)[0])
-    grad_normed = spread([(grad_qkv, qkv_pieces)])
-    grad_normed_own = lax.psum_scatter(
-        grad_normed, "expert", scatter_dimension=0, tiled=True
-    ).astype(F32)
-    grad_normed_own, _ = tie(grad_normed_own, (qkv_last, up_last))
-
-    qkv_grad_rows = qkv_sum.finish(qkv_last)
-    grad_gate_w = gate_sum.finish(gate_last)
-    grad_down_w = down_sum.finish(down_last)
-    grad_w_out = wo_sum.finish(wo_last)
-    grad_up_w = up_sum.finish(up_last)
-    qkv_back = lax.all_to_all(
-        qkv_grad_rows.astype(BF16).reshape(count, rows_flat, 3 * wide),
-        "expert",
-        split_axis=0,
-        concat_axis=0,
-        tiled=True,
-    )
-
-    def from_heads(i):
-        w = qkv_back[..., i * wide : (i + 1) * wide].astype(F32)
-        w = w.reshape(runs, part, rows_flat, heads, HD).transpose(2, 1, 3, 0, 4)
-        return w.reshape(rows_flat, width)
-
-    small_sum, _ = tie(small_sum, (qkv_last, up_last))
+    wo_sum.send_first()
+    grad_w_out = wo_sum.finish(send_last([wo_sum])[0])
+
+    def to_heads(row):
+        full = jnp.zeros((part, heads, runs, HD), F32)
+        full = lax.dynamic_update_slice(
+            full, row.reshape(1, heads, 1, HD), (member, 0, run, 0)
+        )
+        return full.reshape(planes * count, rows_flat)
+
+    bias_sums = bias_sums[0]
+    grad_gain_attn = jnp.sum(
+        grad_normed.astype(F32) * (all_tokens.astype(F32) * inverse), 0
+    )
+    small_grads = jnp.concatenate(
+        [to_heads(bias_sums[i * wide : (i + 1) * wide]) for i in range(3)]
+        + [
+            grad_gain_attn.reshape(-1, rows_flat),
+            grad_gain_ffn.reshape(-1, rows_flat),
+            grad_router_switch[:, count].reshape(-1, rows_flat),
+            grad_router_switch[:, :count].reshape(planes * count, rows_flat * count),
+        ],
+        1,
+    )
+    small_grads, _ = tie(small_grads, qkv_last)
+    small_sum = small_scatter(small_grads, ("dp", "context"))
     small_sum = small_scatter(small_sum, ("expert",))[0]
-    pieces = [small_sum[i * rows_flat : (i + 1) * rows_flat] for i in range(5)]
-    grad_router = small_sum[5 * rows_flat :].reshape(rows_flat, count)
-
-    w_grads = [from_heads(i) for i in range(3)]
-    grad_gain_attn = sum(
-        jnp.sum(w.astype(F32) * grad, 1)
-        for w, grad in zip((w_query, w_key, w_value), w_grads)
-    ) / norm_attn.astype(F32)
+    pieces = [small_sum[i * rows_flat : (i + 1) * rows_flat] for i in range(6)]
+    grad_router = small_sum[6 * rows_flat :].reshape(rows_flat, count)
 
     unit_one, scale_one = rms_unit(token_rows.astype(F32))
     grad_unit = grad_normed_own * gain_attn
@@ -1114,18 +1132,20 @@
     return (
         out_tokens[None],
         grad_tokens.astype(BF16)[None],
-        *w_grads,
+        from_heads(0),
+        from_heads(1),
+        from_heads(2),
         grad_w_out,
         pieces[0],
         pieces[1],
         pieces[2],
-        grad_gain_attn,
         pieces[3],
+        pieces[4],
         grad_router,
         grad_gate_w[:, fe_width : fe_width + fs_width],
         grad_up_w[:, fe_width : fe_width + fs_width],
         grad_down_w[:, fe_width : fe_width + fs_width].T,
-        pieces[4],
+        pieces[5],
         grad_gate_w[None, :, :fe_width],
         grad_up_w[None, :, :fe_width],
         grad_down_w[:, :fe_width].T[None],

time: 811 us -> 788 us (0.972)
  waiting for transfers between devices: 308 us -> 276 us
  other arithmetic: 67.9 us -> 83.2 us
    ppermute x5, waiting for transfers between devices: 78.2 us -> 34.5 us  [small_scatter(): other = lax.ppermute(jnp.where(high, low_part, high_part), axis, pairs)]
    slice x2 -> x8, local copies, waits for them, and re-layouts: 0.68 us -> 15.1 us  [the longest x2 6.2 us: send_last(): x[rows]]
    ppermute x5, waiting for transfers between devices: 10.9 us -> 22.1 us  [small_gather(): other = lax.ppermute(x, axis, pairs)]
    ppermute x34 -> x38, waiting for transfers between devices: 199 us -> 192 us  [shift(): return lax.ppermute(x, axis, [(i, (i + step) % n) for i in range(n)])]
    unnamed x186 -> x208, local copies, waits for them, and re-layouts: 47.5 us -> 50 us
    ppermute x34 -> x38, starting transfers between devices: 43.3 us -> 42.3 us  [shift(): return lax.ppermute(x, axis, [(i, (i + step) % n) for i in range(n)])]
  transfers between devices with their start and end apart: 58 -> 62, of which waited for: 25 -> 28; matrix products, arithmetic and copies ran while one was open for 18% -> 20% of each run, Pallas kernels for 17% -> 19%
where the time goes in v4:
time: 788 us; the launch traced here: 779 us
  waiting for transfers between devices  276 us (35%)
  Pallas kernels  213 us (27%)
  local copies, waits for them, and re-layouts  123 us (16%)
  other arithmetic  83.2 us (11%)
  starting transfers between devices  64 us (8%)
  between operations  16.3 us (2%)
    ppermute x38, waiting for transfers between devices, shift(): return lax.ppermute(x, axis, [(i, (i + step) % n) for i in range(n)])  192 us
    pallas_call x6, Pallas kernels, weight_grad(): pl.pallas_call(functools.partial(weight_grad_kernel, counts, half), out_s...  67.4 us
    pallas_call x3, Pallas kernels, spread(): pl.pallas_call(functools.partial(spread_kernel, steps, len(pairs), extra...  62.8 us
    unnamed x208, local copies, waits for them, and re-layouts  50 us
    ppermute x38, starting transfers between devices, shift(): return lax.ppermute(x, axis, [(i, (i + step) % n) for i in range(n)])  42.3 us
    pallas_call x1, Pallas kernels, ffn(): pl.pallas_call(functools.partial(ffn_kernel, len(gates.parts), gates.half...  35.6 us
    ppermute x5, waiting for transfers between devices, small_scatter(): other = lax.ppermute(jnp.where(high, low_part, high_part), axis, pairs)  34.5 us
    ppermute x5, waiting for transfers between devices, small_gather(): other = lax.ppermute(x, axis, pairs)  22.1 us
  transfers between devices with their start and end apart: 62, of which 28 were waited for; matrix products, arithmetic and copies ran while one was open for 20% of the time, Pallas kernels for 19%

profile of v4, /device:TPU:0, one launch (start us, length us, event | category | flops | bytes accessed | tf_op | source)
XLA Modules:
  0.0 778.9 jit_solution(11854597825421036959)
XLA Ops:
  43.2 7.8 pad_maximum_fusion.refs_0_.refs_1_.refs_14_.refs_15_.refs_10_.refs_11_.refs_2_
  52.2 12.8 %collective-permute-done = f32[1,1666]{1,0:T(1,128)S(1)} collective-permute-done((f32[1,1666]{1,0:T(1,128)S(1)}, f32[1,1666]{1,0:T(1,128)S(1)}, u32[]{:S(2)}, u32[]{:S(2)}) %collective-permute-start) | collective-permute-done | bytes 6696 | tf_op jit(solution)/shard_map/ppermute | solution.py:215
  73.0 5.9 collective-permute-done.5
  92.5 7.3 collective-permute-done.8.refs_4_.refs_5_.refs_6_
  104.7 5.2 collective-permute-done.10.refs_7_.refs_8_
  119.7 6.1 qkv_project.1
  135.8 6.0 collective-permute-done.17.refs_13_.refs_9_
  141.8 18.8 %collective-permute-done.16.refs_1_ = bf16[1024,512]{1,0:T(8,128)(2,1)S(1)} collective-permute-done((bf16[1024,512]{1,0:T(8,128)(2,1)S(1)}, bf16[1024,512]{1,0:T(8,128)(2,1)S(1)}, u32[]{:S(2)}, u32[]{:S(2)}) %collective-permute-start.16) | collective-permute-done | bytes 1048608 | tf_op jit(solution)/shard_map/ppermute | solution.py:938
  165.1 8.8 %attend.1 = (bf16[1024,256]{1,0:T(8,128)(2,1)S(1)}, bf16[1024,2048]{1,0:T(8,128)(2,1)S(1)}) custom-call(bf16[1024,256]{1,0:T(8,128)(2,1)S(1)} %copy-done.19, f32[8,128,256]{2,1,0:T(8,128)S(1)} %add_convert_fusion.7.allowed, bf16[256,2048]{1,0:T(8,128)(2,1)S(1)} %bitcast.192, bf16[1024,512]{1,0:T(8,128)(2,1)S(1)} %copy-done.12, bf16[1024,512]{1,0:T(8,128)(2,1)S(1)} %copy-done.15), custom_call_target="tpu_custom_call" | custom-call | flops 671088640 | bytes 4194304 | tf_op jit(solution)/shard_map/attend/pallas_call | solution.py:631
  180.5 91.4 %collective-permute-done.20.refs_4_.refs_5_.refs_18_.refs_19_.refs_14_.refs_15_.refs_6_ = bf16[1024,2176]{1,0:T(8,128)(2,1)} collective-permute-done((bf16[1024,2176]{1,0:T(8,128)(2,1)}, bf16[1024,2176]{1,0:T(8,128)(2,1)}, u32[]{:S(2)}, u32[]{:S(2)}) %collective-permute-start.20) | collective-permute-done | bytes 4456480 | tf_op jit(solution)/shard_map/ppermute | solution.py:37
  298.5 13.4 %collective-permute-done.21.refs_7_.refs_8_ = bf16[256,2176]{1,0:T(8,128)(2,1)} collective-permute-done((bf16[256,2176]{1,0:T(8,128)(2,1)}, bf16[256,2176]{1,0:T(8,128)(2,1)}, u32[]{:S(2)}, u32[]{:S(2)}) %collective-permute-start.21) | collective-permute-done | bytes 1114144 | tf_op jit(solution)/shard_map/ppermute | solution.py:37
  311.9 5.2 collective-permute-done.22.refs_6_.refs_7_
  319.2 15.9 %hidden_grad.1.refs_5_ = f32[1024,2176]{1,0:T(8,128)} custom-call(s32[8]{0:T(128)S(1)} %stack.44.places.refs_0_, bf16[1024,2048]{1,0:T(8,128)(2,1)S(1)} %copy-done, bf16[1024,2176]{1,0:T(8,128)(2,1)} %pad_maximum_fusion.refs_0_.refs_1_.refs_14_.refs_15_.refs_10_.refs_11_.refs_2_, ...), custom_call_target="tpu_custom_call" | custom-call | flops 4563402752 | bytes 10485760 | tf_op jit(solution)/shard_map/hidden_grad/pallas_call | solution.py:338
  337.2 35.6 %ffn.1 = (bf16[1024,2176]{1,0:T(8,128)(2,1)}, bf16[1024,2176]{1,0:T(8,128)(2,1)}, bf16[1024,2176]{1,0:T(8,128)(2,1)}, bf16[1024,128]{1,0:T(8,128)(2,1)S(1)}) custom-call(s32[8]{0:T(128)S(1)} %stack.44.places.refs_0_, s32[1]{0:T(128)} %bitcast.44.refs_1_, ...), custom_call_target="tpu_custom_call" | custom-call | flops 9126805504 | bytes 20971520 | tf_op jit(solution)/shard_map/ffn/pallas_call | solution.py:447
  372.9 9.9 %weight_grad.6 = (bf16[512,2176]{1,0:T(8,128)(2,1)}, bf16[512,2176]{1,0:T(8,128)(2,1)}) custom-call(s32[4]{0:T(128)S(1)} %get-tuple-element.363.numbers, bf16[1024,2048]{1,0:T(8,128)(2,1)} %all-gather.6.cloned.1.call-done.acts.refs_0_.refs_1_.refs_2_.refs_3_, bf16[1024,2048]{1,0:T(8,128)(2,1)} %all-gather.6.cloned.1.call-done.acts.refs_0_.refs_1_.refs_2_.refs_3_, ...), custom_call_target="tpu_custom_call" | custom-call | flops 2281701376 | bytes 6291456 | tf_op jit(solution)/shard_map/weight_grad/pallas_call | solution.py:296
  383.7 34.2 %spread.3 = bf16[1024,2048]{1,0:T(8,128)(2,1)} custom-call(s32[8]{0:T(128)} %copy-done.32, bf16[1024,2176]{1,0:T(8,128)(2,1)} %get-tuple-element.137.refs_0_.refs_4_, bf16[1024,2176]{1,0:T(8,128)(2,1)} %get-tuple-element.157.refs_1_.refs_8_, bf16[512,2176]{1,0:T(8,128)(2,1)} %concatenate.97.refs_6_.refs_7_.refs_2_.refs_3_, ...), custom_call_target="tpu_custom_call" | custom-call | flops 9126805504 | bytes 10485760 | tf_op jit(solution)/shard_map/spread/pallas_call | solution.py:522
  417.9 9.0 %collective-permute-done.25 = bf16[512,2176]{1,0:T(8,128)(2,1)} collective-permute-done((bf16[512,2176]{1,0:T(8,128)(2,1)}, bf16[512,2176]{1,0:T(8,128)(2,1)}, u32[]{:S(2)}, u32[]{:S(2)}) %collective-permute-start.25) | collective-permute-done | bytes 2228256 | tf_op jit(solution)/shard_map/ppermute | solution.py:37
  427.7 10.2 %weight_grad.7 = (bf16[512,2176]{1,0:T(8,128)(2,1)}, bf16[512,2176]{1,0:T(8,128)(2,1)}) custom-call(s32[4]{0:T(128)S(1)} %get-tuple-element.363.numbers, bf16[1024,2048]{1,0:T(8,128)(2,1)} %all-gather.8.cloned.1.call-done.refs_2_.refs_0_.refs_1_.refs_3_.refs_4_.refs_5_.refs_6_.refs_7_, ...), custom_call_target="tpu_custom_call" | custom-call | flops 2281701376 | bytes 6291456 | tf_op jit(solution)/shard_map/weight_grad/pallas_call | solution.py:296
  439.5 10.8 %weight_grad.9 = (f32[256,2176]{1,0:T(8,128)}, f32[256,2176]{1,0:T(8,128)}, f32[512,2176]{1,0:T(8,128)}) custom-call(s32[4]{0:T(128)S(1)} %get-tuple-element.364.numbers, bf16[1024,2048]{1,0:T(8,128)(2,1)} %all-gather.8.cloned.1.call-done.refs_2_.refs_0_.refs_1_.refs_3_.refs_4_.refs_5_.refs_6_.refs_7_, ...), custom_call_target="tpu_custom_call" | custom-call | flops 2281701376 | bytes 6291456 | tf_op jit(solution)/shard_map/weight_grad/pallas_call | solution.py:296
  450.3 10.8 %weight_grad.8 = (f32[256,2176]{1,0:T(8,128)}, f32[256,2176]{1,0:T(8,128)}, f32[512,2176]{1,0:T(8,128)}) custom-call(s32[4]{0:T(128)S(1)} %get-tuple-element.364.numbers, bf16[1024,2048]{1,0:T(8,128)(2,1)} %all-gather.6.cloned.1.call-done.acts.refs_0_.refs_1_.refs_2_.refs_3_, ...), custom_call_target="tpu_custom_call" | custom-call | flops 2281701376 | bytes 6291456 | tf_op jit(solution)/shard_map/weight_grad/pallas_call | solution.py:296
  461.1 18.9 %spread.4 = bf16[1024,2048]{1,0:T(8,128)(2,1)} custom-call(s32[8]{0:T(128)} %copy-done.32, bf16[1024,2176]{1,0:T(8,128)(2,1)} %get-tuple-element.140.refs_4_.refs_0_, bf16[1024,2176]{1,0:T(8,128)(2,1)} %pad_maximum_fusion.refs_0_.refs_1_.refs_14_.refs_15_.refs_10_.refs_11_.refs_2_, ...), custom_call_target="tpu_custom_call" | custom-call | flops 4563402752 | bytes 10485760 | tf_op jit(solution)/shard_map/spread/pallas_call | solution.py:522
  506.4 17.3 %weight_grad.10 = (bf16[512,2176]{1,0:T(8,128)(2,1)}, bf16[512,2176]{1,0:T(8,128)(2,1)}, f32[256,2176]{1,0:T(8,128)}, f32[256,2176]{1,0:T(8,128)}, f32[512,2176]{1,0:T(8,128)}) custom-call(s32[8]{0:T(128)S(1)} %stack.53.numbers, bf16[1024,2048]{1,0:T(8,128)(2,1)} %all-gather.8.cloned.1.call-done.refs_2_.refs_0_.refs_1_.refs_3_.refs_4_.refs_5_.refs_6_.refs_7_, ...), custom_call_target="tpu_custom_call" | custom-call | flops 4563402752 | bytes 6291456 | tf_op jit(solution)/shard_map/weight_grad/pallas_call | solution.py:296
  527.1 15.1 %collective-permute-done.30 = bf16[512,2176]{1,0:T(8,128)(2,1)} collective-permute-done((bf16[512,2176]{1,0:T(8,128)(2,1)}, bf16[512,2176]{1,0:T(8,128)(2,1)}, u32[]{:S(2)}, u32[]{:S(2)}) %collective-permute-start.30) | collective-permute-done | bytes 2228256 | tf_op jit(solution)/shard_map/ppermute | solution.py:37
  555.0 11.1 %collective-permute-done.36 = bf16[256,2176]{1,0:T(8,128)(2,1)} collective-permute-done((bf16[256,2176]{1,0:T(8,128)(2,1)}, bf16[256,2176]{1,0:T(8,128)(2,1)}, u32[]{:S(2)}, u32[]{:S(2)}) %collective-permute-start.36) | collective-permute-done | bytes 1114144 | tf_op jit(solution)/shard_map/ppermute | solution.py:37
  574.4 15.0 %attend_back.1 = (bf16[1024,256]{1,0:T(8,128)(2,1)S(1)}, f32[1024,512]{1,0:T(8,128)S(1)}, bf16[1024,512]{1,0:T(8,128)(2,1)}) custom-call(bf16[1024,256]{1,0:T(8,128)(2,1)S(1)} %copy-done.20, f32[8,128,256]{2,1,0:T(8,128)S(1)} %add_convert_fusion.7.allowed, bf16[256,2048]{1,0:T(8,128)(2,1)S(1)} %bitcast.193, bf16[1024,2048]{1,0:T(8,128)(2,1)S(1)} %copy-done.9, ...), custom_call_target="tpu_custom_call" | custom-call | flops 939524096 | bytes 4194304 | tf_op jit(solution)/shard_map/attend_back/pallas_call | solution.py:690
  612.7 6.6 collective-permute-done.33.refs_0_
  623.9 8.5 %weight_grad.11 = (bf16[512,768]{1,0:T(8,128)(2,1)S(1)}, bf16[512,768]{1,0:T(8,128)(2,1)S(1)}, f32[256,768]{1,0:T(8,128)}, f32[256,768]{1,0:T(8,128)}, f32[512,768]{1,0:T(8,128)}) custom-call(s32[8]{0:T(128)S(1)} %stack.53.numbers, bf16[1024,2048]{1,0:T(8,128)(2,1)} %copy-done.1, bf16[1024,2048]{1,0:T(8,128)(2,1)} %copy-done.1, ...), custom_call_target="tpu_custom_call" | custom-call | flops 1610612736 | bytes 6291456 | tf_op jit(solution)/shard_map/weight_grad/pallas_call | solution.py:296
  643.8 9.6 %spread.5 = bf16[1024,2048]{1,0:T(8,128)(2,1)} custom-call(s32[8]{0:T(128)} %copy-done.32, bf16[1024,768]{1,0:T(8,128)(2,1)} %copy-done.7, bf16[512,768]{1,0:T(8,128)(2,1)} %bitcast.189, bf16[512,768]{1,0:T(8,128)(2,1)} %bitcast.190, bf16[512,768]{1,0:T(8,128)(2,1)} %copy-done.6, bf16[512,768]{1,0:T(8,128)(2,1)} %copy-done.6, bf16[512,768]{1,0:T(8,128)(2,1)} %copy-done.5, ...), custom_call_target="tpu_custom_call" | custom-call | flops 1610612736 | bytes 10485760 | tf_op jit(solution)/shard_map/spread/pallas_call | solution.py:522
  658.2 19.9 %collective-permute-done.35 = bf16[256,2176]{1,0:T(8,128)(2,1)} collective-permute-done((bf16[256,2176]{1,0:T(8,128)(2,1)}, bf16[256,2176]{1,0:T(8,128)(2,1)}, u32[]{:S(2)}, u32[]{:S(2)}) %collective-permute-start.35) | collective-permute-done | bytes 1114144 | tf_op jit(solution)/shard_map/ppermute | solution.py:37
  692.1 6.3 all-to-all-start.1
  698.4 13.8 %collective-permute-done.45 = f32[16,896]{1,0:T(8,128)S(1)} collective-permute-done((f32[16,896]{1,0:T(8,128)S(1)}, f32[16,896]{1,0:T(8,128)S(1)}, u32[]{:S(2)}, u32[]{:S(2)}) %collective-permute-start.45) | collective-permute-done | bytes 57376 | tf_op jit(solution)/shard_map/ppermute | solution.py:228
  718.8 14.8 %collective-permute-done.47 = f32[4,896]{1,0:T(4,128)S(1)} collective-permute-done((f32[4,896]{1,0:T(4,128)S(1)}, f32[4,896]{1,0:T(4,128)S(1)}, u32[]{:S(2)}, u32[]{:S(2)}) %collective-permute-start.47) | collective-permute-done | bytes 14368 | tf_op jit(solution)/shard_map/ppermute | solution.py:228
  (533 shorter events, 280.7 us)
Async XLA Ops:
  7.2 108.3 %all-gather.12.cloned.1.call-start = ((), (), s32[]{:S(2)}) async-start(), calls=%async_computation.13 | async-start | bytes 4718592 | tf_op jit(solution)/shard_map/all_gather | solution.py:819
  11.7 57.2 %collective-permute-start.3 = (bf16[512,2176]{1,0:T(8,128)(2,1)}, bf16[512,2176]{1,0:T(8,128)(2,1)}, u32[]{:S(2)}, u32[]{:S(2)}) collective-permute-start(bf16[512,2176]{1,0:T(8,128)(2,1)} %concatenate.97.refs_6_.refs_7_.refs_2_.refs_3_), channel_id=1, source_target_pairs={{0,16},{16,0},{1,17},{17,1},{2,18},{18,2},{3,19},{19,3},{4,20},{20... | collective-permute-start | bytes 6684680 | tf_op jit(solution)/shard_map/ppermute | solution.py:37
  14.6 54.2 %collective-permute-start.2 = (bf16[512,2176]{1,0:T(8,128)(2,1)}, bf16[512,2176]{1,0:T(8,128)(2,1)}, u32[]{:S(2)}, u32[]{:S(2)}) collective-permute-start(bf16[512,2176]{1,0:T(8,128)(2,1)} %concatenate.97.refs_6_.refs_7_.refs_2_.refs_3_), channel_id=1, source_target_pairs={{0,8},{8,0},{1,9},{9,1},{2,10},{10,2},{3,11},{11,3},{4,12},{12,4},... | collective-permute-start | bytes 6684680 | tf_op jit(solution)/shard_map/ppermute | solution.py:37
  20.1 48.8 %all-to-all-start = ((bf16[8,64,768]{2,1,0:T(8,128)(2,1)}), bf16[8,64,768]{2,1,0:T(8,128)(2,1)S(1)}, u32[]{:S(2)}, u32[]{:S(2)}) async-start(bf16[8,64,768]{2,1,0:T(8,128)(2,1)} %constant_dynamic-update-slice_fusion), calls=%async_computation | async-start | bytes 1572864 | tf_op jit(solution)/shard_map/all_to_all | solution.py:820
  25.1 136.5 %all-gather.6.cloned.1.call-start = ((), (), s32[]{:S(2)}) async-start(), calls=%async_computation.6 | async-start | bytes 4718592 | tf_op jit(solution)/shard_map/all_gather | solution.py:865
  83.2 190.4 %reduce-scatter.5.cloned.1.call-start = ((), (), s32[]{:S(2)}) async-start(), calls=%async_computation.7 | async-start | bytes 4718592 | tf_op jit(solution)/shard_map/reduce_scatter | solution.py:954
  113.6 28.1 %collective-permute-start.17 = (bf16[256,2176]{1,0:T(8,128)(2,1)}, bf16[256,2176]{1,0:T(8,128)(2,1)}, u32[]{:S(2)}, u32[]{:S(2)}) collective-permute-start(bf16[256,2176]{1,0:T(8,128)(2,1)} %slice.450), channel_id=1, source_target_pairs={{0,8},{8,0},{1,9},{9,1},{2,10},{10,2},{3,11},{11,3},{4,12},{12,4},... | collective-permute-start | bytes 3342344 | tf_op jit(solution)/shard_map/ppermute | solution.py:37
  127.4 33.2 %collective-permute-start.16 = (bf16[1024,512]{1,0:T(8,128)(2,1)S(1)}, bf16[1024,512]{1,0:T(8,128)(2,1)S(1)}, u32[]{:S(2)}, u32[]{:S(2)}) collective-permute-start(bf16[1024,512]{1,0:T(8,128)(2,1)S(1)} %get-tuple-element.129.refs_0_), channel_id=1, source_target_pairs={{0,8},{1,9},{2,10},{3,11},{4,12},{5,13},{6,14},{7,15},{16,24},{17,... | collective-permute-start | bytes 3145736 | tf_op jit(solution)/shard_map/ppermute | solution.py:938
  176.8 158.3 %all-gather.8.cloned.1.call-start = ((), (), s32[]{:S(2)}) async-start(), calls=%async_computation.8 | async-start | bytes 4718592 | tf_op jit(solution)/shard_map/all_gather | solution.py:962
  176.9 95.0 %collective-permute-start.20 = (bf16[1024,2176]{1,0:T(8,128)(2,1)}, bf16[1024,2176]{1,0:T(8,128)(2,1)}, u32[]{:S(2)}, u32[]{:S(2)}) collective-permute-start(bf16[1024,2176]{1,0:T(8,128)(2,1)} %pad_maximum_fusion.refs_0_.refs_1_.refs_14_.refs_15_.refs_10_.refs_11_.refs_2_), channel_id=1, source_target_pairs={{0,16},{16,0},{1,17},{17,1},{2,18},{18,2},{3,19},{19,3},{4,20},{20... | collective-permute-start | bytes 13369352 | tf_op jit(solution)/shard_map/ppermute | solution.py:37
  178.0 95.6 %collective-permute-start.19 = (bf16[1024,2176]{1,0:T(8,128)(2,1)}, bf16[1024,2176]{1,0:T(8,128)(2,1)}, u32[]{:S(2)}, u32[]{:S(2)}) collective-permute-start(bf16[1024,2176]{1,0:T(8,128)(2,1)} %pad_maximum_fusion.refs_0_.refs_1_.refs_14_.refs_15_.refs_10_.refs_11_.refs_2_), channel_id=1, source_target_pairs={{0,8},{8,0},{1,9},{9,1},{2,10},{10,2},{3,11},{11,3},{4,12},{12,4},... | collective-permute-start | bytes 13369352 | tf_op jit(solution)/shard_map/ppermute | solution.py:37
  277.3 202.7 %reduce-scatter.7.cloned.1.call-start = ((), (), s32[]{:S(2)}) async-start(), calls=%async_computation.9 | async-start | bytes 4718592 | tf_op jit(solution)/shard_map/reduce_scatter | solution.py:1014
  291.0 44.2 %collective-permute-start.24 = (bf16[256,2176]{1,0:T(8,128)(2,1)}, bf16[256,2176]{1,0:T(8,128)(2,1)}, u32[]{:S(2)}, u32[]{:S(2)}) collective-permute-start(bf16[256,2176]{1,0:T(8,128)(2,1)} %get-tuple-element.299), channel_id=1, source_target_pairs={{0,8},{8,0},{1,9},{9,1},{2,10},{10,2},{3,11},{11,3},{4,12},{12,4},... | collective-permute-start | bytes 3342344 | tf_op jit(solution)/shard_map/ppermute | solution.py:37
  291.3 43.8 %collective-permute-start.23 = (bf16[256,2176]{1,0:T(8,128)(2,1)}, bf16[256,2176]{1,0:T(8,128)(2,1)}, u32[]{:S(2)}, u32[]{:S(2)}) collective-permute-start(bf16[256,2176]{1,0:T(8,128)(2,1)} %get-tuple-element.301), channel_id=1, source_target_pairs={{0,16},{16,0},{1,17},{17,1},{2,18},{18,2},{3,19},{19,3},{4,20},{20... | collective-permute-start | bytes 3342344 | tf_op jit(solution)/shard_map/ppermute | solution.py:37
  382.7 44.2 %collective-permute-start.25 = (bf16[512,2176]{1,0:T(8,128)(2,1)}, bf16[512,2176]{1,0:T(8,128)(2,1)}, u32[]{:S(2)}, u32[]{:S(2)}) collective-permute-start(bf16[512,2176]{1,0:T(8,128)(2,1)} %get-tuple-element.141), channel_id=1, source_target_pairs={{0,8},{8,0},{1,9},{9,1},{2,10},{10,2},{3,11},{11,3},{4,12},{12,4},... | collective-permute-start | bytes 6684680 | tf_op jit(solution)/shard_map/ppermute | solution.py:37
  382.9 44.7 %collective-permute-start.26 = (bf16[512,2176]{1,0:T(8,128)(2,1)}, bf16[512,2176]{1,0:T(8,128)(2,1)}, u32[]{:S(2)}, u32[]{:S(2)}) collective-permute-start(bf16[512,2176]{1,0:T(8,128)(2,1)} %get-tuple-element.142), channel_id=1, source_target_pairs={{0,16},{16,0},{1,17},{17,1},{2,18},{18,2},{3,19},{19,3},{4,20},{20... | collective-permute-start | bytes 6684680 | tf_op jit(solution)/shard_map/ppermute | solution.py:37
  427.6 141.0 %all-gather.10.cloned.1.call-start = ((), (), s32[]{:S(2)}) async-start(), calls=%async_computation.10 | async-start | bytes 4718592 | tf_op jit(solution)/shard_map/all_gather | solution.py:1035
  437.8 43.6 %collective-permute-start.27 = (bf16[512,2176]{1,0:T(8,128)(2,1)}, bf16[512,2176]{1,0:T(8,128)(2,1)}, u32[]{:S(2)}, u32[]{:S(2)}) collective-permute-start(bf16[512,2176]{1,0:T(8,128)(2,1)} %get-tuple-element.144), channel_id=1, source_target_pairs={{0,8},{8,0},{1,9},{9,1},{2,10},{10,2},{3,11},{11,3},{4,12},{12,4},... | collective-permute-start | bytes 6684680 | tf_op jit(solution)/shard_map/ppermute | solution.py:37
  438.7 43.0 %collective-permute-start.28 = (bf16[512,2176]{1,0:T(8,128)(2,1)}, bf16[512,2176]{1,0:T(8,128)(2,1)}, u32[]{:S(2)}, u32[]{:S(2)}) collective-permute-start(bf16[512,2176]{1,0:T(8,128)(2,1)} %get-tuple-element.145), channel_id=1, source_target_pairs={{0,16},{16,0},{1,17},{17,1},{2,18},{18,2},{3,19},{19,3},{4,20},{20... | collective-permute-start | bytes 6684680 | tf_op jit(solution)/shard_map/ppermute | solution.py:37
  484.8 136.7 %reduce-scatter.9.cloned.1.call-start = ((), (), s32[]{:S(2)}) async-start(), calls=%async_computation.11 | async-start | bytes 4718592 | tf_op jit(solution)/shard_map/reduce_scatter | solution.py:1036
  490.5 51.7 %collective-permute-start.30 = (bf16[512,2176]{1,0:T(8,128)(2,1)}, bf16[512,2176]{1,0:T(8,128)(2,1)}, u32[]{:S(2)}, u32[]{:S(2)}) collective-permute-start(bf16[512,2176]{1,0:T(8,128)(2,1)} %pad_maximum_fusion.5), channel_id=1, source_target_pairs={{0,16},{16,0},{1,17},{17,1},{2,18},{18,2},{3,19},{19,3},{4,20},{20... | collective-permute-start | bytes 6684680 | tf_op jit(solution)/shard_map/ppermute | solution.py:37
  491.8 276.4 %reduce-scatter.11.cloned.1.call-start = ((), (), s32[]{:S(2)}) async-start(), calls=%async_computation.12 | async-start | bytes 4718592 | tf_op jit(solution)/shard_map/reduce_scatter | solution.py:1064
  497.9 47.4 %collective-permute-start.29 = (bf16[512,2176]{1,0:T(8,128)(2,1)}, bf16[512,2176]{1,0:T(8,128)(2,1)}, u32[]{:S(2)}, u32[]{:S(2)}) collective-permute-start(bf16[512,2176]{1,0:T(8,128)(2,1)} %pad_maximum_fusion.4), channel_id=1, source_target_pairs={{0,8},{8,0},{1,9},{9,1},{2,10},{10,2},{3,11},{11,3},{4,12},{12,4},... | collective-permute-start | bytes 6684680 | tf_op jit(solution)/shard_map/ppermute | solution.py:37
  526.0 40.0 %collective-permute-start.36 = (bf16[256,2176]{1,0:T(8,128)(2,1)}, bf16[256,2176]{1,0:T(8,128)(2,1)}, u32[]{:S(2)}, u32[]{:S(2)}) collective-permute-start(bf16[256,2176]{1,0:T(8,128)(2,1)} %slice.374), channel_id=1, source_target_pairs={{0,16},{16,0},{1,17},{17,1},{2,18},{18,2},{3,19},{19,3},{4,20},{20... | collective-permute-start | bytes 3342344 | tf_op jit(solution)/shard_map/ppermute | solution.py:37
  552.0 39.7 %collective-permute-start.32 = (bf16[256,2176]{1,0:T(8,128)(2,1)}, bf16[256,2176]{1,0:T(8,128)(2,1)}, u32[]{:S(2)}, u32[]{:S(2)}) collective-permute-start(bf16[256,2176]{1,0:T(8,128)(2,1)} %slice.372), channel_id=1, source_target_pairs={{0,16},{16,0},{1,17},{17,1},{2,18},{18,2},{3,19},{19,3},{4,20},{20... | collective-permute-start | bytes 3342344 | tf_op jit(solution)/shard_map/ppermute | solution.py:37
  553.3 38.4 %collective-permute-start.31 = (bf16[256,2176]{1,0:T(8,128)(2,1)}, bf16[256,2176]{1,0:T(8,128)(2,1)}, u32[]{:S(2)}, u32[]{:S(2)}) collective-permute-start(bf16[256,2176]{1,0:T(8,128)(2,1)} %slice.371), channel_id=1, source_target_pairs={{0,8},{8,0},{1,9},{9,1},{2,10},{10,2},{3,11},{11,3},{4,12},{12,4},... | collective-permute-start | bytes 3342344 | tf_op jit(solution)/shard_map/ppermute | solution.py:37
  633.7 44.5 %collective-permute-start.39 = (bf16[512,768]{1,0:T(8,128)(2,1)S(1)}, bf16[512,768]{1,0:T(8,128)(2,1)}, u32[]{:S(2)}, u32[]{:S(2)}) collective-permute-start(bf16[512,768]{1,0:T(8,128)(2,1)S(1)} %get-tuple-element.177), channel_id=1, source_target_pairs={{0,8},{8,0},{1,9},{9,1},{2,10},{10,2},{3,11},{11,3},{4,12},{12,4},... | collective-permute-start | bytes 2359304 | tf_op jit(solution)/shard_map/ppermute | solution.py:37
  633.7 44.5 %collective-permute-start.35 = (bf16[256,2176]{1,0:T(8,128)(2,1)}, bf16[256,2176]{1,0:T(8,128)(2,1)}, u32[]{:S(2)}, u32[]{:S(2)}) collective-permute-start(bf16[256,2176]{1,0:T(8,128)(2,1)} %slice.373), channel_id=1, source_target_pairs={{0,8},{8,0},{1,9},{9,1},{2,10},{10,2},{3,11},{11,3},{4,12},{12,4},... | collective-permute-start | bytes 3342344 | tf_op jit(solution)/shard_map/ppermute | solution.py:37
  658.1 30.4 %collective-permute-start.38 = (bf16[256,768]{1,0:T(8,128)(2,1)S(1)}, bf16[256,768]{1,0:T(8,128)(2,1)S(1)}, u32[]{:S(2)}, u32[]{:S(2)}) collective-permute-start(bf16[256,768]{1,0:T(8,128)(2,1)S(1)} %add_convert_fusion.11), channel_id=1, source_target_pairs={{0,8},{8,0},{1,9},{9,1},{2,10},{10,2},{3,11},{11,3},{4,12},{12,4},... | collective-permute-start | bytes 1179656 | tf_op jit(solution)/shard_map/ppermute | solution.py:37
  687.5 62.6 %collective-permute-start.50 = (bf16[256,2176]{1,0:T(8,128)(2,1)}, bf16[256,2176]{1,0:T(8,128)(2,1)}, u32[]{:S(2)}, u32[]{:S(2)}) collective-permute-start(bf16[256,2176]{1,0:T(8,128)(2,1)} %add_convert_fusion), channel_id=1, source_target_pairs={{0,16},{16,0},{1,17},{17,1},{2,18},{18,2},{3,19},{19,3},{4,20},{20... | collective-permute-start | bytes 3342344 | tf_op jit(solution)/shard_map/ppermute | solution.py:37
  688.5 61.6 %collective-permute-start.51 = (bf16[256,2176]{1,0:T(8,128)(2,1)}, bf16[256,2176]{1,0:T(8,128)(2,1)}, u32[]{:S(2)}, u32[]{:S(2)}) collective-permute-start(bf16[256,2176]{1,0:T(8,128)(2,1)} %add_convert_fusion.1), channel_id=1, source_target_pairs={{0,8},{8,0},{1,9},{9,1},{2,10},{10,2},{3,11},{11,3},{4,12},{12,4},... | collective-permute-start | bytes 3342344 | tf_op jit(solution)/shard_map/ppermute | solution.py:37
  692.1 70.9 %all-to-all-start.1 = ((bf16[8,64,768]{2,1,0:T(8,128)(2,1)}), bf16[8,64,768]{2,1,0:T(8,128)(2,1)S(1)}, u32[]{:S(2)}, u32[]{:S(2)}) async-start(bf16[8,64,768]{2,1,0:T(8,128)(2,1)} %bitcast.64), calls=%async_computation.5 | async-start | bytes 1572864 | tf_op jit(solution)/shard_map/all_to_all | solution.py:1073
  (130 other events, 1560.2 us)
Sparse Core Ops, SparseCore 0:
  16.3 63.3 all-gather.11
  83.3 45.9 all-gather.5
  176.9 50.7 reduce-scatter.4
  277.4 47.7 all-gather.7
  427.7 50.8 reduce-scatter.6
  484.9 48.7 all-gather.9
  536.0 48.7 reduce-scatter.8
  678.3 63.8 reduce-scatter.10
